TPU v7x, 256 devices: a whole 4x4x8 slice. The times are simulated.
256 devices in a mesh: ctx: 128 (over x, y, z_lo, core), head: 2 (over z_hi).
Axes of the slice: x: 4, y: 4, z: 8 (z_hi: 2, z_lo: 4; z = z_hi * 4 + z_lo), core: 2. Of those that a mesh axis runs over, the one named last changes fastest.
Arguments:
- latent: bfloat16 [16384, 512], P('ctx'), may hold values from -6 to 6
- rope_key: bfloat16 [16384, 64], P('ctx'), may hold values from -6 to 6
- queries: bfloat16 [16384, 64, 512], P('ctx', 'head'), may hold values from -89 to 89
- query_rope: bfloat16 [16384, 4096], P('ctx', 'head'), may hold values from -6 to 6
- grad_out: bfloat16 [16384, 64, 512], P('ctx', 'head'), may hold values from -6 to 6
- sel_blocks: int32 [256, 5], P('ctx'), may hold values from 0 to 255, as said below
Outputs:
- attention_out: bfloat16 [16384, 64, 512], P('ctx', 'head')
- d_latent: float32 [16384, 512], P('ctx')
- d_rope_key: float32 [16384, 64], P('ctx')
Inputs may be any that keep to these rules, and one draw needn't show every extreme that they name: `sel_blocks`: row b lists the key blocks of query block b: slot 0 holds b, slots 1 to min(b, 4) hold distinct blocks below b, any of them, and any later slots hold b and are not used.
All inputs are finite; a program needn't handle non-finite values.
Results may differ from a plain program's by a relative error of at most 0.007.
Values may be sent and summed in bfloat16 or wider, within the bound.
No kernel may reach another device: no remote copies, remote signals or barrier semaphores. Data moves between devices by JAX's collectives and lax.ppermute only.
A program may use at most 192 MiB of HBM per device.

v0:
```python
import jax
import jax.numpy as jnp
from jax import lax
from jax.sharding import PartitionSpec as P

BLK = 64
SEL = 5


softmax_scale = 192.0 ** (-0.5)
rope_base = 10000.0


def rotate_pairs(values, positions, direction):
    half_width = values.shape[-1] // 2
    freq_steps = jnp.arange(half_width, dtype=jnp.float32)
    inverse_freq = rope_base ** (-2.0 * freq_steps / values.shape[-1])
    angles = positions.astype(jnp.float32)[:, None] * inverse_freq[None, :]
    cosine = jnp.cos(angles)
    sine_part = jnp.sin(angles) * direction
    lower_half = values[:, :half_width]
    upper_half = values[:, half_width:]
    return jnp.concatenate(
        [
            lower_half * cosine - upper_half * sine_part,
            upper_half * cosine + lower_half * sine_part,
        ],
        axis=1,
    )


def shards(latent, rope_key, queries, query_rope, grad_out, sel_blocks):
    token_count = latent.shape[0]
    latent_width = latent.shape[1]
    rope_width = rope_key.shape[1]
    head_count = queries.shape[1]
    block_count = token_count // BLK
    ctx_position = lax.axis_index("ctx")
    positions = ctx_position * token_count + jnp.arange(token_count, dtype=jnp.int32)
    rotated = rotate_pairs(rope_key.astype(jnp.float32), positions, 1.0).astype(jnp.bfloat16)
    whole_latent, whole_rotated = (
        lax.all_gather(latent, "ctx", axis=0, tiled=True),
        lax.all_gather(rotated, "ctx", axis=0, tiled=True),
    )
    offsets = jnp.arange(BLK, dtype=jnp.int32)
    key_rows = (sel_blocks[:, :, None] * BLK + offsets[None, None, :]).reshape(
        block_count, SEL * BLK
    )
    latent_key_rows = whole_latent[key_rows]
    keys_rotated = whole_rotated[key_rows]
    joined_keys = jnp.concatenate([latent_key_rows, keys_rotated], axis=2)
    latent_query_rows = queries.reshape(block_count, BLK, head_count, latent_width)
    query_rotary = query_rope.reshape(block_count, BLK, head_count, rope_width)
    joined_queries = jnp.concatenate([latent_query_rows, query_rotary], axis=3)
    upstream_gradient = grad_out.reshape(block_count, BLK, head_count, latent_width)
    scores = jnp.einsum(
        "sicu,squ->sicq", joined_queries, joined_keys, preferred_element_type=jnp.float32
    )
    block_ids = ctx_position * block_count + jnp.arange(block_count, dtype=jnp.int32)
    slot_index = jnp.arange(SEL * BLK, dtype=jnp.int32) // BLK
    slot_valid = slot_index[None, :] < jnp.minimum(block_ids + 1, SEL)[:, None]
    query_pos = positions.reshape(block_count, BLK)
    allowed = slot_valid[:, None, :] & (key_rows[:, None, :] <= query_pos[:, :, None])
    scores = jnp.where(allowed[:, :, None, :], scores * softmax_scale, -jnp.inf)
    row_max = jnp.max(scores, axis=-1, keepdims=True)
    expon = jnp.exp(scores - row_max)
    probs = expon / jnp.sum(expon, axis=-1, keepdims=True)
    probability_lowered = probs.astype(jnp.bfloat16)
    attention_out = jnp.einsum(
        "gpac,gcs->gpas", probability_lowered, latent_key_rows, preferred_element_type=jnp.float32
    )
    attention_out = attention_out.astype(jnp.bfloat16).reshape(
        token_count, head_count, latent_width
    )
    dprobs = jnp.einsum(
        "sicu,squ->sicq", upstream_gradient, latent_key_rows, preferred_element_type=jnp.float32
    )
    row_delta = jnp.sum(probs * dprobs, axis=-1, keepdims=True)
    scores_gradient = (probs * (dprobs - row_delta)).astype(jnp.bfloat16)
    grad_latent = softmax_scale * jnp.einsum(
        "rcfg,rcfq->rgq", scores_gradient, latent_query_rows, preferred_element_type=jnp.float32
    )
    grad_latent = grad_latent + jnp.einsum(
        "rcfg,rcfq->rgq", probability_lowered, upstream_gradient, preferred_element_type=jnp.float32
    )
    grad_rotary = softmax_scale * jnp.einsum(
        "bthk,bthr->bkr", scores_gradient, query_rotary, preferred_element_type=jnp.float32
    )
    grad_terms = jnp.concatenate([grad_latent, grad_rotary], axis=2).reshape(
        block_count * SEL * BLK, latent_width + rope_width
    )
    flat_rows = key_rows.reshape(-1)
    local_rows = flat_rows
    local_rows = jnp.where(
        (local_rows >= 0) & (local_rows < token_count * lax.axis_size("ctx")),
        local_rows,
        token_count * lax.axis_size("ctx"),
    )
    empty = jnp.zeros((token_count * lax.axis_size("ctx"), latent_width + rope_width), jnp.float32)
    owned = lax.psum_scatter(
        empty.at[local_rows].add(grad_terms, mode="drop"), "ctx", scatter_dimension=0, tiled=True
    )
    owned = lax.psum(owned, "head")
    d_latent = owned[:, :latent_width]
    d_rope_key = rotate_pairs(owned[:, latent_width:], positions, -1.0)
    return (attention_out, d_latent, d_rope_key)


def solution(mesh):
    return jax.shard_map(
        shards,
        mesh=mesh,
        in_specs=(
            P("ctx", None),
            P("ctx", None),
            P("ctx", "head", None),
            P("ctx", "head"),
            P("ctx", "head", None),
            P("ctx", None),
        ),
        out_specs=(P("ctx", "head", None), P("ctx", None), P("ctx", None)),
        check_vma=False,
    )
```

profile of v0, /device:TPU:1, one launch (start us, length us, event | category | flops | bytes accessed | tf_op | source)
XLA Modules:
  0.0 1357.6 jit_solution(7002328799493679324)
XLA Ops:
  7.2 0.0 all-gather.5.cloned.1.call-start
  7.2 0.7 convert_element_type.21
  8.0 0.1 fusion.39
  8.1 0.6 pad_maximum_fusion.2
  8.7 0.0 all-gather.5.cloned.1.call-update
  8.8 0.0 all-gather.3.cloned.1.call-start
  8.8 0.7 all-gather.3.cloned.1.call-update
  9.5 0.0 reduce-scatter.2.cloned.1.call-start
  9.6 0.7 broadcast_multiply_fusion
  10.2 0.1 add.139
  10.3 0.1 add.147
  10.4 0.1 add.140
  10.5 0.1 add.142
  10.6 0.1 reshape.200
  10.6 0.1 iota_add_fusion
  10.7 0.1 add.156
  10.8 2.1 reshape.194
  12.9 0.1 broadcast_compare_fusion
  13.0 0.1 compare_and_fusion
  13.1 203.5 %all-gather.5.cloned.1.call-done = bf16[16384,64]{0,1:T(8,128)(2,1)} async-done(((bf16[128,64]{0,1:T(8,128)(2,1)}), bf16[16384,64]{0,1:T(8,128)(2,1)}) %all-gather.5.cloned.1.call-update) | async-done | bytes 2097168 | tf_op jit(solution)/shard_map/all_gather | solution.py:43
  216.7 4.7 copy.37
  221.4 4.4 gather_fusion.1
  225.9 206.5 %all-gather.3.cloned.1.call-done = bf16[16384,512]{1,0:T(8,128)(2,1)} async-done(((bf16[128,512]{1,0:T(8,128)(2,1)}), bf16[16384,512]{1,0:T(8,128)(2,1)}) %all-gather.3.cloned.1.call-update) | async-done | bytes 16777232 | tf_op jit(solution)/shard_map/all_gather | solution.py:42
  432.4 10.7 gather_fusion
  443.1 0.0 copy-start.1
  443.1 5.6 fusion.6
  448.7 0.0 copy-start.4
  448.7 23.1 %fusion.49 = (f32[2,64,32]{2,1,0:T(8,128)S(1)}, f32[2,64,32,320]{3,2,1,0:T(8,128)S(1)}) fusion(f32[2,64,32,320]{3,2,1,0:T(8,128)S(1)} %fusion.6, pred[2,64,320]{2,1,0:T(8,128)(4,1)S(1)} %compare_and_fusion), kind=kOutput, calls=%fused_computation.79 | output fusion | flops 7864639 | bytes 10543104 | tf_op jit(solution)/shard_map/sub | solution.py:66
  471.8 0.0 copy-start
  471.8 0.0 copy-done.1
  471.8 0.0 copy-done.4
  471.8 2.7 fusion.3
  474.6 0.0 copy-start.3
  474.6 1.7 fusion.5
  476.3 0.7 fusion.24
  476.9 0.0 copy-done.3
  477.0 1.6 fusion.20
  478.6 0.0 copy-done
  478.6 2.7 fusion.21
  481.3 0.1 copy.40
  481.5 0.1 pad_maximum_fusion
  481.6 23.6 %scatter_custom_fusion = f32[16384,576]{1,0:T(8,128)} fusion(s32[640]{0:T(1024)S(1)} %fusion.42, f32[640,576]{1,0:T(8,128)S(1)} %bitcast.49, f32[]{:T(128)} %constant.56.clone.1), kind=kCustom, calls=%fused_computation.4 | custom fusion | flops 368640 | bytes 37748740 | tf_op jit(solution)/shard_map/scatter-add | solution.py:101
  505.2 39.2 %copy.41 = f32[16384,576]{0,1:T(8,128)} copy(f32[16384,576]{1,0:T(8,128)} %scatter_custom_fusion) | data formatting | bytes 75497472 | tf_op jit(solution)/shard_map/scatter-add | solution.py:101
  544.4 0.0 copy-start.2
  544.4 0.0 reduce-scatter.2.cloned.1.call-update
  544.4 0.0 all-reduce.2.cloned.1.call-start
  544.4 753.9 %reduce-scatter.2.cloned.1.call-done = f32[128,576]{0,1:T(8,128)} async-done(((f32[16384,576]{0,1:T(8,128)}), f32[128,576]{0,1:T(8,128)}) %reduce-scatter.2.cloned.1.call-update) | async-done | bytes 294928 | tf_op jit(solution)/shard_map/reduce_scatter | solution.py:100
  1298.3 0.0 all-reduce.2.cloned.1.call-update
  1298.3 0.0 copy-done.2
  1298.4 7.2 convolution_convert_fusion
  1305.6 42.2 %all-reduce.2.cloned.1.call-done = f32[128,576]{0,1:T(8,128)} async-done(((f32[128,576]{0,1:T(8,128)}), f32[128,576]{0,1:T(8,128)}) %all-reduce.2.cloned.1.call-update) | async-done | bytes 294928 | tf_op jit(solution)/shard_map/psum | solution.py:103
  1347.8 1.0 slice.29
  1348.8 0.8 copy.42
  1349.6 0.9 fusion.36
  1350.5 0.6 pad_maximum_fusion.1
  (10 shorter events, 0.1 us)
Async XLA Ops:
  7.2 209.5 %all-gather.5.cloned.1.call-start = ((), (), s32[]{:S(2)}) async-start(), calls=%async_computation.2 | async-start | bytes 2113536 | tf_op jit(solution)/shard_map/all_gather | solution.py:43
  8.8 423.6 %all-gather.3.cloned.1.call-start = ((), (), s32[]{:S(2)}) async-start(), calls=%async_computation.1 | async-start | bytes 16908288 | tf_op jit(solution)/shard_map/all_gather | solution.py:42
  9.5 1288.8 %reduce-scatter.2.cloned.1.call-start = ((), (), s32[]{:S(2)}) async-start(), calls=%async_computation.3 | async-start | bytes 38043648 | tf_op jit(solution)/shard_map/reduce_scatter | solution.py:100
  443.1 28.7 %copy-start.1 = (bf16[640,512]{1,0:T(8,128)(2,1)}, bf16[640,512]{1,0:T(8,128)(2,1)S(1)}, u32[]{:S(2)}) copy-start(bf16[640,512]{1,0:T(8,128)(2,1)S(1)} %gather_fusion) | copy-start | bytes 1966084
  448.7 23.1 %copy-start.4 = (bf16[128,32,512]{2,1,0:T(8,128)(2,1)S(1)}, bf16[128,32,512]{2,1,0:T(8,128)(2,1)}, u32[]{:S(2)}) copy-start(bf16[128,32,512]{2,1,0:T(8,128)(2,1)} %param.10) | copy-start | bytes 12582916
  471.8 6.8 copy-start
  474.6 2.4 copy-start.3
  544.4 754.0 %copy-start.2 = (bf16[640,512]{1,0:T(8,128)(2,1)S(1)}, bf16[640,512]{1,0:T(8,128)(2,1)}, u32[]{:S(2)}) copy-start(bf16[640,512]{1,0:T(8,128)(2,1)} %copy-done.1) | copy-start | bytes 1966084
  544.4 803.4 %all-reduce.2.cloned.1.call-start = ((), (), s32[]{:S(2)}) async-start(), calls=%async_computation.4 | async-start | bytes 589824 | tf_op jit(solution)/shard_map/psum | solution.py:103
Sparse Core Ops, SparseCore 0:
  10.4 206.2 all-gather.4
  218.5 213.7 all-gather.2
  544.5 753.7 reduce-scatter.1
  1300.8 46.9 all-reduce.1
where the time goes:
time: 1360 us
  waiting for transfers between devices  1210 us (89%)
  local copies, waits for them, and re-layouts  63.6 us (5%)
  other arithmetic  52.5 us (4%)
  matrix products  20.5 us (2%)
  between operations  14 us (1%)
    reduce_scatter x1, waiting for transfers between devices, shards(): lax.psum_scatter(empty.at[local_rows].add(grad_terms, mode='drop'), 'ctx'...  754 us
    all_gather x1, waiting for transfers between devices, shards(): lax.all_gather(latent, 'ctx', axis=0, tiled=True)  206 us
    all_gather x1, waiting for transfers between devices, shards(): lax.all_gather(rotated, 'ctx', axis=0, tiled=True)  204 us
    psum x1, waiting for transfers between devices, shards(): owned = lax.psum(owned, 'head')  42.2 us
    scatter-add x1, local copies, waits for them, and re-layouts, shards(): empty.at[local_rows].add(grad_terms, mode='drop')  39.2 us
  transfers between devices with their start and end apart: 4, of which 4 were waited for; matrix products, arithmetic and copies ran while one was open for 1% of the time, Pallas kernels for 0%

commit v1 on v0

v1 whole, which is shorter than its diff:
```python
import functools

import jax
import jax.numpy as jnp
from jax import lax
from jax.experimental import pallas as pl
from jax.experimental.pallas import tpu as pltpu
from jax.sharding import Mesh, PartitionSpec as P

BLK = 64
SEL = 5
LAT = 512
ROPE = 64
HEADS = 32
UNIT = 16
HALF = 144
TILE = 512

softmax_scale = 192.0 ** (-0.5)
rope_base = 10000.0

bf16 = jnp.bfloat16
f32 = jnp.float32
VMEM = pl.BlockSpec(memory_space=pltpu.VMEM)
SMEM = pl.BlockSpec(memory_space=pltpu.SMEM)
PARAMS = pltpu.CompilerParams(vmem_limit_bytes=48 * 1024 * 1024)


def call(kernel, ins, outs, scratch=(), scalars=0, name=None):
    specs = [SMEM] * scalars + [VMEM] * (len(ins) - scalars)
    return pl.pallas_call(
        kernel,
        out_shape=[jax.ShapeDtypeStruct(s, d) for s, d in outs],
        in_specs=specs,
        out_specs=[VMEM] * len(outs),
        scratch_shapes=list(scratch),
        compiler_params=PARAMS,
        name=name,
    )(*ins)


MESH = ("x", "y", "z", "c", "h")


def partner(place, phase, k):
    x, y, z, c, h = place
    axis = "z" if phase == "u" else "xy"[c if phase == "v" else 1 - c]
    if axis == "x":
        x ^= k
    elif axis == "y":
        y ^= k
    else:
        ring = h * 4 + z
        if k == 3:
            ring = (ring + (1 if ring % 2 else 7)) % 8
        else:
            ring ^= k
        h, z = ring // 4, ring % 4
    return x, y, z, c, h


def number(place):
    x, y, z, c, h = place
    return (((x * 4 + y) * 4 + z) * 2 + c) * 2 + h


def exchange(a, phase, k):
    places = [(i // 64, i // 16 % 4, i // 4 % 4, i // 2 % 2, i % 2) for i in range(256)]
    return lax.ppermute(a, MESH, [(number(p), number(partner(p, phase, k))) for p in places])


def swap(a, axis):
    return lax.ppermute(a, axis, [(0, 1), (1, 0)])


def prep_kernel(meta, lat, rope, cosine, sine, sel, mine, other, rot_out, units):
    c = meta[0]
    x = rope[...].astype(f32)
    lo, hi = x[:, :32], x[:, 32:]
    rot = jnp.concatenate(
        [lo * cosine[...] - hi * sine[...], hi * cosine[...] + lo * sine[...]], axis=1
    ).astype(bf16)
    rot_out[...] = rot
    for i in range(2):
        packed = jnp.concatenate([rot[i * 64 : i * 64 + 32], rot[i * 64 + 32 : i * 64 + 64]], axis=1)
        for n in range(18):
            if n < 16:
                l, r = n // 4, n % 4
                v = lat[i * 64 + r * UNIT : i * 64 + (r + 1) * UNIT, l * 128 : (l + 1) * 128]
            else:
                v = packed[(n - 16) * UNIT : (n - 15) * UNIT]
            row = i * HALF + (n % 9) * UNIT
            units[n // 9, row : row + UNIT, :] = v
    for half in range(2):
        units[half, 288:304, :] = sel[...]
    mine[...] = units[c]
    other[...] = units[1 - c]


def chip_kernel(mine, recv, x, sel):
    x[0:288] = mine[0:288]
    x[288:576] = recv[0:288]
    row = lax.broadcasted_iota(jnp.int32, (UNIT, 128), 0)
    sel[...] = jnp.where(
        row == 0, mine[288:304].astype(f32), recv[288:304].astype(f32)
    ).astype(bf16)


def line_kernel(*refs):
    for k in range(4):
        refs[4][k * 576 : (k + 1) * 576] = refs[k][...]


def pack_kernel(where_, *refs):
    ins, outs, held = refs[:4], refs[4:8], refs[8]
    for k in range(4):
        held[k * 16 : (k + 1) * 16] = ins[k][...].reshape(16, HALF, 128)
    for k in range(4):
        for s in range(16):
            outs[k][s * HALF : (s + 1) * HALF] = held[where_[k * 16 + s]]


def merge_kernel(where_, *refs):
    ins, mine, other, held = refs[:4], refs[4], refs[5], refs[6]
    for k in range(4):
        held[k * 16 : (k + 1) * 16] = ins[k][...].reshape(16, HALF, 128)
    for s in range(16):
        out = mine if s < 8 else other
        row = (s % 8) * HALF
        out[row : row + HALF] = held[where_[s] * 16 + s]


def attention_kernel(
    meta, lat, rot, mine, other, q_ref, qr_ref, do_ref,
    out_ref, dkl_ref, dkr_ref, gm_ref, go_ref,
    units, keys, keys_r, acc, acc_r,
):
    i, t = pl.program_id(0), pl.program_id(1)
    c = meta[0]
    block = meta[1] + i

    @pl.when(t == 0)
    def _():
        rows = pl.ds(pl.multiple_of(i * BLK, BLK), BLK)
        keys[0:BLK] = lat[rows, :]
        keys_r[0:BLK] = rot[rows, :]
        part = pl.ds(pl.multiple_of(i * 576, 576), 576)
        units[c] = mine[part, :]
        units[1 - c] = other[part, :]
        for s in range(4):
            base = (s + 1) * BLK
            for n in range(16):
                row = s * HALF + (n % 9) * UNIT
                l, r = n // 4, n % 4
                keys[base + r * UNIT : base + (r + 1) * UNIT, l * 128 : (l + 1) * 128] = units[
                    n // 9, row : row + UNIT, :
                ]
            packed = units[1, s * HALF + 112 : s * HALF + 144, :]
            keys_r[base : base + 32] = packed[:, :64]
            keys_r[base + 32 : base + 64] = packed[:, 64:]
        acc[...] = jnp.zeros_like(acc)
        acc_r[...] = jnp.zeros_like(acc_r)

    q, qr, do = q_ref[...], qr_ref[...], do_ref[...]
    nt = (((1,), (1,)), ((), ()))
    raw = lax.dot_general(keys[...], q, nt, preferred_element_type=f32)
    raw = raw + lax.dot_general(keys_r[...], qr, nt, preferred_element_type=f32)
    key_row = lax.broadcasted_iota(jnp.int32, raw.shape, 0)
    query = lax.broadcasted_iota(jnp.int32, raw.shape, 1) // HEADS + t * (TILE // HEADS)
    limit = jnp.minimum(block + 1, SEL) * BLK
    allowed = (key_row < limit) & ((key_row >= BLK) | (key_row <= query))
    raw = jnp.where(allowed, raw, -jnp.inf)
    top = jnp.max(raw, axis=0, keepdims=True)
    expon = jnp.exp((raw - top) * softmax_scale)
    probs = expon * (1.0 / jnp.sum(expon, axis=0, keepdims=True))
    probs_low = probs.astype(bf16)
    dprobs = lax.dot_general(keys[...], do, nt, preferred_element_type=f32)
    row_delta = jnp.sum(probs * dprobs, axis=0, keepdims=True)
    dscores = (probs * (dprobs - row_delta) * softmax_scale).astype(bf16)
    out_ref[...] = lax.dot_general(
        probs_low, keys[...], (((0,), (0,)), ((), ())), preferred_element_type=f32
    ).astype(bf16)
    acc[...] += jnp.dot(dscores, q, preferred_element_type=f32) + jnp.dot(
        probs_low, do, preferred_element_type=f32
    )
    acc_r[...] += jnp.dot(dscores, qr, preferred_element_type=f32)

    @pl.when(t == pl.num_programs(1) - 1)
    def _():
        rows = pl.ds(pl.multiple_of(i * BLK, BLK), BLK)
        dkl_ref[rows, :] = acc[0:BLK]
        dkr_ref[rows, :] = acc_r[0:BLK]
        for s in range(4):
            base = (s + 1) * BLK
            packed = jnp.concatenate(
                [acc_r[base : base + 32, :], acc_r[base + 32 : base + 64, :]], axis=1
            )
            for n in range(18):
                m = n % 9
                if n < 16:
                    l, r = n // 4, n % 4
                    v = acc[base + r * UNIT : base + (r + 1) * UNIT, l * 128 : (l + 1) * 128]
                else:
                    v = packed[(n - 16) * UNIT : (n - 15) * UNIT]
                row = s * HALF + m * UNIT
                units[n // 9, row : row + UNIT, :] = v.astype(bf16)
        part = pl.ds(pl.multiple_of(i * 576, 576), 576)
        gm_ref[part, :] = units[c]
        go_ref[part, :] = units[1 - c]


def attention(meta, lat, rot, mine, other, q, qr, do):
    tiles = BLK * HEADS // TILE
    whole = lambda shape: pl.BlockSpec(shape, lambda i, t: (0, 0))
    rows = lambda width: pl.BlockSpec((TILE, width), lambda i, t: (i * tiles + t, 0))
    return pl.pallas_call(
        attention_kernel,
        grid=(2, tiles),
        out_shape=[
            jax.ShapeDtypeStruct(q.shape, bf16),
            jax.ShapeDtypeStruct((128, LAT), f32),
            jax.ShapeDtypeStruct((128, ROPE), f32),
            jax.ShapeDtypeStruct((8 * HALF, 128), bf16),
            jax.ShapeDtypeStruct((8 * HALF, 128), bf16),
        ],
        in_specs=[
            SMEM,
            whole((128, LAT)),
            whole((128, ROPE)),
            whole((8 * HALF, 128)),
            whole((8 * HALF, 128)),
            rows(LAT),
            rows(ROPE),
            rows(LAT),
        ],
        out_specs=[
            rows(LAT),
            whole((128, LAT)),
            whole((128, ROPE)),
            whole((8 * HALF, 128)),
            whole((8 * HALF, 128)),
        ],
        scratch_shapes=[
            pltpu.VMEM((2, 576, 128), bf16),
            pltpu.VMEM((SEL * BLK, LAT), bf16),
            pltpu.VMEM((SEL * BLK, ROPE), bf16),
            pltpu.VMEM((SEL * BLK, LAT), f32),
            pltpu.VMEM((SEL * BLK, ROPE), f32),
        ],
        compiler_params=PARAMS,
        name="attention",
    )(meta, lat, rot, mine, other, q, qr, do)


def slots_kernel(mine, recv, g):
    g[0:1152] = mine[...]
    g[1152:2304] = recv[...]


def plane_kernel(where_, *refs):
    ins, outs, acc = refs[:4], refs[4:8], refs[8]
    acc[...] = jnp.zeros_like(acc)
    for k in range(4):
        for s in range(16):
            f = where_[k * 16 + s]
            acc[f] = acc[f] + ins[k][s * HALF : (s + 1) * HALF].astype(f32)
    for k in range(4):
        for j in range(16):
            outs[k][j * HALF : (j + 1) * HALF] = acc[k * 16 + j].astype(outs[k].dtype)


def sum_rows(ins, at):
    total = ins[0][at : at + HALF]
    for k in range(1, 4):
        total = total + ins[k][at : at + HALF].astype(f32)
    return total


def column_kernel(*refs):
    ins, outs = refs[:4], refs[4:8]
    for j in range(16):
        out, row = outs[j // 4], (j % 4) * HALF
        out[row : row + HALF] = sum_rows(ins, j * HALF).astype(out.dtype)


def owner_kernel(*refs):
    ins, outs = refs[:4], refs[4:6]
    for j in range(4):
        row = (j % 2) * HALF
        outs[j // 2][row : row + HALF] = sum_rows(ins, j * HALF)


def half_sum_kernel(meta, mine, recv, dkl, dkr, out, units):
    c = meta[0]
    units[c] = mine[...]
    units[1 - c] = recv[...]
    for i in range(2):
        lo, hi = slice(i * 64, i * 64 + 32), slice(i * 64 + 32, i * 64 + 64)
        packed = jnp.concatenate([dkr[lo, :], dkr[hi, :]], axis=1)
        for n in range(18):
            if n < 16:
                l, r = n // 4, n % 4
                own = dkl[i * 64 + r * UNIT : i * 64 + (r + 1) * UNIT, l * 128 : (l + 1) * 128]
            else:
                own = packed[(n - 16) * UNIT : (n - 15) * UNIT]
            row = i * HALF + (n % 9) * UNIT
            to = (i * 18 + n) * UNIT
            out[to : to + UNIT] = (units[n // 9, row : row + UNIT, :] + own).astype(bf16)


def final_kernel(mine, recv, cosine, sine, lat_out, rope_out):
    for i in range(2):
        for n in range(16):
            l, r = n // 4, n % 4
            at = (i * 18 + n) * UNIT
            lat_out[i * 64 + r * UNIT : i * 64 + (r + 1) * UNIT, l * 128 : (l + 1) * 128] = mine[
                at : at + UNIT
            ].astype(f32) + recv[at : at + UNIT].astype(f32)
        at = (i * 18 + 16) * UNIT
        packed = mine[at : at + 32].astype(f32) + recv[at : at + 32].astype(f32)
        for part in range(2):
            rows = slice(i * 64 + part * 32, i * 64 + part * 32 + 32)
            g = packed[:, part * 64 : part * 64 + 64]
            lo, hi = g[:, :32], g[:, 32:]
            cs, sn = cosine[rows, :], sine[rows, :]
            rope_out[rows, :] = jnp.concatenate([lo * cs + hi * sn, hi * cs - lo * sn], axis=1)


def shards(latent, rope_key, queries, query_rope, grad_out, sel_blocks):
    x, y, z, c = [lax.axis_index(a) for a in "xyzc"]
    ctx = ((x * 4 + y) * 4 + z) * 2 + c
    meta = jnp.stack([c, ctx * 2]).astype(jnp.int32)

    positions = ctx * 128 + jnp.arange(128, dtype=jnp.int32)
    freq_steps = jnp.arange(ROPE // 2, dtype=f32)
    inverse_freq = rope_base ** (-2.0 * freq_steps / ROPE)
    angles = positions.astype(f32)[:, None] * inverse_freq[None, :]
    cosine, sine = jnp.cos(angles), jnp.sin(angles)

    sel_row = sel_blocks[:, 1:].reshape(1, 8).astype(bf16)
    sel_unit = jnp.broadcast_to(jnp.pad(sel_row, ((0, 0), (0, 120))), (UNIT, 128))
    mine, other, rot = call(
        prep_kernel,
        (meta, latent, rope_key, cosine, sine, sel_unit),
        [((304, 128), bf16), ((304, 128), bf16), ((128, ROPE), bf16)],
        [pltpu.VMEM((2, 304, 128), bf16)],
        scalars=1,
        name="prep",
    )
    chip, sel = call(
        chip_kernel, (mine, swap(other, "c")), [((576, 128), bf16), ((UNIT, 128), bf16)], name="chip"
    )

    def all_of(a, phase):
        return [a] + [exchange(a, phase, k) for k in (1, 2, 3)]

    lines = all_of(chip, "u")
    (line,) = call(line_kernel, lines, [((2304, 128), bf16)], name="line")
    planes = all_of(line, "v")

    asked = jnp.stack([t[:2, :8] for t in all_of(sel, "w")]).astype(jnp.int32).reshape(4, 16)
    sx, sy, sz = asked >> 6, (asked >> 4) & 3, (asked >> 2) & 3
    local = jnp.where(((asked >> 1) & 1) == c, 0, 2) + (asked & 1)
    on_v = jnp.where(c == 0, x ^ sx, y ^ sy)
    on_w = jnp.where(c == 0, y ^ sy, x ^ sx)
    pos = on_v * 16 + (z ^ sz) * 4 + local
    pack_at = pos.reshape(-1)
    add_at = jnp.where(on_w == 0, pos, 64).reshape(-1)
    merge_at = on_w[0]

    packed = call(
        pack_kernel,
        [pack_at] + planes,
        [((2304, 128), bf16)] * 4,
        [pltpu.VMEM((64, HALF, 128), bf16)],
        scalars=1,
        name="pack",
    )
    got = [packed[0]] + [exchange(packed[k], "w", k) for k in (1, 2, 3)]
    key_mine, key_other = call(
        merge_kernel,
        [merge_at] + got,
        [((8 * HALF, 128), bf16)] * 2,
        [pltpu.VMEM((64, HALF, 128), bf16)],
        scalars=1,
        name="merge",
    )
    key_recv = swap(key_other, "c")

    q = queries.reshape(128 * HEADS, LAT)
    do = grad_out.reshape(128 * HEADS, LAT)
    qr = query_rope.reshape(128 * HEADS, ROPE)
    out, dkl, dkr, g_mine, g_other = attention(meta, latent, rot, key_mine, key_recv, q, qr, do)

    (slots,) = call(slots_kernel, (g_mine, swap(g_other, "c")), [((2304, 128), bf16)], name="slots")
    sums = call(
        plane_kernel,
        [add_at] + all_of(slots, "w"),
        [((2304, 128), bf16 if k else f32) for k in range(4)],
        [pltpu.VMEM((65, HALF, 128), f32)],
        scalars=1,
        name="plane",
    )
    got = [sums[0]] + [exchange(sums[k], "v", k) for k in (1, 2, 3)]
    sums = call(column_kernel, got, [((576, 128), bf16 if k else f32) for k in range(4)], name="column")
    got = [sums[0]] + [exchange(sums[k], "u", k) for k in (1, 2, 3)]
    f_mine, f_other = call(owner_kernel, got, [((288, 128), f32)] * 2, name="owner")
    (total,) = call(
        half_sum_kernel,
        (meta, f_mine, swap(f_other, "c"), dkl, dkr),
        [((576, 128), bf16)],
        [pltpu.VMEM((2, 288, 128), f32)],
        scalars=1,
        name="half_sum",
    )
    d_latent, d_rope_key = call(
        final_kernel,
        (total, swap(total, "h"), cosine, sine),
        [((128, LAT), f32), ((128, ROPE), f32)],
        name="final",
    )
    return out.reshape(128, HEADS, LAT), d_latent, d_rope_key


def solution(mesh):
    lines = Mesh(mesh.devices.reshape(4, 4, 4, 2, 2), MESH)
    ctx = ("x", "y", "z", "c")
    return jax.shard_map(
        shards,
        mesh=lines,
        in_specs=(
            P(ctx, None),
            P(ctx, None),
            P(ctx, "h", None),
            P(ctx, "h"),
            P(ctx, "h", None),
            P(ctx, None),
        ),
        out_specs=(P(ctx, "h", None), P(ctx, None), P(ctx, None)),
        check_vma=False,
    )
```

time: 1360 us -> 149 us (0.11)
  waiting for transfers between devices: 1210 us -> 72.3 us
  local copies, waits for them, and re-layouts: 63.6 us -> 4.2 us
  other arithmetic: 52.5 us -> 1.17 us
  starting transfers between devices: 0.16 us -> 47.4 us
  Pallas kernels: 0 us -> 20.7 us
  matrix products: 20.5 us -> 0 us
    reduce_scatter x1 -> x0, waiting for transfers between devices: 754 us -> none  [shards(): lax.psum_scatter(empty.at[local_rows].add(grad_terms, mode='drop'), 'ctx'...]
    all_gather x2 -> x0, waiting for transfers between devices: 410 us -> none  [the longest x1 206 us: shards(): lax.all_gather(latent, 'ctx', axis=0, tiled=True)]
    ppermute x0 -> x26, waiting for transfers between devices: none -> 72.3 us  [the longest x21 64.4 us: exchange(): lax.ppermute(a, MESH, [(number(p), number(partner(p, phase, k))) for p in...]
    ppermute x0 -> x26, starting transfers between devices: none -> 47.4 us  [the longest x21 28.9 us: exchange(): lax.ppermute(a, MESH, [(number(p), number(partner(p, phase, k))) for p in...]
    psum x1 -> x0, waiting for transfers between devices: 42.2 us -> none  [shards(): owned = lax.psum(owned, 'head')]
    scatter-add x1 -> x0, local copies, waits for them, and re-layouts: 39.2 us -> none  [shards(): empty.at[local_rows].add(grad_terms, mode='drop')]
    sub x2 -> x0, other arithmetic: 23.9 us -> none  [the longest x1 23.1 us: shards(): expon = jnp.exp(scores - row_max)]
    scatter-add x1 -> x0, other arithmetic: 23.6 us -> none  [shards(): empty.at[local_rows].add(grad_terms, mode='drop')]
  transfers between devices with their start and end apart: 4 -> 26, of which waited for: 4 -> 21; matrix products, arithmetic and copies ran while one was open for 1% -> 1% of each run, Pallas kernels for 0% -> 0%
where the time goes in v1:
time: 149 us; the launch traced here: 146 us
  waiting for transfers between devices  72.3 us (49%)
  starting transfers between devices  47.4 us (32%)
  Pallas kernels  20.7 us (14%)
  local copies, waits for them, and re-layouts  4.2 us (3%)
    ppermute x21, waiting for transfers between devices, exchange(): lax.ppermute(a, MESH, [(number(p), number(partner(p, phase, k))) for p in...  64.4 us
    ppermute x21, starting transfers between devices, exchange(): lax.ppermute(a, MESH, [(number(p), number(partner(p, phase, k))) for p in...  28.9 us
    ppermute x5, starting transfers between devices, swap(): return lax.ppermute(a, axis, [(0, 1), (1, 0)])  18.5 us
    pallas_call x1, Pallas kernels, attention(): pl.pallas_call(attention_kernel, grid=(2, tiles), out_shape=[jax.ShapeDty...  14.7 us
    ppermute x5, waiting for transfers between devices, swap(): return lax.ppermute(a, axis, [(0, 1), (1, 0)])  7.94 us
    pallas_call x11, Pallas kernels, call(): pl.pallas_call(kernel, out_shape=[jax.ShapeDtypeStruct(s, d) for s, d in...  5.95 us
  transfers between devices with their start and end apart: 26, of which 21 were waited for; matrix products, arithmetic and copies ran while one was open for 1% of the time, Pallas kernels for 0%

profile of v1, /device:TPU:1, one launch (start us, length us, event | category | flops | bytes accessed | tf_op | source)
XLA Modules:
  0.0 146.5 jit_solution(14025564552066360488)
XLA Ops:
  0.7 0.7 convert.3
  1.5 0.1 convert_element_type.29
  1.6 0.8 copy.11.rope
  2.5 0.3 multiply_sine_fusion
  2.8 0.9 copy-done
  3.7 0.8 prep.1
  4.5 3.3 %collective-permute-start = (bf16[304,128]{1,0:T(8,128)(2,1)S(1)}, bf16[304,128]{1,0:T(8,128)(2,1)S(1)}, u32[]{:S(2)}, u32[]{:S(2)}) collective-permute-start(bf16[304,128]{1,0:T(8,128)(2,1)S(1)} %get-tuple-element.33), channel_id=1, source_target_pairs={{0,2},{2,0},{1,3},{3,1},{4,6},{6,4},{5,7},{7,5},{8,10},{10,8},{9,1... | collective-permute-start | bytes 233480 | tf_op jit(solution)/shard_map/ppermute | solution.py:73
  7.8 0.9 collective-permute-done.recv
  8.8 3.9 %collective-permute-start.6 = (bf16[576,128]{1,0:T(8,128)(2,1)S(1)}, bf16[576,128]{1,0:T(8,128)(2,1)S(1)}, u32[]{:S(2)}, u32[]{:S(2)}) collective-permute-start(bf16[576,128]{1,0:T(8,128)(2,1)S(1)} %get-tuple-element.35.refs_0_), channel_id=1, source_target_pairs={{0,13},{1,12},{2,15},{3,14},{4,8},{5,9},{6,10},{7,11},{8,4},{9,5},... | collective-permute-start | bytes 442376 | tf_op jit(solution)/shard_map/ppermute | solution.py:69
  12.7 1.9 %collective-permute-start.4 = (bf16[576,128]{1,0:T(8,128)(2,1)S(1)}, bf16[576,128]{1,0:T(8,128)(2,1)S(1)}, u32[]{:S(2)}, u32[]{:S(2)}) collective-permute-start(bf16[576,128]{1,0:T(8,128)(2,1)S(1)} %get-tuple-element.35.refs_0_), channel_id=1, source_target_pairs={{0,4},{1,5},{2,6},{3,7},{4,0},{5,1},{6,2},{7,3},{8,12},{9,13},{10,... | collective-permute-start | bytes 442376 | tf_op jit(solution)/shard_map/ppermute | solution.py:69
  14.6 2.0 %collective-permute-done.6.refs_3_ = bf16[576,128]{1,0:T(8,128)(2,1)S(1)} collective-permute-done((bf16[576,128]{1,0:T(8,128)(2,1)S(1)}, bf16[576,128]{1,0:T(8,128)(2,1)S(1)}, u32[]{:S(2)}, u32[]{:S(2)}) %collective-permute-start.6) | collective-permute-done | bytes 147488 | tf_op jit(solution)/shard_map/ppermute | solution.py:69
  16.6 5.2 %collective-permute-done.5.refs_2_ = bf16[576,128]{1,0:T(8,128)(2,1)S(1)} collective-permute-done((bf16[576,128]{1,0:T(8,128)(2,1)S(1)}, bf16[576,128]{1,0:T(8,128)(2,1)S(1)}, u32[]{:S(2)}, u32[]{:S(2)}) %collective-permute-start.5) | collective-permute-done | bytes 147488 | tf_op jit(solution)/shard_map/ppermute | solution.py:69
  21.9 2.8 %collective-permute-start.9 = (bf16[2304,128]{1,0:T(8,128)(2,1)S(1)}, bf16[2304,128]{1,0:T(8,128)(2,1)S(1)}, u32[]{:S(2)}, u32[]{:S(2)}) collective-permute-start(bf16[2304,128]{1,0:T(8,128)(2,1)S(1)} %line.1.refs_0_), channel_id=1, source_target_pairs={{0,192},{1,193},{2,50},{3,51},{4,196},{5,197},{6,54},{7,55},{8,200... | collective-permute-start | bytes 1769480 | tf_op jit(solution)/shard_map/ppermute | solution.py:69
  24.7 0.3 collective-permute-start.8
  25.0 0.3 collective-permute-start.7
  25.4 2.5 %collective-permute-start.3 = (bf16[16,128]{1,0:T(8,128)(2,1)S(1)}, bf16[16,128]{1,0:T(8,128)(2,1)S(1)}, u32[]{:S(2)}, u32[]{:S(2)}) collective-permute-start(bf16[16,128]{1,0:T(8,128)(2,1)S(1)} %get-tuple-element.34), channel_id=1, source_target_pairs={{0,48},{1,49},{2,194},{3,195},{4,52},{5,53},{6,198},{7,199},{8,56}... | collective-permute-start | bytes 12296 | tf_op jit(solution)/shard_map/ppermute | solution.py:69
  27.8 0.5 collective-permute-start.2
  28.4 1.1 collective-permute-done.3
  29.4 0.1 stack.27
  29.5 0.1 stack.30
  29.6 2.6 %collective-permute-done.2 = bf16[16,128]{1,0:T(8,128)(2,1)S(1)} collective-permute-done((bf16[16,128]{1,0:T(8,128)(2,1)S(1)}, bf16[16,128]{1,0:T(8,128)(2,1)S(1)}, u32[]{:S(2)}, u32[]{:S(2)}) %collective-permute-start.2) | collective-permute-done | bytes 4128 | tf_op jit(solution)/shard_map/ppermute | solution.py:69
  32.2 0.1 stack.29
  32.3 0.1 stack.28
  32.5 6.2 %collective-permute-done.9.refs_3_ = bf16[2304,128]{1,0:T(8,128)(2,1)S(1)} collective-permute-done((bf16[2304,128]{1,0:T(8,128)(2,1)S(1)}, bf16[2304,128]{1,0:T(8,128)(2,1)S(1)}, u32[]{:S(2)}, u32[]{:S(2)}) %collective-permute-start.9) | collective-permute-done | bytes 589856 | tf_op jit(solution)/shard_map/ppermute | solution.py:69
  38.7 0.7 collective-permute-done.7.refs_1_
  39.4 0.9 pack.1
  40.2 1.3 collective-permute-start.10
  41.5 2.4 %collective-permute-start.11 = (bf16[2304,128]{1,0:T(8,128)(2,1)S(1)}, bf16[2304,128]{1,0:T(8,128)(2,1)S(1)}, u32[]{:S(2)}, u32[]{:S(2)}) collective-permute-start(bf16[2304,128]{1,0:T(8,128)(2,1)S(1)} %get-tuple-element.38), channel_id=1, source_target_pairs={{0,32},{1,33},{2,130},{3,131},{4,36},{5,37},{6,134},{7,135},{8,40}... | collective-permute-start | bytes 1769480 | tf_op jit(solution)/shard_map/ppermute | solution.py:69
  44.0 0.2 collective-permute-start.12
  44.2 5.1 %collective-permute-done.10.refs_1_ = bf16[2304,128]{1,0:T(8,128)(2,1)S(1)} collective-permute-done((bf16[2304,128]{1,0:T(8,128)(2,1)S(1)}, bf16[2304,128]{1,0:T(8,128)(2,1)S(1)}, u32[]{:S(2)}, u32[]{:S(2)}) %collective-permute-start.10) | collective-permute-done | bytes 589856 | tf_op jit(solution)/shard_map/ppermute | solution.py:69
  49.3 8.6 %collective-permute-done.11.refs_2_ = bf16[2304,128]{1,0:T(8,128)(2,1)S(1)} collective-permute-done((bf16[2304,128]{1,0:T(8,128)(2,1)S(1)}, bf16[2304,128]{1,0:T(8,128)(2,1)S(1)}, u32[]{:S(2)}, u32[]{:S(2)}) %collective-permute-start.11) | collective-permute-done | bytes 589856 | tf_op jit(solution)/shard_map/ppermute | solution.py:69
  57.9 2.6 %collective-permute-done.12.refs_3_ = bf16[2304,128]{1,0:T(8,128)(2,1)S(1)} collective-permute-done((bf16[2304,128]{1,0:T(8,128)(2,1)S(1)}, bf16[2304,128]{1,0:T(8,128)(2,1)S(1)}, u32[]{:S(2)}, u32[]{:S(2)}) %collective-permute-start.12) | collective-permute-done | bytes 589856 | tf_op jit(solution)/shard_map/ppermute | solution.py:69
  60.5 0.7 merge.1
  61.3 3.5 %collective-permute-start.13 = (bf16[1152,128]{1,0:T(8,128)(2,1)S(1)}, bf16[1152,128]{1,0:T(8,128)(2,1)S(1)}, u32[]{:S(2)}, u32[]{:S(2)}) collective-permute-start(bf16[1152,128]{1,0:T(8,128)(2,1)S(1)} %get-tuple-element.41), channel_id=1, source_target_pairs={{0,2},{2,0},{1,3},{3,1},{4,6},{6,4},{5,7},{7,5},{8,10},{10,8},{9,1... | collective-permute-start | bytes 884744 | tf_op jit(solution)/shard_map/ppermute | solution.py:73
  64.7 1.1 reshape.81.qr_ref
  65.8 0.1 collective-permute-done.13.other
  66.0 14.7 %attention.1 = (bf16[4096,512]{1,0:T(8,128)(2,1)}, f32[128,512]{1,0:T(8,128)S(1)}, f32[128,64]{1,0:T(8,128)S(1)}, bf16[1152,128]{1,0:T(8,128)(2,1)S(1)}, bf16[1152,128]{1,0:T(8,128)(2,1)S(1)}) custom-call(s32[2]{0:T(128)S(1)} %pad_add_fusion.meta, bf16[128,512]{1,0:T(8,128)(2,1)S(1)} %copy-done.1, bf16[128,64]{1,0:T(8,128)(2,1)S(1)} %get-tuple-element.31.rot, ...), custom_call_target="tpu_custom_call" | custom-call | tf_op jit(solution)/shard_map/attention/pallas_call | solution.py:216
  80.7 0.4 collective-permute-start.14
  81.1 1.2 collective-permute-done.14.recv
  82.3 2.7 %collective-permute-start.17 = (bf16[2304,128]{1,0:T(8,128)(2,1)S(1)}, bf16[2304,128]{1,0:T(8,128)(2,1)S(1)}, u32[]{:S(2)}, u32[]{:S(2)}) collective-permute-start(bf16[2304,128]{1,0:T(8,128)(2,1)S(1)} %slots.1.refs_0_), channel_id=1, source_target_pairs={{0,48},{1,49},{2,194},{3,195},{4,52},{5,53},{6,198},{7,199},{8,56}... | collective-permute-start | bytes 1769480 | tf_op jit(solution)/shard_map/ppermute | solution.py:69
  85.1 0.5 collective-permute-start.16
  85.6 0.3 collective-permute-start.15
  85.9 13.2 %collective-permute-done.17.refs_3_ = bf16[2304,128]{1,0:T(8,128)(2,1)S(1)} collective-permute-done((bf16[2304,128]{1,0:T(8,128)(2,1)S(1)}, bf16[2304,128]{1,0:T(8,128)(2,1)S(1)}, u32[]{:S(2)}, u32[]{:S(2)}) %collective-permute-start.17) | collective-permute-done | bytes 589856 | tf_op jit(solution)/shard_map/ppermute | solution.py:69
  99.1 0.6 collective-permute-done.15.refs_1_
  99.8 1.6 %plane.1 = (f32[2304,128]{1,0:T(8,128)S(1)}, bf16[2304,128]{1,0:T(8,128)(2,1)S(1)}, bf16[2304,128]{1,0:T(8,128)(2,1)S(1)}, bf16[2304,128]{1,0:T(8,128)(2,1)S(1)}) custom-call(s32[64]{0:T(128)S(1)} %broadcast_select_fusion.where_, bf16[2304,128]{1,0:T(8,128)(2,1)S(1)} %slots.1.refs_0_, bf16[2304,128]{1,0:T(8,128)(2,1)S(1)} %collective-permute-done.15.refs_1_, ...), custom_call_target="tpu_custom_call" | custom-call | tf_op jit(solution)/shard_map/plane/pallas_call | solution.py:31
  101.4 0.1 collective-permute-start.18
  101.5 1.1 collective-permute-start.19
  102.6 2.7 %collective-permute-start.20 = (bf16[2304,128]{1,0:T(8,128)(2,1)S(1)}, bf16[2304,128]{1,0:T(8,128)(2,1)S(1)}, u32[]{:S(2)}, u32[]{:S(2)}) collective-permute-start(bf16[2304,128]{1,0:T(8,128)(2,1)S(1)} %get-tuple-element.48), channel_id=1, source_target_pairs={{0,192},{1,193},{2,50},{3,51},{4,196},{5,197},{6,54},{7,55},{8,200... | collective-permute-start | bytes 1769480 | tf_op jit(solution)/shard_map/ppermute | solution.py:69
  105.3 5.2 %collective-permute-done.18.refs_1_ = bf16[2304,128]{1,0:T(8,128)(2,1)S(1)} collective-permute-done((bf16[2304,128]{1,0:T(8,128)(2,1)S(1)}, bf16[2304,128]{1,0:T(8,128)(2,1)S(1)}, u32[]{:S(2)}, u32[]{:S(2)}) %collective-permute-start.18) | collective-permute-done | bytes 589856 | tf_op jit(solution)/shard_map/ppermute | solution.py:69
  110.5 6.0 %collective-permute-done.19.refs_2_ = bf16[2304,128]{1,0:T(8,128)(2,1)S(1)} collective-permute-done((bf16[2304,128]{1,0:T(8,128)(2,1)S(1)}, bf16[2304,128]{1,0:T(8,128)(2,1)S(1)}, u32[]{:S(2)}, u32[]{:S(2)}) %collective-permute-start.19) | collective-permute-done | bytes 589856 | tf_op jit(solution)/shard_map/ppermute | solution.py:69
  116.5 2.7 %collective-permute-done.20.refs_3_ = bf16[2304,128]{1,0:T(8,128)(2,1)S(1)} collective-permute-done((bf16[2304,128]{1,0:T(8,128)(2,1)S(1)}, bf16[2304,128]{1,0:T(8,128)(2,1)S(1)}, u32[]{:S(2)}, u32[]{:S(2)}) %collective-permute-start.20) | collective-permute-done | bytes 589856 | tf_op jit(solution)/shard_map/ppermute | solution.py:69
  119.2 0.3 column.1
  119.5 0.1 collective-permute-start.21
  119.6 1.9 %collective-permute-start.22 = (bf16[576,128]{1,0:T(8,128)(2,1)S(1)}, bf16[576,128]{1,0:T(8,128)(2,1)S(1)}, u32[]{:S(2)}, u32[]{:S(2)}) collective-permute-start(bf16[576,128]{1,0:T(8,128)(2,1)S(1)} %get-tuple-element.51), channel_id=1, source_target_pairs={{0,8},{1,9},{2,10},{3,11},{4,12},{5,13},{6,14},{7,15},{8,0},{9,1},... | collective-permute-start | bytes 442376 | tf_op jit(solution)/shard_map/ppermute | solution.py:69
  121.5 3.2 %collective-permute-start.23 = (bf16[576,128]{1,0:T(8,128)(2,1)S(1)}, bf16[576,128]{1,0:T(8,128)(2,1)S(1)}, u32[]{:S(2)}, u32[]{:S(2)}) collective-permute-start(bf16[576,128]{1,0:T(8,128)(2,1)S(1)} %get-tuple-element.52), channel_id=1, source_target_pairs={{0,13},{1,12},{2,15},{3,14},{4,8},{5,9},{6,10},{7,11},{8,4},{9,5},... | collective-permute-start | bytes 442376 | tf_op jit(solution)/shard_map/ppermute | solution.py:69
  124.7 1.5 %collective-permute-done.22.refs_2_ = bf16[576,128]{1,0:T(8,128)(2,1)S(1)} collective-permute-done((bf16[576,128]{1,0:T(8,128)(2,1)S(1)}, bf16[576,128]{1,0:T(8,128)(2,1)S(1)}, u32[]{:S(2)}, u32[]{:S(2)}) %collective-permute-start.22) | collective-permute-done | bytes 147488 | tf_op jit(solution)/shard_map/ppermute | solution.py:69
  126.2 1.0 collective-permute-done.23.refs_3_
  127.3 6.9 %collective-permute-start.24 = (f32[288,128]{1,0:T(8,128)S(1)}, f32[288,128]{1,0:T(8,128)S(1)}, u32[]{:S(2)}, u32[]{:S(2)}) collective-permute-start(f32[288,128]{1,0:T(8,128)S(1)} %get-tuple-element.54), channel_id=1, source_target_pairs={{0,2},{2,0},{1,3},{3,1},{4,6},{6,4},{5,7},{7,5},{8,10},{10,8},{9,1... | collective-permute-start | bytes 442376 | tf_op jit(solution)/shard_map/ppermute | solution.py:73
  134.2 1.0 collective-permute-done.24.recv
  135.2 0.6 half_sum.1.mine
  135.8 4.4 %collective-permute-start.25 = (bf16[576,128]{1,0:T(8,128)(2,1)S(1)}, bf16[576,128]{1,0:T(8,128)(2,1)S(1)}, u32[]{:S(2)}, u32[]{:S(2)}) collective-permute-start(bf16[576,128]{1,0:T(8,128)(2,1)S(1)} %half_sum.1.mine), channel_id=1, source_target_pairs={{0,1},{1,0},{2,3},{3,2},{4,5},{5,4},{6,7},{7,6},{8,9},{9,8},{10,11... | collective-permute-start | bytes 442376 | tf_op jit(solution)/shard_map/ppermute | solution.py:73
  140.2 4.7 %collective-permute-done.25.recv = bf16[576,128]{1,0:T(8,128)(2,1)S(1)} collective-permute-done((bf16[576,128]{1,0:T(8,128)(2,1)S(1)}, bf16[576,128]{1,0:T(8,128)(2,1)S(1)}, u32[]{:S(2)}, u32[]{:S(2)}) %collective-permute-start.25) | collective-permute-done | bytes 147488 | tf_op jit(solution)/shard_map/ppermute | solution.py:73
  144.9 0.9 final.1
  145.8 0.7 copy.12
  (32 shorter events, 0.6 us)
Async XLA Ops:
  0.6 65.3 %copy-start.1 = (bf16[128,512]{1,0:T(8,128)(2,1)S(1)}, bf16[128,512]{1,0:T(8,128)(2,1)}, u32[]{:S(2)}) copy-start(bf16[128,512]{1,0:T(8,128)(2,1)} %lat.3) | copy-start | bytes 393220
  2.8 0.9 copy-start
  3.7 61.0 %copy-start.2 = (bf16[128,2048]{1,0:T(8,128)(2,1)S(1)}, bf16[128,2048]{1,0:T(8,128)(2,1)}, u32[]{:S(2)}) copy-start(bf16[128,2048]{1,0:T(8,128)(2,1)} %param.9) | copy-start | bytes 1572868
  4.5 4.2 %collective-permute-start = (bf16[304,128]{1,0:T(8,128)(2,1)S(1)}, bf16[304,128]{1,0:T(8,128)(2,1)S(1)}, u32[]{:S(2)}, u32[]{:S(2)}) collective-permute-start(bf16[304,128]{1,0:T(8,128)(2,1)S(1)} %get-tuple-element.33), channel_id=1, source_target_pairs={{0,2},{2,0},{1,3},{3,1},{4,6},{6,4},{5,7},{7,5},{8,10},{10,8},{9,1... | collective-permute-start | bytes 233480 | tf_op jit(solution)/shard_map/ppermute | solution.py:73
  8.8 7.9 %collective-permute-start.6 = (bf16[576,128]{1,0:T(8,128)(2,1)S(1)}, bf16[576,128]{1,0:T(8,128)(2,1)S(1)}, u32[]{:S(2)}, u32[]{:S(2)}) collective-permute-start(bf16[576,128]{1,0:T(8,128)(2,1)S(1)} %get-tuple-element.35.refs_0_), channel_id=1, source_target_pairs={{0,13},{1,12},{2,15},{3,14},{4,8},{5,9},{6,10},{7,11},{8,4},{9,5},... | collective-permute-start | bytes 442376 | tf_op jit(solution)/shard_map/ppermute | solution.py:69
  12.7 9.1 %collective-permute-start.5 = (bf16[576,128]{1,0:T(8,128)(2,1)S(1)}, bf16[576,128]{1,0:T(8,128)(2,1)S(1)}, u32[]{:S(2)}, u32[]{:S(2)}) collective-permute-start(bf16[576,128]{1,0:T(8,128)(2,1)S(1)} %get-tuple-element.35.refs_0_), channel_id=1, source_target_pairs={{0,8},{1,9},{2,10},{3,11},{4,12},{5,13},{6,14},{7,15},{8,0},{9,1},... | collective-permute-start | bytes 442376 | tf_op jit(solution)/shard_map/ppermute | solution.py:69
  12.7 9.1 %collective-permute-start.4 = (bf16[576,128]{1,0:T(8,128)(2,1)S(1)}, bf16[576,128]{1,0:T(8,128)(2,1)S(1)}, u32[]{:S(2)}, u32[]{:S(2)}) collective-permute-start(bf16[576,128]{1,0:T(8,128)(2,1)S(1)} %get-tuple-element.35.refs_0_), channel_id=1, source_target_pairs={{0,4},{1,5},{2,6},{3,7},{4,0},{5,1},{6,2},{7,3},{8,12},{9,13},{10,... | collective-permute-start | bytes 442376 | tf_op jit(solution)/shard_map/ppermute | solution.py:69
  21.9 16.8 %collective-permute-start.9 = (bf16[2304,128]{1,0:T(8,128)(2,1)S(1)}, bf16[2304,128]{1,0:T(8,128)(2,1)S(1)}, u32[]{:S(2)}, u32[]{:S(2)}) collective-permute-start(bf16[2304,128]{1,0:T(8,128)(2,1)S(1)} %line.1.refs_0_), channel_id=1, source_target_pairs={{0,192},{1,193},{2,50},{3,51},{4,196},{5,197},{6,54},{7,55},{8,200... | collective-permute-start | bytes 1769480 | tf_op jit(solution)/shard_map/ppermute | solution.py:69
  24.7 14.0 %collective-permute-start.8 = (bf16[2304,128]{1,0:T(8,128)(2,1)S(1)}, bf16[2304,128]{1,0:T(8,128)(2,1)S(1)}, u32[]{:S(2)}, u32[]{:S(2)}) collective-permute-start(bf16[2304,128]{1,0:T(8,128)(2,1)S(1)} %line.1.refs_0_), channel_id=1, source_target_pairs={{0,128},{1,129},{2,34},{3,35},{4,132},{5,133},{6,38},{7,39},{8,136... | collective-permute-start | bytes 1769480 | tf_op jit(solution)/shard_map/ppermute | solution.py:69
  25.0 14.3 %collective-permute-start.7 = (bf16[2304,128]{1,0:T(8,128)(2,1)S(1)}, bf16[2304,128]{1,0:T(8,128)(2,1)S(1)}, u32[]{:S(2)}, u32[]{:S(2)}) collective-permute-start(bf16[2304,128]{1,0:T(8,128)(2,1)S(1)} %line.1.refs_0_), channel_id=1, source_target_pairs={{0,64},{1,65},{2,18},{3,19},{4,68},{5,69},{6,22},{7,23},{8,72},{9,... | collective-permute-start | bytes 1769480 | tf_op jit(solution)/shard_map/ppermute | solution.py:69
  25.4 4.1 %collective-permute-start.3 = (bf16[16,128]{1,0:T(8,128)(2,1)S(1)}, bf16[16,128]{1,0:T(8,128)(2,1)S(1)}, u32[]{:S(2)}, u32[]{:S(2)}) collective-permute-start(bf16[16,128]{1,0:T(8,128)(2,1)S(1)} %get-tuple-element.34), channel_id=1, source_target_pairs={{0,48},{1,49},{2,194},{3,195},{4,52},{5,53},{6,198},{7,199},{8,56}... | collective-permute-start | bytes 12296 | tf_op jit(solution)/shard_map/ppermute | solution.py:69
  27.8 4.4 %collective-permute-start.2 = (bf16[16,128]{1,0:T(8,128)(2,1)S(1)}, bf16[16,128]{1,0:T(8,128)(2,1)S(1)}, u32[]{:S(2)}, u32[]{:S(2)}) collective-permute-start(bf16[16,128]{1,0:T(8,128)(2,1)S(1)} %get-tuple-element.34), channel_id=1, source_target_pairs={{0,32},{1,33},{2,130},{3,131},{4,36},{5,37},{6,134},{7,135},{8,40}... | collective-permute-start | bytes 12296 | tf_op jit(solution)/shard_map/ppermute | solution.py:69
  29.4 2.9 %collective-permute-start.1 = (bf16[16,128]{1,0:T(8,128)(2,1)S(1)}, bf16[16,128]{1,0:T(8,128)(2,1)S(1)}, u32[]{:S(2)}, u32[]{:S(2)}) collective-permute-start(bf16[16,128]{1,0:T(8,128)(2,1)S(1)} %get-tuple-element.34), channel_id=1, source_target_pairs={{0,16},{1,17},{2,66},{3,67},{4,20},{5,21},{6,70},{7,71},{8,24},{9,... | collective-permute-start | bytes 12296 | tf_op jit(solution)/shard_map/ppermute | solution.py:69
  40.2 9.1 %collective-permute-start.10 = (bf16[2304,128]{1,0:T(8,128)(2,1)S(1)}, bf16[2304,128]{1,0:T(8,128)(2,1)S(1)}, u32[]{:S(2)}, u32[]{:S(2)}) collective-permute-start(bf16[2304,128]{1,0:T(8,128)(2,1)S(1)} %get-tuple-element.37), channel_id=1, source_target_pairs={{0,16},{1,17},{2,66},{3,67},{4,20},{5,21},{6,70},{7,71},{8,24},{9,... | collective-permute-start | bytes 1769480 | tf_op jit(solution)/shard_map/ppermute | solution.py:69
  41.5 16.4 %collective-permute-start.11 = (bf16[2304,128]{1,0:T(8,128)(2,1)S(1)}, bf16[2304,128]{1,0:T(8,128)(2,1)S(1)}, u32[]{:S(2)}, u32[]{:S(2)}) collective-permute-start(bf16[2304,128]{1,0:T(8,128)(2,1)S(1)} %get-tuple-element.38), channel_id=1, source_target_pairs={{0,32},{1,33},{2,130},{3,131},{4,36},{5,37},{6,134},{7,135},{8,40}... | collective-permute-start | bytes 1769480 | tf_op jit(solution)/shard_map/ppermute | solution.py:69
  44.0 16.6 %collective-permute-start.12 = (bf16[2304,128]{1,0:T(8,128)(2,1)S(1)}, bf16[2304,128]{1,0:T(8,128)(2,1)S(1)}, u32[]{:S(2)}, u32[]{:S(2)}) collective-permute-start(bf16[2304,128]{1,0:T(8,128)(2,1)S(1)} %get-tuple-element.39), channel_id=1, source_target_pairs={{0,48},{1,49},{2,194},{3,195},{4,52},{5,53},{6,198},{7,199},{8,56}... | collective-permute-start | bytes 1769480 | tf_op jit(solution)/shard_map/ppermute | solution.py:69
  61.3 4.7 %collective-permute-start.13 = (bf16[1152,128]{1,0:T(8,128)(2,1)S(1)}, bf16[1152,128]{1,0:T(8,128)(2,1)S(1)}, u32[]{:S(2)}, u32[]{:S(2)}) collective-permute-start(bf16[1152,128]{1,0:T(8,128)(2,1)S(1)} %get-tuple-element.41), channel_id=1, source_target_pairs={{0,2},{2,0},{1,3},{3,1},{4,6},{6,4},{5,7},{7,5},{8,10},{10,8},{9,1... | collective-permute-start | bytes 884744 | tf_op jit(solution)/shard_map/ppermute | solution.py:73
  80.7 1.6 %collective-permute-start.14 = (bf16[1152,128]{1,0:T(8,128)(2,1)S(1)}, bf16[1152,128]{1,0:T(8,128)(2,1)S(1)}, u32[]{:S(2)}, u32[]{:S(2)}) collective-permute-start(bf16[1152,128]{1,0:T(8,128)(2,1)S(1)} %get-tuple-element.44), channel_id=1, source_target_pairs={{0,2},{2,0},{1,3},{3,1},{4,6},{6,4},{5,7},{7,5},{8,10},{10,8},{9,1... | collective-permute-start | bytes 884744 | tf_op jit(solution)/shard_map/ppermute | solution.py:73
  82.3 16.8 %collective-permute-start.17 = (bf16[2304,128]{1,0:T(8,128)(2,1)S(1)}, bf16[2304,128]{1,0:T(8,128)(2,1)S(1)}, u32[]{:S(2)}, u32[]{:S(2)}) collective-permute-start(bf16[2304,128]{1,0:T(8,128)(2,1)S(1)} %slots.1.refs_0_), channel_id=1, source_target_pairs={{0,48},{1,49},{2,194},{3,195},{4,52},{5,53},{6,198},{7,199},{8,56}... | collective-permute-start | bytes 1769480 | tf_op jit(solution)/shard_map/ppermute | solution.py:69
  85.1 14.1 %collective-permute-start.16 = (bf16[2304,128]{1,0:T(8,128)(2,1)S(1)}, bf16[2304,128]{1,0:T(8,128)(2,1)S(1)}, u32[]{:S(2)}, u32[]{:S(2)}) collective-permute-start(bf16[2304,128]{1,0:T(8,128)(2,1)S(1)} %slots.1.refs_0_), channel_id=1, source_target_pairs={{0,32},{1,33},{2,130},{3,131},{4,36},{5,37},{6,134},{7,135},{8,40}... | collective-permute-start | bytes 1769480 | tf_op jit(solution)/shard_map/ppermute | solution.py:69
  85.6 14.2 %collective-permute-start.15 = (bf16[2304,128]{1,0:T(8,128)(2,1)S(1)}, bf16[2304,128]{1,0:T(8,128)(2,1)S(1)}, u32[]{:S(2)}, u32[]{:S(2)}) collective-permute-start(bf16[2304,128]{1,0:T(8,128)(2,1)S(1)} %slots.1.refs_0_), channel_id=1, source_target_pairs={{0,16},{1,17},{2,66},{3,67},{4,20},{5,21},{6,70},{7,71},{8,24},{9,... | collective-permute-start | bytes 1769480 | tf_op jit(solution)/shard_map/ppermute | solution.py:69
  101.4 9.1 %collective-permute-start.18 = (bf16[2304,128]{1,0:T(8,128)(2,1)S(1)}, bf16[2304,128]{1,0:T(8,128)(2,1)S(1)}, u32[]{:S(2)}, u32[]{:S(2)}) collective-permute-start(bf16[2304,128]{1,0:T(8,128)(2,1)S(1)} %get-tuple-element.46), channel_id=1, source_target_pairs={{0,64},{1,65},{2,18},{3,19},{4,68},{5,69},{6,22},{7,23},{8,72},{9,... | collective-permute-start | bytes 1769480 | tf_op jit(solution)/shard_map/ppermute | solution.py:69
  101.5 15.1 %collective-permute-start.19 = (bf16[2304,128]{1,0:T(8,128)(2,1)S(1)}, bf16[2304,128]{1,0:T(8,128)(2,1)S(1)}, u32[]{:S(2)}, u32[]{:S(2)}) collective-permute-start(bf16[2304,128]{1,0:T(8,128)(2,1)S(1)} %get-tuple-element.47), channel_id=1, source_target_pairs={{0,128},{1,129},{2,34},{3,35},{4,132},{5,133},{6,38},{7,39},{8,136... | collective-permute-start | bytes 1769480 | tf_op jit(solution)/shard_map/ppermute | solution.py:69
  102.6 16.6 %collective-permute-start.20 = (bf16[2304,128]{1,0:T(8,128)(2,1)S(1)}, bf16[2304,128]{1,0:T(8,128)(2,1)S(1)}, u32[]{:S(2)}, u32[]{:S(2)}) collective-permute-start(bf16[2304,128]{1,0:T(8,128)(2,1)S(1)} %get-tuple-element.48), channel_id=1, source_target_pairs={{0,192},{1,193},{2,50},{3,51},{4,196},{5,197},{6,54},{7,55},{8,200... | collective-permute-start | bytes 1769480 | tf_op jit(solution)/shard_map/ppermute | solution.py:69
  119.5 5.2 %collective-permute-start.21 = (bf16[576,128]{1,0:T(8,128)(2,1)S(1)}, bf16[576,128]{1,0:T(8,128)(2,1)S(1)}, u32[]{:S(2)}, u32[]{:S(2)}) collective-permute-start(bf16[576,128]{1,0:T(8,128)(2,1)S(1)} %get-tuple-element.50), channel_id=1, source_target_pairs={{0,4},{1,5},{2,6},{3,7},{4,0},{5,1},{6,2},{7,3},{8,12},{9,13},{10,... | collective-permute-start | bytes 442376 | tf_op jit(solution)/shard_map/ppermute | solution.py:69
  119.6 6.6 %collective-permute-start.22 = (bf16[576,128]{1,0:T(8,128)(2,1)S(1)}, bf16[576,128]{1,0:T(8,128)(2,1)S(1)}, u32[]{:S(2)}, u32[]{:S(2)}) collective-permute-start(bf16[576,128]{1,0:T(8,128)(2,1)S(1)} %get-tuple-element.51), channel_id=1, source_target_pairs={{0,8},{1,9},{2,10},{3,11},{4,12},{5,13},{6,14},{7,15},{8,0},{9,1},... | collective-permute-start | bytes 442376 | tf_op jit(solution)/shard_map/ppermute | solution.py:69
  121.5 5.7 %collective-permute-start.23 = (bf16[576,128]{1,0:T(8,128)(2,1)S(1)}, bf16[576,128]{1,0:T(8,128)(2,1)S(1)}, u32[]{:S(2)}, u32[]{:S(2)}) collective-permute-start(bf16[576,128]{1,0:T(8,128)(2,1)S(1)} %get-tuple-element.52), channel_id=1, source_target_pairs={{0,13},{1,12},{2,15},{3,14},{4,8},{5,9},{6,10},{7,11},{8,4},{9,5},... | collective-permute-start | bytes 442376 | tf_op jit(solution)/shard_map/ppermute | solution.py:69
  127.3 7.9 %collective-permute-start.24 = (f32[288,128]{1,0:T(8,128)S(1)}, f32[288,128]{1,0:T(8,128)S(1)}, u32[]{:S(2)}, u32[]{:S(2)}) collective-permute-start(f32[288,128]{1,0:T(8,128)S(1)} %get-tuple-element.54), channel_id=1, source_target_pairs={{0,2},{2,0},{1,3},{3,1},{4,6},{6,4},{5,7},{7,5},{8,10},{10,8},{9,1... | collective-permute-start | bytes 442376 | tf_op jit(solution)/shard_map/ppermute | solution.py:73
  135.8 9.0 %collective-permute-start.25 = (bf16[576,128]{1,0:T(8,128)(2,1)S(1)}, bf16[576,128]{1,0:T(8,128)(2,1)S(1)}, u32[]{:S(2)}, u32[]{:S(2)}) collective-permute-start(bf16[576,128]{1,0:T(8,128)(2,1)S(1)} %half_sum.1.mine), channel_id=1, source_target_pairs={{0,1},{1,0},{2,3},{3,2},{4,5},{5,4},{6,7},{7,6},{8,9},{9,8},{10,11... | collective-permute-start | bytes 442376 | tf_op jit(solution)/shard_map/ppermute | solution.py:73

commit v2 on v1

--- a/solution.py
+++ b/solution.py
@@ -14,6 +14,8 @@
 HEADS = 32
 UNIT = 16
 HALF = 144
+ORDER = (0, 3, 2, 1)
+DISTANCES = (1, 2, 3)
 TILE = 512
 
 softmax_scale = 192.0 ** (-0.5)
@@ -112,41 +114,39 @@
 
 
 def pack_kernel(where_, *refs):
-    ins, outs, held = refs[:4], refs[4:8], refs[8]
+    ins, outs, held = refs[:4], refs[4:12], refs[12]
     for k in range(4):
         held[k * 16 : (k + 1) * 16] = ins[k][...].reshape(16, HALF, 128)
+    for i in range(2):
+        for k in range(4):
+            for j in range(8):
+                f = where_[ORDER[k] * 16 + (j // 4) * 8 + i * 4 + j % 4]
+                outs[i * 4 + k][j * HALF : (j + 1) * HALF] = held[f]
+
+
+def merge_kernel(i, where_, *refs):
+    ins, outs, held = refs[:4], refs[4:6], refs[6]
     for k in range(4):
-        for s in range(16):
-            outs[k][s * HALF : (s + 1) * HALF] = held[where_[k * 16 + s]]
-
-
-def merge_kernel(where_, *refs):
-    ins, mine, other, held = refs[:4], refs[4], refs[5], refs[6]
-    for k in range(4):
-        held[k * 16 : (k + 1) * 16] = ins[k][...].reshape(16, HALF, 128)
-    for s in range(16):
-        out = mine if s < 8 else other
-        row = (s % 8) * HALF
-        out[row : row + HALF] = held[where_[s] * 16 + s]
+        held[ORDER[k] * 8 : (ORDER[k] + 1) * 8] = ins[k][...].reshape(8, HALF, 128)
+    for j in range(8):
+        k = where_[(j // 4) * 8 + i * 4 + j % 4]
+        outs[j // 4][(j % 4) * HALF : (j % 4 + 1) * HALF] = held[k * 8 + j]
 
 
 def attention_kernel(
-    meta, lat, rot, mine, other, q_ref, qr_ref, do_ref,
-    out_ref, dkl_ref, dkr_ref, gm_ref, go_ref,
-    units, keys, keys_r, acc, acc_r,
+    i, meta, lat, rot, mine, other, q_ref, qr_ref, do_ref, *refs
 ):
-    i, t = pl.program_id(0), pl.program_id(1)
+    out_ref, dkl_ref, dkr_ref, gm_ref, go_ref, units, keys, keys_r, acc, acc_r = refs[-10:]
+    t = pl.program_id(0)
     c = meta[0]
     block = meta[1] + i
 
     @pl.when(t == 0)
     def _():
-        rows = pl.ds(pl.multiple_of(i * BLK, BLK), BLK)
-        keys[0:BLK] = lat[rows, :]
-        keys_r[0:BLK] = rot[rows, :]
-        part = pl.ds(pl.multiple_of(i * 576, 576), 576)
-        units[c] = mine[part, :]
-        units[1 - c] = other[part, :]
+        keys[0:BLK] = lat[i * BLK : (i + 1) * BLK]
+        keys_r[0:BLK] = rot[i * BLK : (i + 1) * BLK]
+        units[c] = mine[...]
+        units[1 - c] = other[...]
         for s in range(4):
             base = (s + 1) * BLK
             for n in range(16):
@@ -185,11 +185,10 @@
     )
     acc_r[...] += jnp.dot(dscores, qr, preferred_element_type=f32)
 
-    @pl.when(t == pl.num_programs(1) - 1)
+    @pl.when(t == pl.num_programs(0) - 1)
     def _():
-        rows = pl.ds(pl.multiple_of(i * BLK, BLK), BLK)
-        dkl_ref[rows, :] = acc[0:BLK]
-        dkr_ref[rows, :] = acc_r[0:BLK]
+        dkl_ref[...] = acc[0:BLK]
+        dkr_ref[...] = acc_r[0:BLK]
         for s in range(4):
             base = (s + 1) * BLK
             packed = jnp.concatenate(
@@ -204,69 +203,73 @@
                     v = packed[(n - 16) * UNIT : (n - 15) * UNIT]
                 row = s * HALF + m * UNIT
                 units[n // 9, row : row + UNIT, :] = v.astype(bf16)
-        part = pl.ds(pl.multiple_of(i * 576, 576), 576)
-        gm_ref[part, :] = units[c]
-        go_ref[part, :] = units[1 - c]
-
-
-def attention(meta, lat, rot, mine, other, q, qr, do):
+        gm_ref[...] = units[c]
+        go_ref[...] = units[1 - c]
+
+
+def attention(i, meta, lat, rot, mine, other, q, qr, do, out):
     tiles = BLK * HEADS // TILE
-    whole = lambda shape: pl.BlockSpec(shape, lambda i, t: (0, 0))
-    rows = lambda width: pl.BlockSpec((TILE, width), lambda i, t: (i * tiles + t, 0))
+    whole = lambda shape: pl.BlockSpec(shape, lambda t: (0, 0))
+    rows = lambda width: pl.BlockSpec((TILE, width), lambda t: (i * tiles + t, 0))
+    ins = [meta, lat, rot, mine, other, q, qr, do] + ([] if out is None else [out])
     return pl.pallas_call(
-        attention_kernel,
-        grid=(2, tiles),
+        functools.partial(attention_kernel, i),
+        grid=(tiles,),
         out_shape=[
             jax.ShapeDtypeStruct(q.shape, bf16),
-            jax.ShapeDtypeStruct((128, LAT), f32),
-            jax.ShapeDtypeStruct((128, ROPE), f32),
-            jax.ShapeDtypeStruct((8 * HALF, 128), bf16),
-            jax.ShapeDtypeStruct((8 * HALF, 128), bf16),
+            jax.ShapeDtypeStruct((BLK, LAT), f32),
+            jax.ShapeDtypeStruct((BLK, ROPE), f32),
+            jax.ShapeDtypeStruct((4 * HALF, 128), bf16),
+            jax.ShapeDtypeStruct((4 * HALF, 128), bf16),
         ],
         in_specs=[
             SMEM,
             whole((128, LAT)),
             whole((128, ROPE)),
-            whole((8 * HALF, 128)),
-            whole((8 * HALF, 128)),
+            whole((4 * HALF, 128)),
+            whole((4 * HALF, 128)),
             rows(LAT),
             rows(ROPE),
             rows(LAT),
-        ],
+        ]
+        + ([] if out is None else [pl.BlockSpec(memory_space=pl.ANY)]),
         out_specs=[
             rows(LAT),
-            whole((128, LAT)),
-            whole((128, ROPE)),
-            whole((8 * HALF, 128)),
-            whole((8 * HALF, 128)),
+            whole((BLK, LAT)),
+            whole((BLK, ROPE)),
+            whole((4 * HALF, 128)),
+            whole((4 * HALF, 128)),
         ],
         scratch_shapes=[
-            pltpu.VMEM((2, 576, 128), bf16),
+            pltpu.VMEM((2, 4 * HALF, 128), bf16),
             pltpu.VMEM((SEL * BLK, LAT), bf16),
             pltpu.VMEM((SEL * BLK, ROPE), bf16),
             pltpu.VMEM((SEL * BLK, LAT), f32),
             pltpu.VMEM((SEL * BLK, ROPE), f32),
         ],
-        compiler_params=PARAMS,
+        input_output_aliases={} if out is None else {8: 0},
+        compiler_params=pltpu.CompilerParams(vmem_limit_bytes=58 * 1024 * 1024),
+        cost_estimate=pl.CostEstimate(flops=1000, bytes_accessed=1000, transcendentals=0),
         name="attention",
-    )(meta, lat, rot, mine, other, q, qr, do)
+    )(*ins)
 
 
 def slots_kernel(mine, recv, g):
-    g[0:1152] = mine[...]
-    g[1152:2304] = recv[...]
+    g[0:576] = mine[...]
+    g[576:1152] = recv[...]
 
 
 def plane_kernel(where_, *refs):
-    ins, outs, acc = refs[:4], refs[4:8], refs[8]
+    ins, outs, acc = refs[:8], refs[8:12], refs[12]
     acc[...] = jnp.zeros_like(acc)
-    for k in range(4):
-        for s in range(16):
-            f = where_[k * 16 + s]
-            acc[f] = acc[f] + ins[k][s * HALF : (s + 1) * HALF].astype(f32)
+    for i in range(2):
+        for k in range(4):
+            for j in range(8):
+                f = where_[k * 16 + (j // 4) * 8 + i * 4 + j % 4]
+                acc[f] = acc[f] + ins[i * 4 + k][j * HALF : (j + 1) * HALF].astype(f32)
     for k in range(4):
         for j in range(16):
-            outs[k][j * HALF : (j + 1) * HALF] = acc[k * 16 + j].astype(outs[k].dtype)
+            outs[k][j * HALF : (j + 1) * HALF] = acc[ORDER[k] * 16 + j].astype(outs[k].dtype)
 
 
 def sum_rows(ins, at):
@@ -279,7 +282,7 @@
 def column_kernel(*refs):
     ins, outs = refs[:4], refs[4:8]
     for j in range(16):
-        out, row = outs[j // 4], (j % 4) * HALF
+        out, row = outs[ORDER.index(j // 4)], (j % 4) * HALF
         out[row : row + HALF] = sum_rows(ins, j * HALF).astype(out.dtype)
 
 
@@ -290,17 +293,17 @@
         outs[j // 2][row : row + HALF] = sum_rows(ins, j * HALF)
 
 
-def half_sum_kernel(meta, mine, recv, dkl, dkr, out, units):
+def half_sum_kernel(meta, mine, recv, dkl0, dkl1, dkr0, dkr1, out, units):
     c = meta[0]
     units[c] = mine[...]
     units[1 - c] = recv[...]
     for i in range(2):
-        lo, hi = slice(i * 64, i * 64 + 32), slice(i * 64 + 32, i * 64 + 64)
-        packed = jnp.concatenate([dkr[lo, :], dkr[hi, :]], axis=1)
+        dkl, dkr = (dkl0, dkl1)[i], (dkr0, dkr1)[i]
+        packed = jnp.concatenate([dkr[0:32], dkr[32:64]], axis=1)
         for n in range(18):
             if n < 16:
                 l, r = n // 4, n % 4
-                own = dkl[i * 64 + r * UNIT : i * 64 + (r + 1) * UNIT, l * 128 : (l + 1) * 128]
+                own = dkl[r * UNIT : (r + 1) * UNIT, l * 128 : (l + 1) * 128]
             else:
                 own = packed[(n - 16) * UNIT : (n - 15) * UNIT]
             row = i * HALF + (n % 9) * UNIT
@@ -351,9 +354,13 @@
         chip_kernel, (mine, swap(other, "c")), [((576, 128), bf16), ((UNIT, 128), bf16)], name="chip"
     )
 
+    def each_of(parts, phase):
+        return [parts[0]] + [exchange(part, phase, k) for part, k in zip(parts[1:], ORDER[1:])]
+
     def all_of(a, phase):
-        return [a] + [exchange(a, phase, k) for k in (1, 2, 3)]
-
+        return [a] + [exchange(a, phase, k) for k in DISTANCES]
+
+    qr, chip = lax.optimization_barrier((query_rope.reshape(128 * HEADS, ROPE), chip))
     lines = all_of(chip, "u")
     (line,) = call(line_kernel, lines, [((2304, 128), bf16)], name="line")
     planes = all_of(line, "v")
@@ -368,46 +375,53 @@
     add_at = jnp.where(on_w == 0, pos, 64).reshape(-1)
     merge_at = on_w[0]
 
+    q = queries.reshape(128 * HEADS, LAT)
+    do = grad_out.reshape(128 * HEADS, LAT)
     packed = call(
         pack_kernel,
         [pack_at] + planes,
-        [((2304, 128), bf16)] * 4,
+        [((8 * HALF, 128), bf16)] * 8,
         [pltpu.VMEM((64, HALF, 128), bf16)],
         scalars=1,
         name="pack",
     )
-    got = [packed[0]] + [exchange(packed[k], "w", k) for k in (1, 2, 3)]
-    key_mine, key_other = call(
-        merge_kernel,
-        [merge_at] + got,
-        [((8 * HALF, 128), bf16)] * 2,
-        [pltpu.VMEM((64, HALF, 128), bf16)],
-        scalars=1,
-        name="merge",
-    )
-    key_recv = swap(key_other, "c")
-
-    q = queries.reshape(128 * HEADS, LAT)
-    do = grad_out.reshape(128 * HEADS, LAT)
-    qr = query_rope.reshape(128 * HEADS, ROPE)
-    out, dkl, dkr, g_mine, g_other = attention(meta, latent, rot, key_mine, key_recv, q, qr, do)
-
-    (slots,) = call(slots_kernel, (g_mine, swap(g_other, "c")), [((2304, 128), bf16)], name="slots")
+    got = [each_of(packed[i * 4 : i * 4 + 4], "w") for i in range(2)]
+    out, own_grads, grads = None, [], []
+    for i in range(2):
+        key_mine, key_other = call(
+            functools.partial(merge_kernel, i),
+            [merge_at] + got[i],
+            [((4 * HALF, 128), bf16)] * 2,
+            [pltpu.VMEM((32, HALF, 128), bf16)],
+            scalars=1,
+            name="merge",
+        )
+        key_recv = swap(key_other, "c")
+        out, dkl, dkr, g_mine, g_other = attention(
+            i, meta, latent, rot, key_mine, key_recv, q, qr, do, out
+        )
+        g_recv = swap(g_other, "c")
+        if grads:
+            *grads, g_recv = lax.optimization_barrier((*grads, g_recv))
+        (slots,) = call(slots_kernel, (g_mine, g_recv), [((8 * HALF, 128), bf16)], name="slots")
+        own_grads.append((dkl, dkr))
+        grads += all_of(slots, "w")
+        merge_at, meta, _ = lax.optimization_barrier((merge_at, meta, slots))
     sums = call(
         plane_kernel,
-        [add_at] + all_of(slots, "w"),
+        [add_at] + grads,
         [((2304, 128), bf16 if k else f32) for k in range(4)],
         [pltpu.VMEM((65, HALF, 128), f32)],
         scalars=1,
         name="plane",
     )
-    got = [sums[0]] + [exchange(sums[k], "v", k) for k in (1, 2, 3)]
+    got = each_of(sums, "v")
     sums = call(column_kernel, got, [((576, 128), bf16 if k else f32) for k in range(4)], name="column")
-    got = [sums[0]] + [exchange(sums[k], "u", k) for k in (1, 2, 3)]
+    got = each_of(sums, "u")
     f_mine, f_other = call(owner_kernel, got, [((288, 128), f32)] * 2, name="owner")
     (total,) = call(
         half_sum_kernel,
-        (meta, f_mine, swap(f_other, "c"), dkl, dkr),
+        (meta, f_mine, swap(f_other, "c"), own_grads[0][0], own_grads[1][0], own_grads[0][1], own_grads[1][1]),
         [((576, 128), bf16)],
         [pltpu.VMEM((2, 288, 128), f32)],
         scalars=1,

time: 149 us -> 151 us (1.013); the launches traced: 146 us -> 151 us
  local copies, waits for them, and re-layouts: 4.2 us -> 11 us
  waiting for transfers between devices: 72.3 us -> 66.4 us
  Pallas kernels: 20.7 us -> 24.1 us
    ppermute x21 -> x27, waiting for transfers between devices: 64.4 us -> 53.2 us  [exchange(): lax.ppermute(a, MESH, [(number(p), number(partner(p, phase, k))) for p in...]
    ppermute x5 -> x7, starting transfers between devices: 18.5 us -> 12.9 us  [swap(): return lax.ppermute(a, axis, [(0, 1), (1, 0)])]
    ppermute x5 -> x7, waiting for transfers between devices: 7.94 us -> 13.2 us  [swap(): return lax.ppermute(a, axis, [(0, 1), (1, 0)])]
    ppermute x21 -> x27, starting transfers between devices: 28.9 us -> 34.1 us  [exchange(): lax.ppermute(a, MESH, [(number(p), number(partner(p, phase, k))) for p in...]
    unnamed x8 -> x30, local copies, waits for them, and re-layouts: 2.43 us -> 7.49 us
    pallas_call x1 -> x2, Pallas kernels: 14.7 us -> 17.6 us  [attention(): pl.pallas_call(functools.partial(attention_kernel, i), grid=(tiles,), out...]
    reshape x1, local copies, waits for them, and re-layouts: 1.07 us -> 2.78 us  [shards(): query_rope.reshape(128 * HEADS, ROPE)]
    pallas_call x11 -> x13, Pallas kernels: 5.95 us -> 6.5 us  [call(): pl.pallas_call(kernel, out_shape=[jax.ShapeDtypeStruct(s, d) for s, d in...]
  transfers between devices with their start and end apart: 26 -> 34, of which waited for: 21 -> 18; matrix products, arithmetic and copies ran while one was open for 1% -> 2% of each run, Pallas kernels for 0% -> 12%
where the time goes in v2:
time: 151 us
  waiting for transfers between devices  66.4 us (44%)
  starting transfers between devices  47 us (31%)
  Pallas kernels  24.1 us (16%)
  local copies, waits for them, and re-layouts  11 us (7%)
    ppermute x27, waiting for transfers between devices, exchange(): lax.ppermute(a, MESH, [(number(p), number(partner(p, phase, k))) for p in...  53.2 us
    ppermute x27, starting transfers between devices, exchange(): lax.ppermute(a, MESH, [(number(p), number(partner(p, phase, k))) for p in...  34.1 us
    pallas_call x2, Pallas kernels, attention(): pl.pallas_call(functools.partial(attention_kernel, i), grid=(tiles,), out...  17.6 us
    ppermute x7, waiting for transfers between devices, swap(): return lax.ppermute(a, axis, [(0, 1), (1, 0)])  13.2 us
    ppermute x7, starting transfers between devices, swap(): return lax.ppermute(a, axis, [(0, 1), (1, 0)])  12.9 us
    unnamed x30, local copies, waits for them, and re-layouts  7.49 us
    pallas_call x13, Pallas kernels, call(): pl.pallas_call(kernel, out_shape=[jax.ShapeDtypeStruct(s, d) for s, d in...  6.5 us
  transfers between devices with their start and end apart: 34, of which 18 were waited for; matrix products, arithmetic and copies ran while one was open for 2% of the time, Pallas kernels for 12%

profile of v2, /device:TPU:1, one launch (start us, length us, event | category | flops | bytes accessed | tf_op | source)
XLA Modules:
  0.0 150.6 jit_solution(14245361111177741078)
XLA Ops:
  0.7 0.7 convert.3
  1.5 0.8 copy.12.rope
  2.8 0.9 copy-done
  3.7 0.8 prep.1
  4.5 0.6 copy-done.5
  5.1 3.2 %collective-permute-start = (bf16[304,128]{1,0:T(8,128)(2,1)S(1)}, bf16[304,128]{1,0:T(8,128)(2,1)S(1)}, u32[]{:S(2)}, u32[]{:S(2)}) collective-permute-start(bf16[304,128]{1,0:T(8,128)(2,1)S(1)} %get-tuple-element.53), channel_id=1, source_target_pairs={{0,2},{2,0},{1,3},{3,1},{4,6},{6,4},{5,7},{7,5},{8,10},{10,8},{9,1... | collective-permute-start | bytes 233480 | tf_op jit(solution)/shard_map/ppermute | solution.py:75
  8.3 2.8 %reshape.80.qr_ref = bf16[4096,64]{1,0:T(8,128)(2,1)} reshape(bf16[128,2048]{1,0:T(8,128)(2,1)} %param.9) | data formatting | bytes 1048576 | tf_op jit(solution)/shard_map/reshape | solution.py:363
  11.1 3.9 %collective-permute-start.6 = (bf16[576,128]{1,0:T(8,128)(2,1)S(1)}, bf16[576,128]{1,0:T(8,128)(2,1)S(1)}, u32[]{:S(2)}, u32[]{:S(2)}) collective-permute-start(bf16[576,128]{1,0:T(8,128)(2,1)S(1)} %get-tuple-element.57.refs_0_), channel_id=1, source_target_pairs={{0,13},{1,12},{2,15},{3,14},{4,8},{5,9},{6,10},{7,11},{8,4},{9,5},... | collective-permute-start | bytes 442376 | tf_op jit(solution)/shard_map/ppermute | solution.py:71
  15.0 1.9 %collective-permute-start.4 = (bf16[576,128]{1,0:T(8,128)(2,1)S(1)}, bf16[576,128]{1,0:T(8,128)(2,1)S(1)}, u32[]{:S(2)}, u32[]{:S(2)}) collective-permute-start(bf16[576,128]{1,0:T(8,128)(2,1)S(1)} %get-tuple-element.57.refs_0_), channel_id=1, source_target_pairs={{0,4},{1,5},{2,6},{3,7},{4,0},{5,1},{6,2},{7,3},{8,12},{9,13},{10,... | collective-permute-start | bytes 442376 | tf_op jit(solution)/shard_map/ppermute | solution.py:71
  16.9 2.3 %collective-permute-done.6.refs_3_ = bf16[576,128]{1,0:T(8,128)(2,1)S(1)} collective-permute-done((bf16[576,128]{1,0:T(8,128)(2,1)S(1)}, bf16[576,128]{1,0:T(8,128)(2,1)S(1)}, u32[]{:S(2)}, u32[]{:S(2)}) %collective-permute-start.6) | collective-permute-done | bytes 147488 | tf_op jit(solution)/shard_map/ppermute | solution.py:71
  19.3 4.9 %collective-permute-done.5.refs_2_ = bf16[576,128]{1,0:T(8,128)(2,1)S(1)} collective-permute-done((bf16[576,128]{1,0:T(8,128)(2,1)S(1)}, bf16[576,128]{1,0:T(8,128)(2,1)S(1)}, u32[]{:S(2)}, u32[]{:S(2)}) %collective-permute-start.5) | collective-permute-done | bytes 147488 | tf_op jit(solution)/shard_map/ppermute | solution.py:71
  24.2 2.8 %collective-permute-start.9 = (bf16[2304,128]{1,0:T(8,128)(2,1)S(1)}, bf16[2304,128]{1,0:T(8,128)(2,1)S(1)}, u32[]{:S(2)}, u32[]{:S(2)}) collective-permute-start(bf16[2304,128]{1,0:T(8,128)(2,1)S(1)} %line.1.refs_0_), channel_id=1, source_target_pairs={{0,192},{1,193},{2,50},{3,51},{4,196},{5,197},{6,54},{7,55},{8,200... | collective-permute-start | bytes 1769480 | tf_op jit(solution)/shard_map/ppermute | solution.py:71
  27.1 0.3 collective-permute-start.8
  27.7 2.5 %collective-permute-start.3 = (bf16[16,128]{1,0:T(8,128)(2,1)S(1)}, bf16[16,128]{1,0:T(8,128)(2,1)S(1)}, u32[]{:S(2)}, u32[]{:S(2)}) collective-permute-start(bf16[16,128]{1,0:T(8,128)(2,1)S(1)} %get-tuple-element.54), channel_id=1, source_target_pairs={{0,48},{1,49},{2,194},{3,195},{4,52},{5,53},{6,198},{7,199},{8,56}... | collective-permute-start | bytes 12296 | tf_op jit(solution)/shard_map/ppermute | solution.py:71
  30.2 0.5 collective-permute-start.2
  30.7 1.1 collective-permute-done.3
  32.0 2.6 %collective-permute-done.2 = bf16[16,128]{1,0:T(8,128)(2,1)S(1)} collective-permute-done((bf16[16,128]{1,0:T(8,128)(2,1)S(1)}, bf16[16,128]{1,0:T(8,128)(2,1)S(1)}, u32[]{:S(2)}, u32[]{:S(2)}) %collective-permute-start.2) | collective-permute-done | bytes 4128 | tf_op jit(solution)/shard_map/ppermute | solution.py:71
  34.9 6.2 %collective-permute-done.9.refs_3_ = bf16[2304,128]{1,0:T(8,128)(2,1)S(1)} collective-permute-done((bf16[2304,128]{1,0:T(8,128)(2,1)S(1)}, bf16[2304,128]{1,0:T(8,128)(2,1)S(1)}, u32[]{:S(2)}, u32[]{:S(2)}) %collective-permute-start.9) | collective-permute-done | bytes 589856 | tf_op jit(solution)/shard_map/ppermute | solution.py:71
  41.0 0.7 collective-permute-done.7.refs_1_
  41.8 0.9 pack.1
  42.6 2.6 %collective-permute-start.10 = (bf16[1152,128]{1,0:T(8,128)(2,1)S(1)}, bf16[1152,128]{1,0:T(8,128)(2,1)S(1)}, u32[]{:S(2)}, u32[]{:S(2)}) collective-permute-start(bf16[1152,128]{1,0:T(8,128)(2,1)S(1)} %get-tuple-element.59), channel_id=1, source_target_pairs={{0,48},{1,49},{2,194},{3,195},{4,52},{5,53},{6,198},{7,199},{8,56}... | collective-permute-start | bytes 884744 | tf_op jit(solution)/shard_map/ppermute | solution.py:71
  45.2 0.5 collective-permute-start.11
  46.0 7.0 %collective-permute-done.10.refs_1_ = bf16[1152,128]{1,0:T(8,128)(2,1)S(1)} collective-permute-done((bf16[1152,128]{1,0:T(8,128)(2,1)S(1)}, bf16[1152,128]{1,0:T(8,128)(2,1)S(1)}, u32[]{:S(2)}, u32[]{:S(2)}) %collective-permute-start.10) | collective-permute-done | bytes 294944 | tf_op jit(solution)/shard_map/ppermute | solution.py:71
  52.9 0.6 collective-permute-done.12.refs_3_
  53.6 0.6 merge.2
  54.2 0.7 copy-done.4
  54.9 2.8 %collective-permute-start.13 = (bf16[576,128]{1,0:T(8,128)(2,1)S(1)}, bf16[576,128]{1,0:T(8,128)(2,1)S(1)}, u32[]{:S(2)}, u32[]{:S(2)}) collective-permute-start(bf16[576,128]{1,0:T(8,128)(2,1)S(1)} %get-tuple-element.63), channel_id=1, source_target_pairs={{0,2},{2,0},{1,3},{3,1},{4,6},{6,4},{5,7},{7,5},{8,10},{10,8},{9,1... | collective-permute-start | bytes 442376 | tf_op jit(solution)/shard_map/ppermute | solution.py:75
  57.7 2.5 %collective-permute-start.15 = (bf16[1152,128]{1,0:T(8,128)(2,1)S(1)}, bf16[1152,128]{1,0:T(8,128)(2,1)S(1)}, u32[]{:S(2)}, u32[]{:S(2)}) collective-permute-start(bf16[1152,128]{1,0:T(8,128)(2,1)S(1)} %get-tuple-element.70), channel_id=1, source_target_pairs={{0,48},{1,49},{2,194},{3,195},{4,52},{5,53},{6,198},{7,199},{8,56}... | collective-permute-start | bytes 884744 | tf_op jit(solution)/shard_map/ppermute | solution.py:71
  60.2 0.5 collective-permute-start.16
  60.9 0.7 copy-done.13
  61.6 8.8 %attention.2 = (bf16[4096,512]{1,0:T(8,128)(2,1)}, f32[64,512]{1,0:T(8,128)}, f32[64,64]{1,0:T(8,128)}, bf16[576,128]{1,0:T(8,128)(2,1)}, bf16[576,128]{1,0:T(8,128)(2,1)}) custom-call(s32[2]{0:T(128)} %copy-done.10, bf16[128,512]{1,0:T(8,128)(2,1)} %lat.5, bf16[128,64]{1,0:T(8,128)(2,1)} %copy-done.5, bf16[576,128]{1,0:T(8,128)(2,1)} %copy-done.4, ...), custom_call_target="tpu_custom_call" | custom-call | flops 1000 | bytes 1000 | tf_op jit(solution)/shard_map/attention/pallas_call | solution.py:215
  70.4 0.9 collective-permute-start.14
  71.3 1.2 collective-permute-done.14.recv
  72.5 0.9 copy-done.2
  73.5 0.6 merge.3
  74.2 0.7 copy-done.3
  74.8 0.4 collective-permute-start.18
  75.2 2.5 %collective-permute-start.21 = (bf16[1152,128]{1,0:T(8,128)(2,1)S(1)}, bf16[1152,128]{1,0:T(8,128)(2,1)S(1)}, u32[]{:S(2)}, u32[]{:S(2)}) collective-permute-start(bf16[1152,128]{1,0:T(8,128)(2,1)S(1)} %slots.2.refs_0_), channel_id=1, source_target_pairs={{0,48},{1,49},{2,194},{3,195},{4,52},{5,53},{6,198},{7,199},{8,56}... | collective-permute-start | bytes 884744 | tf_op jit(solution)/shard_map/ppermute | solution.py:71
  77.7 0.5 collective-permute-start.20
  78.4 0.7 copy-done.12
  79.1 8.8 %attention.3 = (bf16[4096,512]{1,0:T(8,128)(2,1)}, f32[64,512]{1,0:T(8,128)}, f32[64,64]{1,0:T(8,128)}, bf16[576,128]{1,0:T(8,128)(2,1)}, bf16[576,128]{1,0:T(8,128)(2,1)}) custom-call(s32[2]{0:T(128)} %copy-done.10, bf16[128,512]{1,0:T(8,128)(2,1)} %lat.5, bf16[128,64]{1,0:T(8,128)(2,1)} %copy-done.5, ...), custom_call_target="tpu_custom_call", output_to_operand_aliasing={{0}: (8, {})} | custom-call | flops 1000 | bytes 1000 | tf_op jit(solution)/shard_map/attention/pallas_call | solution.py:215
  87.9 1.1 collective-permute-start.22
  89.0 1.2 collective-permute-done.22.recv
  90.3 0.9 copy-done.1
  91.2 2.6 %collective-permute-start.25 = (bf16[1152,128]{1,0:T(8,128)(2,1)S(1)}, bf16[1152,128]{1,0:T(8,128)(2,1)S(1)}, u32[]{:S(2)}, u32[]{:S(2)}) collective-permute-start(bf16[1152,128]{1,0:T(8,128)(2,1)S(1)} %slots.3.refs_4_), channel_id=1, source_target_pairs={{0,48},{1,49},{2,194},{3,195},{4,52},{5,53},{6,198},{7,199},{8,56}... | collective-permute-start | bytes 884744 | tf_op jit(solution)/shard_map/ppermute | solution.py:71
  93.7 0.5 collective-permute-start.24
  94.6 6.9 %collective-permute-done.25.refs_7_ = bf16[1152,128]{1,0:T(8,128)(2,1)S(1)} collective-permute-done((bf16[1152,128]{1,0:T(8,128)(2,1)S(1)}, bf16[1152,128]{1,0:T(8,128)(2,1)S(1)}, u32[]{:S(2)}, u32[]{:S(2)}) %collective-permute-start.25) | collective-permute-done | bytes 294944 | tf_op jit(solution)/shard_map/ppermute | solution.py:71
  101.5 0.6 collective-permute-done.23.refs_5_
  102.1 1.6 %plane.1 = (f32[2304,128]{1,0:T(8,128)S(1)}, bf16[2304,128]{1,0:T(8,128)(2,1)S(1)}, bf16[2304,128]{1,0:T(8,128)(2,1)S(1)}, bf16[2304,128]{1,0:T(8,128)(2,1)S(1)}) custom-call(s32[64]{0:T(128)S(1)} %broadcast_select_fusion.where_, bf16[1152,128]{1,0:T(8,128)(2,1)S(1)} %slots.2.refs_0_, bf16[1152,128]{1,0:T(8,128)(2,1)S(1)} %collective-permute-done.19.refs_1_, ...), custom_call_target="tpu_custom_call" | custom-call | tf_op jit(solution)/shard_map/plane/pallas_call | solution.py:33
  103.8 2.8 %collective-permute-start.26 = (bf16[2304,128]{1,0:T(8,128)(2,1)S(1)}, bf16[2304,128]{1,0:T(8,128)(2,1)S(1)}, u32[]{:S(2)}, u32[]{:S(2)}) collective-permute-start(bf16[2304,128]{1,0:T(8,128)(2,1)S(1)} %get-tuple-element.86), channel_id=1, source_target_pairs={{0,192},{1,193},{2,50},{3,51},{4,196},{5,197},{6,54},{7,55},{8,200... | collective-permute-start | bytes 1769480 | tf_op jit(solution)/shard_map/ppermute | solution.py:71
  106.6 0.4 collective-permute-start.27
  107.2 13.2 %collective-permute-done.26.refs_1_ = bf16[2304,128]{1,0:T(8,128)(2,1)S(1)} collective-permute-done((bf16[2304,128]{1,0:T(8,128)(2,1)S(1)}, bf16[2304,128]{1,0:T(8,128)(2,1)S(1)}, u32[]{:S(2)}, u32[]{:S(2)}) %collective-permute-start.26) | collective-permute-done | bytes 589856 | tf_op jit(solution)/shard_map/ppermute | solution.py:71
  120.4 0.7 collective-permute-done.28.refs_3_
  121.5 3.2 %collective-permute-start.29 = (bf16[576,128]{1,0:T(8,128)(2,1)S(1)}, bf16[576,128]{1,0:T(8,128)(2,1)S(1)}, u32[]{:S(2)}, u32[]{:S(2)}) collective-permute-start(bf16[576,128]{1,0:T(8,128)(2,1)S(1)} %get-tuple-element.90), channel_id=1, source_target_pairs={{0,13},{1,12},{2,15},{3,14},{4,8},{5,9},{6,10},{7,11},{8,4},{9,5},... | collective-permute-start | bytes 442376 | tf_op jit(solution)/shard_map/ppermute | solution.py:71
  124.7 1.9 %collective-permute-start.31 = (bf16[576,128]{1,0:T(8,128)(2,1)S(1)}, bf16[576,128]{1,0:T(8,128)(2,1)S(1)}, u32[]{:S(2)}, u32[]{:S(2)}) collective-permute-start(bf16[576,128]{1,0:T(8,128)(2,1)S(1)} %get-tuple-element.92), channel_id=1, source_target_pairs={{0,4},{1,5},{2,6},{3,7},{4,0},{5,1},{6,2},{7,3},{8,12},{9,13},{10,... | collective-permute-start | bytes 442376 | tf_op jit(solution)/shard_map/ppermute | solution.py:71
  126.6 0.6 collective-permute-done.29.refs_1_
  127.2 5.8 %collective-permute-done.30.refs_2_ = bf16[576,128]{1,0:T(8,128)(2,1)S(1)} collective-permute-done((bf16[576,128]{1,0:T(8,128)(2,1)S(1)}, bf16[576,128]{1,0:T(8,128)(2,1)S(1)}, u32[]{:S(2)}, u32[]{:S(2)}) %collective-permute-start.30) | collective-permute-done | bytes 147488 | tf_op jit(solution)/shard_map/ppermute | solution.py:71
  133.1 2.2 %collective-permute-start.32 = (f32[288,128]{1,0:T(8,128)S(1)}, f32[288,128]{1,0:T(8,128)S(1)}, u32[]{:S(2)}, u32[]{:S(2)}) collective-permute-start(f32[288,128]{1,0:T(8,128)S(1)} %get-tuple-element.94), channel_id=1, source_target_pairs={{0,2},{2,0},{1,3},{3,1},{4,6},{6,4},{5,7},{7,5},{8,10},{10,8},{9,1... | collective-permute-start | bytes 442376 | tf_op jit(solution)/shard_map/ppermute | solution.py:75
  135.3 1.0 collective-permute-done.32.recv
  136.3 0.6 half_sum.1.mine
  136.9 2.3 %collective-permute-start.33 = (bf16[576,128]{1,0:T(8,128)(2,1)S(1)}, bf16[576,128]{1,0:T(8,128)(2,1)S(1)}, u32[]{:S(2)}, u32[]{:S(2)}) collective-permute-start(bf16[576,128]{1,0:T(8,128)(2,1)S(1)} %half_sum.1.mine), channel_id=1, source_target_pairs={{0,1},{1,0},{2,3},{3,2},{4,5},{5,4},{6,7},{7,6},{8,9},{9,8},{10,11... | collective-permute-start | bytes 442376 | tf_op jit(solution)/shard_map/ppermute | solution.py:75
  139.2 9.8 %collective-permute-done.33.recv = bf16[576,128]{1,0:T(8,128)(2,1)S(1)} collective-permute-done((bf16[576,128]{1,0:T(8,128)(2,1)S(1)}, bf16[576,128]{1,0:T(8,128)(2,1)S(1)}, u32[]{:S(2)}, u32[]{:S(2)}) %collective-permute-start.33) | collective-permute-done | bytes 147488 | tf_op jit(solution)/shard_map/ppermute | solution.py:75
  149.0 0.9 final.1
  149.9 0.7 copy.13
  (73 shorter events, 3.3 us)
Async XLA Ops:
  2.4 58.5 %copy-start.10 = (s32[2]{0:T(128)}, s32[2]{0:T(128)S(1)}, u32[]{:S(2)}) copy-start(s32[2]{0:T(128)S(1)} %pad_add_fusion.meta) | copy-start | bytes 28
  2.8 0.9 copy-start
  4.5 0.6 copy-start.5
  5.1 6.0 %collective-permute-start = (bf16[304,128]{1,0:T(8,128)(2,1)S(1)}, bf16[304,128]{1,0:T(8,128)(2,1)S(1)}, u32[]{:S(2)}, u32[]{:S(2)}) collective-permute-start(bf16[304,128]{1,0:T(8,128)(2,1)S(1)} %get-tuple-element.53), channel_id=1, source_target_pairs={{0,2},{2,0},{1,3},{3,1},{4,6},{6,4},{5,7},{7,5},{8,10},{10,8},{9,1... | collective-permute-start | bytes 233480 | tf_op jit(solution)/shard_map/ppermute | solution.py:75
  11.1 8.1 %collective-permute-start.6 = (bf16[576,128]{1,0:T(8,128)(2,1)S(1)}, bf16[576,128]{1,0:T(8,128)(2,1)S(1)}, u32[]{:S(2)}, u32[]{:S(2)}) collective-permute-start(bf16[576,128]{1,0:T(8,128)(2,1)S(1)} %get-tuple-element.57.refs_0_), channel_id=1, source_target_pairs={{0,13},{1,12},{2,15},{3,14},{4,8},{5,9},{6,10},{7,11},{8,4},{9,5},... | collective-permute-start | bytes 442376 | tf_op jit(solution)/shard_map/ppermute | solution.py:71
  15.0 9.2 %collective-permute-start.5 = (bf16[576,128]{1,0:T(8,128)(2,1)S(1)}, bf16[576,128]{1,0:T(8,128)(2,1)S(1)}, u32[]{:S(2)}, u32[]{:S(2)}) collective-permute-start(bf16[576,128]{1,0:T(8,128)(2,1)S(1)} %get-tuple-element.57.refs_0_), channel_id=1, source_target_pairs={{0,8},{1,9},{2,10},{3,11},{4,12},{5,13},{6,14},{7,15},{8,0},{9,1},... | collective-permute-start | bytes 442376 | tf_op jit(solution)/shard_map/ppermute | solution.py:71
  15.0 9.2 %collective-permute-start.4 = (bf16[576,128]{1,0:T(8,128)(2,1)S(1)}, bf16[576,128]{1,0:T(8,128)(2,1)S(1)}, u32[]{:S(2)}, u32[]{:S(2)}) collective-permute-start(bf16[576,128]{1,0:T(8,128)(2,1)S(1)} %get-tuple-element.57.refs_0_), channel_id=1, source_target_pairs={{0,4},{1,5},{2,6},{3,7},{4,0},{5,1},{6,2},{7,3},{8,12},{9,13},{10,... | collective-permute-start | bytes 442376 | tf_op jit(solution)/shard_map/ppermute | solution.py:71
  24.2 16.8 %collective-permute-start.9 = (bf16[2304,128]{1,0:T(8,128)(2,1)S(1)}, bf16[2304,128]{1,0:T(8,128)(2,1)S(1)}, u32[]{:S(2)}, u32[]{:S(2)}) collective-permute-start(bf16[2304,128]{1,0:T(8,128)(2,1)S(1)} %line.1.refs_0_), channel_id=1, source_target_pairs={{0,192},{1,193},{2,50},{3,51},{4,196},{5,197},{6,54},{7,55},{8,200... | collective-permute-start | bytes 1769480 | tf_op jit(solution)/shard_map/ppermute | solution.py:71
  27.1 14.0 %collective-permute-start.8 = (bf16[2304,128]{1,0:T(8,128)(2,1)S(1)}, bf16[2304,128]{1,0:T(8,128)(2,1)S(1)}, u32[]{:S(2)}, u32[]{:S(2)}) collective-permute-start(bf16[2304,128]{1,0:T(8,128)(2,1)S(1)} %line.1.refs_0_), channel_id=1, source_target_pairs={{0,128},{1,129},{2,34},{3,35},{4,132},{5,133},{6,38},{7,39},{8,136... | collective-permute-start | bytes 1769480 | tf_op jit(solution)/shard_map/ppermute | solution.py:71
  27.4 14.3 %collective-permute-start.7 = (bf16[2304,128]{1,0:T(8,128)(2,1)S(1)}, bf16[2304,128]{1,0:T(8,128)(2,1)S(1)}, u32[]{:S(2)}, u32[]{:S(2)}) collective-permute-start(bf16[2304,128]{1,0:T(8,128)(2,1)S(1)} %line.1.refs_0_), channel_id=1, source_target_pairs={{0,64},{1,65},{2,18},{3,19},{4,68},{5,69},{6,22},{7,23},{8,72},{9,... | collective-permute-start | bytes 1769480 | tf_op jit(solution)/shard_map/ppermute | solution.py:71
  27.7 4.1 %collective-permute-start.3 = (bf16[16,128]{1,0:T(8,128)(2,1)S(1)}, bf16[16,128]{1,0:T(8,128)(2,1)S(1)}, u32[]{:S(2)}, u32[]{:S(2)}) collective-permute-start(bf16[16,128]{1,0:T(8,128)(2,1)S(1)} %get-tuple-element.54), channel_id=1, source_target_pairs={{0,48},{1,49},{2,194},{3,195},{4,52},{5,53},{6,198},{7,199},{8,56}... | collective-permute-start | bytes 12296 | tf_op jit(solution)/shard_map/ppermute | solution.py:71
  30.2 4.4 %collective-permute-start.2 = (bf16[16,128]{1,0:T(8,128)(2,1)S(1)}, bf16[16,128]{1,0:T(8,128)(2,1)S(1)}, u32[]{:S(2)}, u32[]{:S(2)}) collective-permute-start(bf16[16,128]{1,0:T(8,128)(2,1)S(1)} %get-tuple-element.54), channel_id=1, source_target_pairs={{0,32},{1,33},{2,130},{3,131},{4,36},{5,37},{6,134},{7,135},{8,40}... | collective-permute-start | bytes 12296 | tf_op jit(solution)/shard_map/ppermute | solution.py:71
  31.8 2.9 %collective-permute-start.1 = (bf16[16,128]{1,0:T(8,128)(2,1)S(1)}, bf16[16,128]{1,0:T(8,128)(2,1)S(1)}, u32[]{:S(2)}, u32[]{:S(2)}) collective-permute-start(bf16[16,128]{1,0:T(8,128)(2,1)S(1)} %get-tuple-element.54), channel_id=1, source_target_pairs={{0,16},{1,17},{2,66},{3,67},{4,20},{5,21},{6,70},{7,71},{8,24},{9,... | collective-permute-start | bytes 12296 | tf_op jit(solution)/shard_map/ppermute | solution.py:71
  42.6 10.3 %collective-permute-start.10 = (bf16[1152,128]{1,0:T(8,128)(2,1)S(1)}, bf16[1152,128]{1,0:T(8,128)(2,1)S(1)}, u32[]{:S(2)}, u32[]{:S(2)}) collective-permute-start(bf16[1152,128]{1,0:T(8,128)(2,1)S(1)} %get-tuple-element.59), channel_id=1, source_target_pairs={{0,48},{1,49},{2,194},{3,195},{4,52},{5,53},{6,198},{7,199},{8,56}... | collective-permute-start | bytes 884744 | tf_op jit(solution)/shard_map/ppermute | solution.py:71
  45.2 7.8 %collective-permute-start.11 = (bf16[1152,128]{1,0:T(8,128)(2,1)S(1)}, bf16[1152,128]{1,0:T(8,128)(2,1)S(1)}, u32[]{:S(2)}, u32[]{:S(2)}) collective-permute-start(bf16[1152,128]{1,0:T(8,128)(2,1)S(1)} %get-tuple-element.60), channel_id=1, source_target_pairs={{0,32},{1,33},{2,130},{3,131},{4,36},{5,37},{6,134},{7,135},{8,40}... | collective-permute-start | bytes 884744 | tf_op jit(solution)/shard_map/ppermute | solution.py:71
  45.7 7.9 %collective-permute-start.12 = (bf16[1152,128]{1,0:T(8,128)(2,1)S(1)}, bf16[1152,128]{1,0:T(8,128)(2,1)S(1)}, u32[]{:S(2)}, u32[]{:S(2)}) collective-permute-start(bf16[1152,128]{1,0:T(8,128)(2,1)S(1)} %get-tuple-element.61), channel_id=1, source_target_pairs={{0,16},{1,17},{2,66},{3,67},{4,20},{5,21},{6,70},{7,71},{8,24},{9,... | collective-permute-start | bytes 884744 | tf_op jit(solution)/shard_map/ppermute | solution.py:71
  54.2 0.7 copy-start.4
  54.9 6.1 %collective-permute-start.13 = (bf16[576,128]{1,0:T(8,128)(2,1)S(1)}, bf16[576,128]{1,0:T(8,128)(2,1)S(1)}, u32[]{:S(2)}, u32[]{:S(2)}) collective-permute-start(bf16[576,128]{1,0:T(8,128)(2,1)S(1)} %get-tuple-element.63), channel_id=1, source_target_pairs={{0,2},{2,0},{1,3},{3,1},{4,6},{6,4},{5,7},{7,5},{8,10},{10,8},{9,1... | collective-permute-start | bytes 442376 | tf_op jit(solution)/shard_map/ppermute | solution.py:75
  57.7 15.8 %collective-permute-start.15 = (bf16[1152,128]{1,0:T(8,128)(2,1)S(1)}, bf16[1152,128]{1,0:T(8,128)(2,1)S(1)}, u32[]{:S(2)}, u32[]{:S(2)}) collective-permute-start(bf16[1152,128]{1,0:T(8,128)(2,1)S(1)} %get-tuple-element.70), channel_id=1, source_target_pairs={{0,48},{1,49},{2,194},{3,195},{4,52},{5,53},{6,198},{7,199},{8,56}... | collective-permute-start | bytes 884744 | tf_op jit(solution)/shard_map/ppermute | solution.py:71
  60.2 13.3 %collective-permute-start.16 = (bf16[1152,128]{1,0:T(8,128)(2,1)S(1)}, bf16[1152,128]{1,0:T(8,128)(2,1)S(1)}, u32[]{:S(2)}, u32[]{:S(2)}) collective-permute-start(bf16[1152,128]{1,0:T(8,128)(2,1)S(1)} %get-tuple-element.71), channel_id=1, source_target_pairs={{0,32},{1,33},{2,130},{3,131},{4,36},{5,37},{6,134},{7,135},{8,40}... | collective-permute-start | bytes 884744 | tf_op jit(solution)/shard_map/ppermute | solution.py:71
  60.7 12.8 %collective-permute-start.17 = (bf16[1152,128]{1,0:T(8,128)(2,1)S(1)}, bf16[1152,128]{1,0:T(8,128)(2,1)S(1)}, u32[]{:S(2)}, u32[]{:S(2)}) collective-permute-start(bf16[1152,128]{1,0:T(8,128)(2,1)S(1)} %get-tuple-element.72), channel_id=1, source_target_pairs={{0,16},{1,17},{2,66},{3,67},{4,20},{5,21},{6,70},{7,71},{8,24},{9,... | collective-permute-start | bytes 884744 | tf_op jit(solution)/shard_map/ppermute | solution.py:71
  60.9 0.7 copy-start.13
  70.4 2.1 %collective-permute-start.14 = (bf16[576,128]{1,0:T(8,128)(2,1)}, bf16[576,128]{1,0:T(8,128)(2,1)S(1)}, u32[]{:S(2)}, u32[]{:S(2)}) collective-permute-start(bf16[576,128]{1,0:T(8,128)(2,1)} %get-tuple-element.66), channel_id=1, source_target_pairs={{0,2},{2,0},{1,3},{3,1},{4,6},{6,4},{5,7},{7,5},{8,10},{10,8},{9,1... | collective-permute-start | bytes 442376 | tf_op jit(solution)/shard_map/ppermute | solution.py:75
  72.5 0.9 copy-start.2
  74.1 0.7 copy-start.3
  74.8 3.6 %collective-permute-start.18 = (bf16[576,128]{1,0:T(8,128)(2,1)S(1)}, bf16[576,128]{1,0:T(8,128)(2,1)S(1)}, u32[]{:S(2)}, u32[]{:S(2)}) collective-permute-start(bf16[576,128]{1,0:T(8,128)(2,1)S(1)} %get-tuple-element.74), channel_id=1, source_target_pairs={{0,2},{2,0},{1,3},{3,1},{4,6},{6,4},{5,7},{7,5},{8,10},{10,8},{9,1... | collective-permute-start | bytes 442376 | tf_op jit(solution)/shard_map/ppermute | solution.py:75
  75.2 15.1 %collective-permute-start.21 = (bf16[1152,128]{1,0:T(8,128)(2,1)S(1)}, bf16[1152,128]{1,0:T(8,128)(2,1)S(1)}, u32[]{:S(2)}, u32[]{:S(2)}) collective-permute-start(bf16[1152,128]{1,0:T(8,128)(2,1)S(1)} %slots.2.refs_0_), channel_id=1, source_target_pairs={{0,48},{1,49},{2,194},{3,195},{4,52},{5,53},{6,198},{7,199},{8,56}... | collective-permute-start | bytes 884744 | tf_op jit(solution)/shard_map/ppermute | solution.py:71
  77.7 12.6 %collective-permute-start.20 = (bf16[1152,128]{1,0:T(8,128)(2,1)S(1)}, bf16[1152,128]{1,0:T(8,128)(2,1)S(1)}, u32[]{:S(2)}, u32[]{:S(2)}) collective-permute-start(bf16[1152,128]{1,0:T(8,128)(2,1)S(1)} %slots.2.refs_0_), channel_id=1, source_target_pairs={{0,32},{1,33},{2,130},{3,131},{4,36},{5,37},{6,134},{7,135},{8,40}... | collective-permute-start | bytes 884744 | tf_op jit(solution)/shard_map/ppermute | solution.py:71
  78.2 12.1 %collective-permute-start.19 = (bf16[1152,128]{1,0:T(8,128)(2,1)S(1)}, bf16[1152,128]{1,0:T(8,128)(2,1)S(1)}, u32[]{:S(2)}, u32[]{:S(2)}) collective-permute-start(bf16[1152,128]{1,0:T(8,128)(2,1)S(1)} %slots.2.refs_0_), channel_id=1, source_target_pairs={{0,16},{1,17},{2,66},{3,67},{4,20},{5,21},{6,70},{7,71},{8,24},{9,... | collective-permute-start | bytes 884744 | tf_op jit(solution)/shard_map/ppermute | solution.py:71
  78.4 0.7 copy-start.12
  79.1 57.2 %copy-start.6 = (f32[64,512]{1,0:T(8,128)S(1)}, f32[64,512]{1,0:T(8,128)}, u32[]{:S(2)}) copy-start(f32[64,512]{1,0:T(8,128)} %get-tuple-element.95.dkl0) | copy-start | bytes 393220
  79.1 57.2 %copy-start.8 = (f32[64,64]{1,0:T(8,128)S(1)}, f32[64,64]{1,0:T(8,128)}, u32[]{:S(2)}) copy-start(f32[64,64]{1,0:T(8,128)} %get-tuple-element.97.dkr0) | copy-start | bytes 49156
  87.9 48.4 %copy-start.11 = (s32[2]{0:T(128)S(1)}, s32[2]{0:T(128)}, u32[]{:S(2)}) copy-start(s32[2]{0:T(128)} %copy-done.10) | copy-start | bytes 28
  87.9 2.3 %collective-permute-start.22 = (bf16[576,128]{1,0:T(8,128)(2,1)}, bf16[576,128]{1,0:T(8,128)(2,1)S(1)}, u32[]{:S(2)}, u32[]{:S(2)}) collective-permute-start(bf16[576,128]{1,0:T(8,128)(2,1)} %get-tuple-element.78), channel_id=1, source_target_pairs={{0,2},{2,0},{1,3},{3,1},{4,6},{6,4},{5,7},{7,5},{8,10},{10,8},{9,1... | collective-permute-start | bytes 442376 | tf_op jit(solution)/shard_map/ppermute | solution.py:75
  90.2 0.9 copy-start.1
  91.2 45.1 %copy-start.7 = (f32[64,512]{1,0:T(8,128)S(1)}, f32[64,512]{1,0:T(8,128)}, u32[]{:S(2)}) copy-start(f32[64,512]{1,0:T(8,128)} %get-tuple-element.96.dkl1) | copy-start | bytes 393220
  91.2 45.1 %copy-start.9 = (f32[64,64]{1,0:T(8,128)S(1)}, f32[64,64]{1,0:T(8,128)}, u32[]{:S(2)}) copy-start(f32[64,64]{1,0:T(8,128)} %get-tuple-element.98.dkr1) | copy-start | bytes 49156
  91.2 10.3 %collective-permute-start.25 = (bf16[1152,128]{1,0:T(8,128)(2,1)S(1)}, bf16[1152,128]{1,0:T(8,128)(2,1)S(1)}, u32[]{:S(2)}, u32[]{:S(2)}) collective-permute-start(bf16[1152,128]{1,0:T(8,128)(2,1)S(1)} %slots.3.refs_4_), channel_id=1, source_target_pairs={{0,48},{1,49},{2,194},{3,195},{4,52},{5,53},{6,198},{7,199},{8,56}... | collective-permute-start | bytes 884744 | tf_op jit(solution)/shard_map/ppermute | solution.py:71
  93.7 7.8 %collective-permute-start.24 = (bf16[1152,128]{1,0:T(8,128)(2,1)S(1)}, bf16[1152,128]{1,0:T(8,128)(2,1)S(1)}, u32[]{:S(2)}, u32[]{:S(2)}) collective-permute-start(bf16[1152,128]{1,0:T(8,128)(2,1)S(1)} %slots.3.refs_4_), channel_id=1, source_target_pairs={{0,32},{1,33},{2,130},{3,131},{4,36},{5,37},{6,134},{7,135},{8,40}... | collective-permute-start | bytes 884744 | tf_op jit(solution)/shard_map/ppermute | solution.py:71
  94.3 7.9 %collective-permute-start.23 = (bf16[1152,128]{1,0:T(8,128)(2,1)S(1)}, bf16[1152,128]{1,0:T(8,128)(2,1)S(1)}, u32[]{:S(2)}, u32[]{:S(2)}) collective-permute-start(bf16[1152,128]{1,0:T(8,128)(2,1)S(1)} %slots.3.refs_4_), channel_id=1, source_target_pairs={{0,16},{1,17},{2,66},{3,67},{4,20},{5,21},{6,70},{7,71},{8,24},{9,... | collective-permute-start | bytes 884744 | tf_op jit(solution)/shard_map/ppermute | solution.py:71
  103.8 16.7 %collective-permute-start.26 = (bf16[2304,128]{1,0:T(8,128)(2,1)S(1)}, bf16[2304,128]{1,0:T(8,128)(2,1)S(1)}, u32[]{:S(2)}, u32[]{:S(2)}) collective-permute-start(bf16[2304,128]{1,0:T(8,128)(2,1)S(1)} %get-tuple-element.86), channel_id=1, source_target_pairs={{0,192},{1,193},{2,50},{3,51},{4,196},{5,197},{6,54},{7,55},{8,200... | collective-permute-start | bytes 1769480 | tf_op jit(solution)/shard_map/ppermute | solution.py:71
  106.6 13.9 %collective-permute-start.27 = (bf16[2304,128]{1,0:T(8,128)(2,1)S(1)}, bf16[2304,128]{1,0:T(8,128)(2,1)S(1)}, u32[]{:S(2)}, u32[]{:S(2)}) collective-permute-start(bf16[2304,128]{1,0:T(8,128)(2,1)S(1)} %get-tuple-element.87), channel_id=1, source_target_pairs={{0,128},{1,129},{2,34},{3,35},{4,132},{5,133},{6,38},{7,39},{8,136... | collective-permute-start | bytes 1769480 | tf_op jit(solution)/shard_map/ppermute | solution.py:71
  106.9 14.2 %collective-permute-start.28 = (bf16[2304,128]{1,0:T(8,128)(2,1)S(1)}, bf16[2304,128]{1,0:T(8,128)(2,1)S(1)}, u32[]{:S(2)}, u32[]{:S(2)}) collective-permute-start(bf16[2304,128]{1,0:T(8,128)(2,1)S(1)} %get-tuple-element.88), channel_id=1, source_target_pairs={{0,64},{1,65},{2,18},{3,19},{4,68},{5,69},{6,22},{7,23},{8,72},{9,... | collective-permute-start | bytes 1769480 | tf_op jit(solution)/shard_map/ppermute | solution.py:71
  121.5 5.8 %collective-permute-start.29 = (bf16[576,128]{1,0:T(8,128)(2,1)S(1)}, bf16[576,128]{1,0:T(8,128)(2,1)S(1)}, u32[]{:S(2)}, u32[]{:S(2)}) collective-permute-start(bf16[576,128]{1,0:T(8,128)(2,1)S(1)} %get-tuple-element.90), channel_id=1, source_target_pairs={{0,13},{1,12},{2,15},{3,14},{4,8},{5,9},{6,10},{7,11},{8,4},{9,5},... | collective-permute-start | bytes 442376 | tf_op jit(solution)/shard_map/ppermute | solution.py:71
  124.7 8.3 %collective-permute-start.30 = (bf16[576,128]{1,0:T(8,128)(2,1)S(1)}, bf16[576,128]{1,0:T(8,128)(2,1)S(1)}, u32[]{:S(2)}, u32[]{:S(2)}) collective-permute-start(bf16[576,128]{1,0:T(8,128)(2,1)S(1)} %get-tuple-element.91), channel_id=1, source_target_pairs={{0,8},{1,9},{2,10},{3,11},{4,12},{5,13},{6,14},{7,15},{8,0},{9,1},... | collective-permute-start | bytes 442376 | tf_op jit(solution)/shard_map/ppermute | solution.py:71
  124.7 8.3 %collective-permute-start.31 = (bf16[576,128]{1,0:T(8,128)(2,1)S(1)}, bf16[576,128]{1,0:T(8,128)(2,1)S(1)}, u32[]{:S(2)}, u32[]{:S(2)}) collective-permute-start(bf16[576,128]{1,0:T(8,128)(2,1)S(1)} %get-tuple-element.92), channel_id=1, source_target_pairs={{0,4},{1,5},{2,6},{3,7},{4,0},{5,1},{6,2},{7,3},{8,12},{9,13},{10,... | collective-permute-start | bytes 442376 | tf_op jit(solution)/shard_map/ppermute | solution.py:71
  133.1 3.2 %collective-permute-start.32 = (f32[288,128]{1,0:T(8,128)S(1)}, f32[288,128]{1,0:T(8,128)S(1)}, u32[]{:S(2)}, u32[]{:S(2)}) collective-permute-start(f32[288,128]{1,0:T(8,128)S(1)} %get-tuple-element.94), channel_id=1, source_target_pairs={{0,2},{2,0},{1,3},{3,1},{4,6},{6,4},{5,7},{7,5},{8,10},{10,8},{9,1... | collective-permute-start | bytes 442376 | tf_op jit(solution)/shard_map/ppermute | solution.py:75
  136.9 12.0 %collective-permute-start.33 = (bf16[576,128]{1,0:T(8,128)(2,1)S(1)}, bf16[576,128]{1,0:T(8,128)(2,1)S(1)}, u32[]{:S(2)}, u32[]{:S(2)}) collective-permute-start(bf16[576,128]{1,0:T(8,128)(2,1)S(1)} %half_sum.1.mine), channel_id=1, source_target_pairs={{0,1},{1,0},{2,3},{3,2},{4,5},{5,4},{6,7},{7,6},{8,9},{9,8},{10,11... | collective-permute-start | bytes 442376 | tf_op jit(solution)/shard_map/ppermute | solution.py:75

commit v3 on v1

--- a/solution.py
+++ b/solution.py
@@ -14,10 +14,12 @@
 HEADS = 32
 UNIT = 16
 HALF = 144
-TILE = 512
+TILE = 1024
+ORDER = (0, 3, 2, 1)
 
 softmax_scale = 192.0 ** (-0.5)
 rope_base = 10000.0
+log2_e = 1.4426950408889634
 
 bf16 = jnp.bfloat16
 f32 = jnp.float32
@@ -76,10 +78,10 @@
 def prep_kernel(meta, lat, rope, cosine, sine, sel, mine, other, rot_out, units):
     c = meta[0]
     x = rope[...].astype(f32)
-    lo, hi = x[:, :32], x[:, 32:]
+    lo, hi = x[:32], x[32:]
     rot = jnp.concatenate(
-        [lo * cosine[...] - hi * sine[...], hi * cosine[...] + lo * sine[...]], axis=1
-    ).astype(bf16)
+        [lo * cosine[...] - hi * sine[...], hi * cosine[...] + lo * sine[...]], axis=0
+    ).T.astype(bf16)
     rot_out[...] = rot
     for i in range(2):
         packed = jnp.concatenate([rot[i * 64 : i * 64 + 32], rot[i * 64 + 32 : i * 64 + 64]], axis=1)
@@ -107,23 +109,24 @@
 
 
 def line_kernel(*refs):
+    for k in range(3):
+        refs[3][k * 576 : (k + 1) * 576] = refs[k][...]
+
+
+def pack_kernel(where_, *refs):
+    own, rest, outs, held = refs[:4], refs[4:8], refs[8:12], refs[12]
     for k in range(4):
-        refs[4][k * 576 : (k + 1) * 576] = refs[k][...]
-
-
-def pack_kernel(where_, *refs):
-    ins, outs, held = refs[:4], refs[4:8], refs[8]
-    for k in range(4):
-        held[k * 16 : (k + 1) * 16] = ins[k][...].reshape(16, HALF, 128)
+        held[k * 16 : k * 16 + 4] = own[k][...].reshape(4, HALF, 128)
+        held[k * 16 + 4 : k * 16 + 16] = rest[k][...].reshape(12, HALF, 128)
     for k in range(4):
         for s in range(16):
-            outs[k][s * HALF : (s + 1) * HALF] = held[where_[k * 16 + s]]
+            outs[k][s * HALF : (s + 1) * HALF] = held[where_[ORDER[k] * 16 + s]]
 
 
 def merge_kernel(where_, *refs):
     ins, mine, other, held = refs[:4], refs[4], refs[5], refs[6]
     for k in range(4):
-        held[k * 16 : (k + 1) * 16] = ins[k][...].reshape(16, HALF, 128)
+        held[ORDER[k] * 16 : (ORDER[k] + 1) * 16] = ins[k][...].reshape(16, HALF, 128)
     for s in range(16):
         out = mine if s < 8 else other
         row = (s % 8) * HALF
@@ -161,29 +164,42 @@
         acc[...] = jnp.zeros_like(acc)
         acc_r[...] = jnp.zeros_like(acc_r)
 
-    q, qr, do = q_ref[...], qr_ref[...], do_ref[...]
     nt = (((1,), (1,)), ((), ()))
-    raw = lax.dot_general(keys[...], q, nt, preferred_element_type=f32)
-    raw = raw + lax.dot_general(keys_r[...], qr, nt, preferred_element_type=f32)
-    key_row = lax.broadcasted_iota(jnp.int32, raw.shape, 0)
-    query = lax.broadcasted_iota(jnp.int32, raw.shape, 1) // HEADS + t * (TILE // HEADS)
     limit = jnp.minimum(block + 1, SEL) * BLK
-    allowed = (key_row < limit) & ((key_row >= BLK) | (key_row <= query))
-    raw = jnp.where(allowed, raw, -jnp.inf)
-    top = jnp.max(raw, axis=0, keepdims=True)
-    expon = jnp.exp((raw - top) * softmax_scale)
-    probs = expon * (1.0 / jnp.sum(expon, axis=0, keepdims=True))
-    probs_low = probs.astype(bf16)
-    dprobs = lax.dot_general(keys[...], do, nt, preferred_element_type=f32)
-    row_delta = jnp.sum(probs * dprobs, axis=0, keepdims=True)
-    dscores = (probs * (dprobs - row_delta) * softmax_scale).astype(bf16)
-    out_ref[...] = lax.dot_general(
-        probs_low, keys[...], (((0,), (0,)), ((), ())), preferred_element_type=f32
-    ).astype(bf16)
-    acc[...] += jnp.dot(dscores, q, preferred_element_type=f32) + jnp.dot(
-        probs_low, do, preferred_element_type=f32
-    )
-    acc_r[...] += jnp.dot(dscores, qr, preferred_element_type=f32)
+    part = TILE // 4
+    grad = jnp.zeros((SEL * BLK, LAT), f32)
+    grad_r = jnp.zeros((SEL * BLK, ROPE), f32)
+    raws, dps = [], []
+    for j in range(4):
+        rows = slice(j * part, (j + 1) * part)
+        q, qr, do = q_ref[rows, :], qr_ref[rows, :], do_ref[rows, :]
+        raw = lax.dot_general(keys[...], q, nt, preferred_element_type=f32)
+        raw = raw + lax.dot_general(keys_r[...], qr, nt, preferred_element_type=f32)
+        raws.append(raw)
+        dps.append(lax.dot_general(keys[...], do, nt, preferred_element_type=f32))
+    for j in range(4):
+        rows = slice(j * part, (j + 1) * part)
+        q, qr, do = q_ref[rows, :], qr_ref[rows, :], do_ref[rows, :]
+        raw, dprobs = raws[j], dps[j]
+        key_row = lax.broadcasted_iota(jnp.int32, (BLK, part), 0)
+        query = lax.broadcasted_iota(jnp.int32, (BLK, part), 1) // HEADS + t * (TILE // HEADS) + j * (part // HEADS)
+        bands = [jnp.where(key_row <= query, raw[:BLK], -jnp.inf)]
+        for s in range(1, SEL):
+            bands.append(raw[s * BLK : (s + 1) * BLK] + jnp.where(s * BLK < limit, 0.0, -jnp.inf))
+        raw = jnp.concatenate(bands, axis=0)
+        top = jnp.max(raw, axis=0, keepdims=True)
+        expon = jnp.exp2((raw - top) * (softmax_scale * log2_e))
+        probs = expon * (1.0 / jnp.sum(expon, axis=0, keepdims=True))
+        probs_low = probs.astype(bf16)
+        row_delta = jnp.sum(probs * dprobs, axis=0, keepdims=True)
+        dscores = (probs * ((dprobs - row_delta) * softmax_scale)).astype(bf16)
+        out_ref[rows, :] = lax.dot_general(
+            probs_low, keys[...], (((0,), (0,)), ((), ())), preferred_element_type=f32
+        ).astype(bf16)
+        grad = grad + jnp.dot(dscores, q, preferred_element_type=f32) + jnp.dot(probs_low, do, preferred_element_type=f32)
+        grad_r = grad_r + jnp.dot(dscores, qr, preferred_element_type=f32)
+    acc[...] += grad
+    acc_r[...] += grad_r
 
     @pl.when(t == pl.num_programs(1) - 1)
     def _():
@@ -258,7 +274,7 @@
 
 
 def plane_kernel(where_, *refs):
-    ins, outs, acc = refs[:4], refs[4:8], refs[8]
+    ins, rest, own, acc = refs[:4], refs[4:8], refs[8:12], refs[12]
     acc[...] = jnp.zeros_like(acc)
     for k in range(4):
         for s in range(16):
@@ -266,25 +282,26 @@
             acc[f] = acc[f] + ins[k][s * HALF : (s + 1) * HALF].astype(f32)
     for k in range(4):
         for j in range(16):
-            outs[k][j * HALF : (j + 1) * HALF] = acc[k * 16 + j].astype(outs[k].dtype)
+            out, row = (own[k], j) if j < 4 else (rest[k], j - 4)
+            out[row * HALF : (row + 1) * HALF] = acc[ORDER[k] * 16 + j].astype(out.dtype)
 
 
 def sum_rows(ins, at):
-    total = ins[0][at : at + HALF]
-    for k in range(1, 4):
-        total = total + ins[k][at : at + HALF].astype(f32)
+    total = ins[0][at : at + HALF].astype(f32)
+    for part in ins[1:]:
+        total = total + part[at : at + HALF].astype(f32)
     return total
 
 
 def column_kernel(*refs):
-    ins, outs = refs[:4], refs[4:8]
-    for j in range(16):
-        out, row = outs[j // 4], (j % 4) * HALF
-        out[row : row + HALF] = sum_rows(ins, j * HALF).astype(out.dtype)
+    ins, outs = refs[:4], refs[4:7]
+    for j in range(12):
+        out, row = outs[ORDER.index(j // 4 + 1) - 1], (j % 4) * HALF
+        out[row : row + HALF] = sum_rows(ins, j * HALF).astype(bf16)
 
 
 def owner_kernel(*refs):
-    ins, outs = refs[:4], refs[4:6]
+    ins, outs = refs[:7], refs[7:9]
     for j in range(4):
         row = (j % 2) * HALF
         outs[j // 2][row : row + HALF] = sum_rows(ins, j * HALF)
@@ -309,6 +326,7 @@
 
 
 def final_kernel(mine, recv, cosine, sine, lat_out, rope_out):
+    parts = []
     for i in range(2):
         for n in range(16):
             l, r = n // 4, n % 4
@@ -318,12 +336,10 @@
             ].astype(f32) + recv[at : at + UNIT].astype(f32)
         at = (i * 18 + 16) * UNIT
         packed = mine[at : at + 32].astype(f32) + recv[at : at + 32].astype(f32)
-        for part in range(2):
-            rows = slice(i * 64 + part * 32, i * 64 + part * 32 + 32)
-            g = packed[:, part * 64 : part * 64 + 64]
-            lo, hi = g[:, :32], g[:, 32:]
-            cs, sn = cosine[rows, :], sine[rows, :]
-            rope_out[rows, :] = jnp.concatenate([lo * cs + hi * sn, hi * cs - lo * sn], axis=1)
+        parts += [packed[:, :64], packed[:, 64:]]
+    g = jnp.concatenate(parts, axis=0).T
+    lo, hi, cs, sn = g[:32], g[32:], cosine[...], sine[...]
+    rope_out[...] = jnp.concatenate([lo * cs + hi * sn, hi * cs - lo * sn], axis=0)
 
 
 def shards(latent, rope_key, queries, query_rope, grad_out, sel_blocks):
@@ -334,14 +350,14 @@
     positions = ctx * 128 + jnp.arange(128, dtype=jnp.int32)
     freq_steps = jnp.arange(ROPE // 2, dtype=f32)
     inverse_freq = rope_base ** (-2.0 * freq_steps / ROPE)
-    angles = positions.astype(f32)[:, None] * inverse_freq[None, :]
+    angles = positions.astype(f32)[None, :] * inverse_freq[:, None]
     cosine, sine = jnp.cos(angles), jnp.sin(angles)
 
     sel_row = sel_blocks[:, 1:].reshape(1, 8).astype(bf16)
     sel_unit = jnp.broadcast_to(jnp.pad(sel_row, ((0, 0), (0, 120))), (UNIT, 128))
     mine, other, rot = call(
         prep_kernel,
-        (meta, latent, rope_key, cosine, sine, sel_unit),
+        (meta, latent, rope_key.T, cosine, sine, sel_unit),
         [((304, 128), bf16), ((304, 128), bf16), ((128, ROPE), bf16)],
         [pltpu.VMEM((2, 304, 128), bf16)],
         scalars=1,
@@ -354,9 +370,15 @@
     def all_of(a, phase):
         return [a] + [exchange(a, phase, k) for k in (1, 2, 3)]
 
+    def each_of(parts, phase):
+        return [exchange(part, phase, k) for part, k in zip(parts, ORDER[1:])]
+
+    own_plane = all_of(chip, "v")
     lines = all_of(chip, "u")
-    (line,) = call(line_kernel, lines, [((2304, 128), bf16)], name="line")
-    planes = all_of(line, "v")
+    got = lax.optimization_barrier((*own_plane[1:], *lines[1:]))
+    own_plane = [chip, *got[:3]]
+    (line,) = call(line_kernel, got[3:], [((1728, 128), bf16)], name="line")
+    rest_plane = all_of(line, "v")
 
     asked = jnp.stack([t[:2, :8] for t in all_of(sel, "w")]).astype(jnp.int32).reshape(4, 16)
     sx, sy, sz = asked >> 6, (asked >> 4) & 3, (asked >> 2) & 3
@@ -370,13 +392,13 @@
 
     packed = call(
         pack_kernel,
-        [pack_at] + planes,
+        [pack_at] + own_plane + rest_plane,
         [((2304, 128), bf16)] * 4,
         [pltpu.VMEM((64, HALF, 128), bf16)],
         scalars=1,
         name="pack",
     )
-    got = [packed[0]] + [exchange(packed[k], "w", k) for k in (1, 2, 3)]
+    got = [packed[0]] + each_of(packed[1:], "w")
     key_mine, key_other = call(
         merge_kernel,
         [merge_at] + got,
@@ -396,14 +418,16 @@
     sums = call(
         plane_kernel,
         [add_at] + all_of(slots, "w"),
-        [((2304, 128), bf16 if k else f32) for k in range(4)],
+        [((rows, 128), bf16 if k else f32) for rows in (1728, 576) for k in range(4)],
         [pltpu.VMEM((65, HALF, 128), f32)],
         scalars=1,
         name="plane",
     )
-    got = [sums[0]] + [exchange(sums[k], "v", k) for k in (1, 2, 3)]
-    sums = call(column_kernel, got, [((576, 128), bf16 if k else f32) for k in range(4)], name="column")
-    got = [sums[0]] + [exchange(sums[k], "u", k) for k in (1, 2, 3)]
+    rest, own = sums[:4], sums[4:]
+    columns = call(
+        column_kernel, [rest[0]] + each_of(rest[1:], "v"), [((576, 128), bf16)] * 3, name="column"
+    )
+    got = [own[0]] + each_of(own[1:], "v") + each_of(columns, "u")
     f_mine, f_other = call(owner_kernel, got, [((288, 128), f32)] * 2, name="owner")
     (total,) = call(
         half_sum_kernel,
@@ -416,10 +440,10 @@
     d_latent, d_rope_key = call(
         final_kernel,
         (total, swap(total, "h"), cosine, sine),
-        [((128, LAT), f32), ((128, ROPE), f32)],
+        [((128, LAT), f32), ((ROPE, 128), f32)],
         name="final",
     )
-    return out.reshape(128, HEADS, LAT), d_latent, d_rope_key
+    return out.reshape(128, HEADS, LAT), d_latent, d_rope_key.T
 
 
 def solution(mesh):

time: 149 us -> 137 us (0.919); the launches traced: 146 us -> 137 us
  waiting for transfers between devices: 72.3 us -> 65.5 us
  Pallas kernels: 20.7 us -> 18.9 us
    ppermute x21 -> x27, waiting for transfers between devices: 64.4 us -> 55.4 us  [exchange(): lax.ppermute(a, MESH, [(number(p), number(partner(p, phase, k))) for p in...]
    ppermute x5, waiting for transfers between devices: 7.94 us -> 10.1 us  [swap(): return lax.ppermute(a, axis, [(0, 1), (1, 0)])]
    ppermute x5, starting transfers between devices: 18.5 us -> 16.3 us  [swap(): return lax.ppermute(a, axis, [(0, 1), (1, 0)])]
    ppermute x21 -> x27, starting transfers between devices: 28.9 us -> 30.7 us  [exchange(): lax.ppermute(a, MESH, [(number(p), number(partner(p, phase, k))) for p in...]
    pallas_call x1, Pallas kernels: 14.7 us -> 13.1 us  [attention(): pl.pallas_call(attention_kernel, grid=(2, tiles), out_shape=[jax.ShapeDty...]
  transfers between devices with their start and end apart: 26 -> 32, of which waited for: 21 -> 21; matrix products, arithmetic and copies ran while one was open for 1% -> 1% of each run, Pallas kernels for 0% -> 0%
where the time goes in v3:
time: 137 us
  waiting for transfers between devices  65.5 us (48%)
  starting transfers between devices  47 us (34%)
  Pallas kernels  18.9 us (14%)
  local copies, waits for them, and re-layouts  3.4 us (2%)
    ppermute x27, waiting for transfers between devices, exchange(): lax.ppermute(a, MESH, [(number(p), number(partner(p, phase, k))) for p in...  55.4 us
    ppermute x27, starting transfers between devices, exchange(): lax.ppermute(a, MESH, [(number(p), number(partner(p, phase, k))) for p in...  30.7 us
    ppermute x5, starting transfers between devices, swap(): return lax.ppermute(a, axis, [(0, 1), (1, 0)])  16.3 us
    pallas_call x1, Pallas kernels, attention(): pl.pallas_call(attention_kernel, grid=(2, tiles), out_shape=[jax.ShapeDty...  13.1 us
    ppermute x5, waiting for transfers between devices, swap(): return lax.ppermute(a, axis, [(0, 1), (1, 0)])  10.1 us
    pallas_call x11, Pallas kernels, call(): pl.pallas_call(kernel, out_shape=[jax.ShapeDtypeStruct(s, d) for s, d in...  5.79 us
  transfers between devices with their start and end apart: 32, of which 21 were waited for; matrix products, arithmetic and copies ran while one was open for 1% of the time, Pallas kernels for 0%

profile of v3, /device:TPU:1, one launch (start us, length us, event | category | flops | bytes accessed | tf_op | source)
XLA Modules:
  0.0 136.6 jit_solution(17932493936889717297)
XLA Ops:
  0.7 0.7 convert.3
  1.6 0.1 multiply_sine_fusion
  1.8 0.9 copy-done
  2.7 0.7 copy-done.2
  3.4 0.7 prep.1
  4.1 3.3 %collective-permute-start = (bf16[304,128]{1,0:T(8,128)(2,1)S(1)}, bf16[304,128]{1,0:T(8,128)(2,1)S(1)}, u32[]{:S(2)}, u32[]{:S(2)}) collective-permute-start(bf16[304,128]{1,0:T(8,128)(2,1)S(1)} %get-tuple-element.42), channel_id=1, source_target_pairs={{0,2},{2,0},{1,3},{3,1},{4,6},{6,4},{5,7},{7,5},{8,10},{10,8},{9,1... | collective-permute-start | bytes 233480 | tf_op jit(solution)/shard_map/ppermute | solution.py:75
  7.5 0.9 collective-permute-done.recv
  8.4 3.9 %collective-permute-start.9 = (bf16[576,128]{1,0:T(8,128)(2,1)S(1)}, bf16[576,128]{1,0:T(8,128)(2,1)S(1)}, u32[]{:S(2)}, u32[]{:S(2)}) collective-permute-start(bf16[576,128]{1,0:T(8,128)(2,1)S(1)} %get-tuple-element.44.refs_0_), channel_id=1, source_target_pairs={{0,13},{1,12},{2,15},{3,14},{4,8},{5,9},{6,10},{7,11},{8,4},{9,5},... | collective-permute-start | bytes 442376 | tf_op jit(solution)/shard_map/ppermute | solution.py:71
  12.3 1.9 %collective-permute-start.7 = (bf16[576,128]{1,0:T(8,128)(2,1)S(1)}, bf16[576,128]{1,0:T(8,128)(2,1)S(1)}, u32[]{:S(2)}, u32[]{:S(2)}) collective-permute-start(bf16[576,128]{1,0:T(8,128)(2,1)S(1)} %get-tuple-element.44.refs_0_), channel_id=1, source_target_pairs={{0,4},{1,5},{2,6},{3,7},{4,0},{5,1},{6,2},{7,3},{8,12},{9,13},{10,... | collective-permute-start | bytes 442376 | tf_op jit(solution)/shard_map/ppermute | solution.py:71
  14.2 2.7 %collective-permute-start.6 = (bf16[576,128]{1,0:T(8,128)(2,1)S(1)}, bf16[576,128]{1,0:T(8,128)(2,1)S(1)}, u32[]{:S(2)}, u32[]{:S(2)}) collective-permute-start(bf16[576,128]{1,0:T(8,128)(2,1)S(1)} %get-tuple-element.44.refs_0_), channel_id=1, source_target_pairs={{0,192},{1,193},{2,50},{3,51},{4,196},{5,197},{6,54},{7,55},{8,200... | collective-permute-start | bytes 442376 | tf_op jit(solution)/shard_map/ppermute | solution.py:71
  17.0 0.3 collective-permute-start.5
  17.3 0.2 collective-permute-start.4
  17.5 3.9 %collective-permute-done.8.refs_1_ = bf16[576,128]{1,0:T(8,128)(2,1)S(1)} collective-permute-done((bf16[576,128]{1,0:T(8,128)(2,1)S(1)}, bf16[576,128]{1,0:T(8,128)(2,1)S(1)}, u32[]{:S(2)}, u32[]{:S(2)}) %collective-permute-start.8) | collective-permute-done | bytes 147488 | tf_op jit(solution)/shard_map/ppermute | solution.py:71
  21.5 1.0 collective-permute-done.5.refs_2_
  22.5 2.1 %collective-permute-start.12 = (bf16[1728,128]{1,0:T(8,128)(2,1)S(1)}, bf16[1728,128]{1,0:T(8,128)(2,1)S(1)}, u32[]{:S(2)}, u32[]{:S(2)}) collective-permute-start(bf16[1728,128]{1,0:T(8,128)(2,1)S(1)} %line.1.refs_4_), channel_id=1, source_target_pairs={{0,192},{1,193},{2,50},{3,51},{4,196},{5,197},{6,54},{7,55},{8,200... | collective-permute-start | bytes 1327112 | tf_op jit(solution)/shard_map/ppermute | solution.py:71
  24.6 0.3 collective-permute-start.11
  25.0 0.8 collective-permute-start.10
  25.8 2.5 %collective-permute-start.3 = (bf16[16,128]{1,0:T(8,128)(2,1)S(1)}, bf16[16,128]{1,0:T(8,128)(2,1)S(1)}, u32[]{:S(2)}, u32[]{:S(2)}) collective-permute-start(bf16[16,128]{1,0:T(8,128)(2,1)S(1)} %get-tuple-element.43), channel_id=1, source_target_pairs={{0,48},{1,49},{2,194},{3,195},{4,52},{5,53},{6,198},{7,199},{8,56}... | collective-permute-start | bytes 12296 | tf_op jit(solution)/shard_map/ppermute | solution.py:71
  28.3 0.5 collective-permute-start.2
  28.8 1.0 collective-permute-done.3
  30.0 2.6 %collective-permute-done.2 = bf16[16,128]{1,0:T(8,128)(2,1)S(1)} collective-permute-done((bf16[16,128]{1,0:T(8,128)(2,1)S(1)}, bf16[16,128]{1,0:T(8,128)(2,1)S(1)}, u32[]{:S(2)}, u32[]{:S(2)}) %collective-permute-start.2) | collective-permute-done | bytes 4128 | tf_op jit(solution)/shard_map/ppermute | solution.py:71
  32.9 3.2 %collective-permute-done.12.refs_7_ = bf16[1728,128]{1,0:T(8,128)(2,1)S(1)} collective-permute-done((bf16[1728,128]{1,0:T(8,128)(2,1)S(1)}, bf16[1728,128]{1,0:T(8,128)(2,1)S(1)}, u32[]{:S(2)}, u32[]{:S(2)}) %collective-permute-start.12) | collective-permute-done | bytes 442400 | tf_op jit(solution)/shard_map/ppermute | solution.py:71
  36.0 0.6 collective-permute-done.10.refs_5_
  36.6 0.9 pack.1
  37.5 2.6 %collective-permute-start.13 = (bf16[2304,128]{1,0:T(8,128)(2,1)S(1)}, bf16[2304,128]{1,0:T(8,128)(2,1)S(1)}, u32[]{:S(2)}, u32[]{:S(2)}) collective-permute-start(bf16[2304,128]{1,0:T(8,128)(2,1)S(1)} %get-tuple-element.52), channel_id=1, source_target_pairs={{0,48},{1,49},{2,194},{3,195},{4,52},{5,53},{6,198},{7,199},{8,56}... | collective-permute-start | bytes 1769480 | tf_op jit(solution)/shard_map/ppermute | solution.py:71
  40.1 0.5 collective-permute-start.14
  40.6 0.3 collective-permute-start.15
  40.9 13.3 %collective-permute-done.13.refs_1_ = bf16[2304,128]{1,0:T(8,128)(2,1)S(1)} collective-permute-done((bf16[2304,128]{1,0:T(8,128)(2,1)S(1)}, bf16[2304,128]{1,0:T(8,128)(2,1)S(1)}, u32[]{:S(2)}, u32[]{:S(2)}) %collective-permute-start.13) | collective-permute-done | bytes 589856 | tf_op jit(solution)/shard_map/ppermute | solution.py:71
  54.1 0.6 collective-permute-done.15.refs_3_
  54.8 0.7 merge.1
  55.5 4.9 %collective-permute-start.16 = (bf16[1152,128]{1,0:T(8,128)(2,1)S(1)}, bf16[1152,128]{1,0:T(8,128)(2,1)S(1)}, u32[]{:S(2)}, u32[]{:S(2)}) collective-permute-start(bf16[1152,128]{1,0:T(8,128)(2,1)S(1)} %get-tuple-element.56), channel_id=1, source_target_pairs={{0,2},{2,0},{1,3},{3,1},{4,6},{6,4},{5,7},{7,5},{8,10},{10,8},{9,1... | collective-permute-start | bytes 884744 | tf_op jit(solution)/shard_map/ppermute | solution.py:75
  60.5 1.1 reshape.81.qr_ref
  61.5 0.1 collective-permute-done.16.other
  61.7 13.1 %attention.1 = (bf16[4096,512]{1,0:T(8,128)(2,1)}, f32[128,512]{1,0:T(8,128)S(1)}, f32[128,64]{1,0:T(8,128)S(1)}, bf16[1152,128]{1,0:T(8,128)(2,1)S(1)}, bf16[1152,128]{1,0:T(8,128)(2,1)S(1)}) custom-call(s32[2]{0:T(128)S(1)} %pad_add_fusion.meta, bf16[128,512]{1,0:T(8,128)(2,1)S(1)} %copy-done.1, bf16[128,64]{1,0:T(8,128)(2,1)S(1)} %get-tuple-element.40.rot, ...), custom_call_target="tpu_custom_call" | custom-call | tf_op jit(solution)/shard_map/attention/pallas_call | solution.py:232
  74.8 0.4 collective-permute-start.17
  75.1 1.2 collective-permute-done.17.recv
  76.4 1.9 %collective-permute-start.20 = (bf16[2304,128]{1,0:T(8,128)(2,1)S(1)}, bf16[2304,128]{1,0:T(8,128)(2,1)S(1)}, u32[]{:S(2)}, u32[]{:S(2)}) collective-permute-start(bf16[2304,128]{1,0:T(8,128)(2,1)S(1)} %slots.1.refs_0_), channel_id=1, source_target_pairs={{0,48},{1,49},{2,194},{3,195},{4,52},{5,53},{6,198},{7,199},{8,56}... | collective-permute-start | bytes 1769480 | tf_op jit(solution)/shard_map/ppermute | solution.py:71
  78.3 0.5 collective-permute-start.19
  78.9 0.9 collective-permute-start.18
  79.8 13.2 %collective-permute-done.20.refs_3_ = bf16[2304,128]{1,0:T(8,128)(2,1)S(1)} collective-permute-done((bf16[2304,128]{1,0:T(8,128)(2,1)S(1)}, bf16[2304,128]{1,0:T(8,128)(2,1)S(1)}, u32[]{:S(2)}, u32[]{:S(2)}) %collective-permute-start.20) | collective-permute-done | bytes 589856 | tf_op jit(solution)/shard_map/ppermute | solution.py:71
  93.0 0.6 collective-permute-done.18.refs_1_
  93.7 1.6 %plane.1 = (f32[1728,128]{1,0:T(8,128)S(1)}, bf16[1728,128]{1,0:T(8,128)(2,1)S(1)}, bf16[1728,128]{1,0:T(8,128)(2,1)S(1)}, bf16[1728,128]{1,0:T(8,128)(2,1)S(1)}...) custom-call(s32[64]{0:T(128)S(1)} %broadcast_select_fusion.where_, ...), custom_call_target="tpu_custom_call" | custom-call | tf_op jit(solution)/shard_map/plane/pallas_call | solution.py:33
  95.3 2.7 %collective-permute-start.24 = (bf16[1728,128]{1,0:T(8,128)(2,1)S(1)}, bf16[1728,128]{1,0:T(8,128)(2,1)S(1)}, u32[]{:S(2)}, u32[]{:S(2)}) collective-permute-start(bf16[1728,128]{1,0:T(8,128)(2,1)S(1)} %get-tuple-element.65), channel_id=1, source_target_pairs={{0,192},{1,193},{2,50},{3,51},{4,196},{5,197},{6,54},{7,55},{8,200... | collective-permute-start | bytes 1327112 | tf_op jit(solution)/shard_map/ppermute | solution.py:71
  98.0 0.4 collective-permute-start.25
  98.4 0.3 collective-permute-start.26
  98.7 2.6 %collective-permute-start.21 = (bf16[576,128]{1,0:T(8,128)(2,1)S(1)}, bf16[576,128]{1,0:T(8,128)(2,1)S(1)}, u32[]{:S(2)}, u32[]{:S(2)}) collective-permute-start(bf16[576,128]{1,0:T(8,128)(2,1)S(1)} %get-tuple-element.61), channel_id=1, source_target_pairs={{0,192},{1,193},{2,50},{3,51},{4,196},{5,197},{6,54},{7,55},{8,200... | collective-permute-start | bytes 442376 | tf_op jit(solution)/shard_map/ppermute | solution.py:71
  101.3 0.4 collective-permute-start.22
  101.6 7.1 %collective-permute-done.24.refs_1_ = bf16[1728,128]{1,0:T(8,128)(2,1)S(1)} collective-permute-done((bf16[1728,128]{1,0:T(8,128)(2,1)S(1)}, bf16[1728,128]{1,0:T(8,128)(2,1)S(1)}, u32[]{:S(2)}, u32[]{:S(2)}) %collective-permute-start.24) | collective-permute-done | bytes 442400 | tf_op jit(solution)/shard_map/ppermute | solution.py:71
  108.8 0.7 collective-permute-done.26.refs_3_
  109.5 0.2 column.1
  109.7 0.7 collective-permute-start.27
  110.4 0.3 collective-permute-start.28
  110.7 0.5 collective-permute-done.21.refs_1_
  111.2 1.2 collective-permute-start.29
  112.3 1.0 collective-permute-done.22.refs_2_
  113.3 1.6 %collective-permute-done.27.refs_4_ = bf16[576,128]{1,0:T(8,128)(2,1)S(1)} collective-permute-done((bf16[576,128]{1,0:T(8,128)(2,1)S(1)}, bf16[576,128]{1,0:T(8,128)(2,1)S(1)}, u32[]{:S(2)}, u32[]{:S(2)}) %collective-permute-start.27) | collective-permute-done | bytes 147488 | tf_op jit(solution)/shard_map/ppermute | solution.py:71
  115.0 4.5 %collective-permute-done.28.refs_5_ = bf16[576,128]{1,0:T(8,128)(2,1)S(1)} collective-permute-done((bf16[576,128]{1,0:T(8,128)(2,1)S(1)}, bf16[576,128]{1,0:T(8,128)(2,1)S(1)}, u32[]{:S(2)}, u32[]{:S(2)}) %collective-permute-start.28) | collective-permute-done | bytes 147488 | tf_op jit(solution)/shard_map/ppermute | solution.py:71
  119.5 0.1 owner.1
  119.6 2.4 %collective-permute-start.30 = (f32[288,128]{1,0:T(8,128)S(1)}, f32[288,128]{1,0:T(8,128)S(1)}, u32[]{:S(2)}, u32[]{:S(2)}) collective-permute-start(f32[288,128]{1,0:T(8,128)S(1)} %get-tuple-element.72), channel_id=1, source_target_pairs={{0,2},{2,0},{1,3},{3,1},{4,6},{6,4},{5,7},{7,5},{8,10},{10,8},{9,1... | collective-permute-start | bytes 442376 | tf_op jit(solution)/shard_map/ppermute | solution.py:75
  122.1 1.0 collective-permute-done.30.recv
  123.1 0.6 half_sum.1.mine
  123.7 5.2 %collective-permute-start.31 = (bf16[576,128]{1,0:T(8,128)(2,1)S(1)}, bf16[576,128]{1,0:T(8,128)(2,1)S(1)}, u32[]{:S(2)}, u32[]{:S(2)}) collective-permute-start(bf16[576,128]{1,0:T(8,128)(2,1)S(1)} %half_sum.1.mine), channel_id=1, source_target_pairs={{0,1},{1,0},{2,3},{3,2},{4,5},{5,4},{6,7},{7,6},{8,9},{9,8},{10,11... | collective-permute-start | bytes 442376 | tf_op jit(solution)/shard_map/ppermute | solution.py:75
  128.9 6.8 %collective-permute-done.31.recv = bf16[576,128]{1,0:T(8,128)(2,1)S(1)} collective-permute-done((bf16[576,128]{1,0:T(8,128)(2,1)S(1)}, bf16[576,128]{1,0:T(8,128)(2,1)S(1)}, u32[]{:S(2)}, u32[]{:S(2)}) %collective-permute-start.31) | collective-permute-done | bytes 147488 | tf_op jit(solution)/shard_map/ppermute | solution.py:75
  135.8 0.8 final.1
  (44 shorter events, 1.0 us)
Async XLA Ops:
  1.8 0.9 copy-start
  2.7 0.7 copy-start.2
  3.4 57.1 %copy-start.3 = (bf16[128,2048]{1,0:T(8,128)(2,1)S(1)}, bf16[128,2048]{1,0:T(8,128)(2,1)}, u32[]{:S(2)}) copy-start(bf16[128,2048]{1,0:T(8,128)(2,1)} %param.9) | copy-start | bytes 1572868
  3.4 58.3 %copy-start.1 = (bf16[128,512]{1,0:T(8,128)(2,1)S(1)}, bf16[128,512]{1,0:T(8,128)(2,1)}, u32[]{:S(2)}) copy-start(bf16[128,512]{1,0:T(8,128)(2,1)} %lat.3) | copy-start | bytes 393220
  4.1 4.2 %collective-permute-start = (bf16[304,128]{1,0:T(8,128)(2,1)S(1)}, bf16[304,128]{1,0:T(8,128)(2,1)S(1)}, u32[]{:S(2)}, u32[]{:S(2)}) collective-permute-start(bf16[304,128]{1,0:T(8,128)(2,1)S(1)} %get-tuple-element.42), channel_id=1, source_target_pairs={{0,2},{2,0},{1,3},{3,1},{4,6},{6,4},{5,7},{7,5},{8,10},{10,8},{9,1... | collective-permute-start | bytes 233480 | tf_op jit(solution)/shard_map/ppermute | solution.py:75
  8.4 8.9 %collective-permute-start.9 = (bf16[576,128]{1,0:T(8,128)(2,1)S(1)}, bf16[576,128]{1,0:T(8,128)(2,1)S(1)}, u32[]{:S(2)}, u32[]{:S(2)}) collective-permute-start(bf16[576,128]{1,0:T(8,128)(2,1)S(1)} %get-tuple-element.44.refs_0_), channel_id=1, source_target_pairs={{0,13},{1,12},{2,15},{3,14},{4,8},{5,9},{6,10},{7,11},{8,4},{9,5},... | collective-permute-start | bytes 442376 | tf_op jit(solution)/shard_map/ppermute | solution.py:71
  12.3 9.1 %collective-permute-start.8 = (bf16[576,128]{1,0:T(8,128)(2,1)S(1)}, bf16[576,128]{1,0:T(8,128)(2,1)S(1)}, u32[]{:S(2)}, u32[]{:S(2)}) collective-permute-start(bf16[576,128]{1,0:T(8,128)(2,1)S(1)} %get-tuple-element.44.refs_0_), channel_id=1, source_target_pairs={{0,8},{1,9},{2,10},{3,11},{4,12},{5,13},{6,14},{7,15},{8,0},{9,1},... | collective-permute-start | bytes 442376 | tf_op jit(solution)/shard_map/ppermute | solution.py:71
  12.3 9.1 %collective-permute-start.7 = (bf16[576,128]{1,0:T(8,128)(2,1)S(1)}, bf16[576,128]{1,0:T(8,128)(2,1)S(1)}, u32[]{:S(2)}, u32[]{:S(2)}) collective-permute-start(bf16[576,128]{1,0:T(8,128)(2,1)S(1)} %get-tuple-element.44.refs_0_), channel_id=1, source_target_pairs={{0,4},{1,5},{2,6},{3,7},{4,0},{5,1},{6,2},{7,3},{8,12},{9,13},{10,... | collective-permute-start | bytes 442376 | tf_op jit(solution)/shard_map/ppermute | solution.py:71
  14.2 7.2 %collective-permute-start.6 = (bf16[576,128]{1,0:T(8,128)(2,1)S(1)}, bf16[576,128]{1,0:T(8,128)(2,1)S(1)}, u32[]{:S(2)}, u32[]{:S(2)}) collective-permute-start(bf16[576,128]{1,0:T(8,128)(2,1)S(1)} %get-tuple-element.44.refs_0_), channel_id=1, source_target_pairs={{0,192},{1,193},{2,50},{3,51},{4,196},{5,197},{6,54},{7,55},{8,200... | collective-permute-start | bytes 442376 | tf_op jit(solution)/shard_map/ppermute | solution.py:71
  17.0 5.5 %collective-permute-start.5 = (bf16[576,128]{1,0:T(8,128)(2,1)S(1)}, bf16[576,128]{1,0:T(8,128)(2,1)S(1)}, u32[]{:S(2)}, u32[]{:S(2)}) collective-permute-start(bf16[576,128]{1,0:T(8,128)(2,1)S(1)} %get-tuple-element.44.refs_0_), channel_id=1, source_target_pairs={{0,128},{1,129},{2,34},{3,35},{4,132},{5,133},{6,38},{7,39},{8,136... | collective-permute-start | bytes 442376 | tf_op jit(solution)/shard_map/ppermute | solution.py:71
  17.3 5.1 %collective-permute-start.4 = (bf16[576,128]{1,0:T(8,128)(2,1)S(1)}, bf16[576,128]{1,0:T(8,128)(2,1)S(1)}, u32[]{:S(2)}, u32[]{:S(2)}) collective-permute-start(bf16[576,128]{1,0:T(8,128)(2,1)S(1)} %get-tuple-element.44.refs_0_), channel_id=1, source_target_pairs={{0,64},{1,65},{2,18},{3,19},{4,68},{5,69},{6,22},{7,23},{8,72},{9,... | collective-permute-start | bytes 442376 | tf_op jit(solution)/shard_map/ppermute | solution.py:71
  22.5 13.5 %collective-permute-start.12 = (bf16[1728,128]{1,0:T(8,128)(2,1)S(1)}, bf16[1728,128]{1,0:T(8,128)(2,1)S(1)}, u32[]{:S(2)}, u32[]{:S(2)}) collective-permute-start(bf16[1728,128]{1,0:T(8,128)(2,1)S(1)} %line.1.refs_4_), channel_id=1, source_target_pairs={{0,192},{1,193},{2,50},{3,51},{4,196},{5,197},{6,54},{7,55},{8,200... | collective-permute-start | bytes 1327112 | tf_op jit(solution)/shard_map/ppermute | solution.py:71
  24.6 11.4 %collective-permute-start.11 = (bf16[1728,128]{1,0:T(8,128)(2,1)S(1)}, bf16[1728,128]{1,0:T(8,128)(2,1)S(1)}, u32[]{:S(2)}, u32[]{:S(2)}) collective-permute-start(bf16[1728,128]{1,0:T(8,128)(2,1)S(1)} %line.1.refs_4_), channel_id=1, source_target_pairs={{0,128},{1,129},{2,34},{3,35},{4,132},{5,133},{6,38},{7,39},{8,136... | collective-permute-start | bytes 1327112 | tf_op jit(solution)/shard_map/ppermute | solution.py:71
  25.0 11.7 %collective-permute-start.10 = (bf16[1728,128]{1,0:T(8,128)(2,1)S(1)}, bf16[1728,128]{1,0:T(8,128)(2,1)S(1)}, u32[]{:S(2)}, u32[]{:S(2)}) collective-permute-start(bf16[1728,128]{1,0:T(8,128)(2,1)S(1)} %line.1.refs_4_), channel_id=1, source_target_pairs={{0,64},{1,65},{2,18},{3,19},{4,68},{5,69},{6,22},{7,23},{8,72},{9,... | collective-permute-start | bytes 1327112 | tf_op jit(solution)/shard_map/ppermute | solution.py:71
  25.8 4.0 %collective-permute-start.3 = (bf16[16,128]{1,0:T(8,128)(2,1)S(1)}, bf16[16,128]{1,0:T(8,128)(2,1)S(1)}, u32[]{:S(2)}, u32[]{:S(2)}) collective-permute-start(bf16[16,128]{1,0:T(8,128)(2,1)S(1)} %get-tuple-element.43), channel_id=1, source_target_pairs={{0,48},{1,49},{2,194},{3,195},{4,52},{5,53},{6,198},{7,199},{8,56}... | collective-permute-start | bytes 12296 | tf_op jit(solution)/shard_map/ppermute | solution.py:71
  28.3 4.3 %collective-permute-start.2 = (bf16[16,128]{1,0:T(8,128)(2,1)S(1)}, bf16[16,128]{1,0:T(8,128)(2,1)S(1)}, u32[]{:S(2)}, u32[]{:S(2)}) collective-permute-start(bf16[16,128]{1,0:T(8,128)(2,1)S(1)} %get-tuple-element.43), channel_id=1, source_target_pairs={{0,32},{1,33},{2,130},{3,131},{4,36},{5,37},{6,134},{7,135},{8,40}... | collective-permute-start | bytes 12296 | tf_op jit(solution)/shard_map/ppermute | solution.py:71
  29.8 2.9 %collective-permute-start.1 = (bf16[16,128]{1,0:T(8,128)(2,1)S(1)}, bf16[16,128]{1,0:T(8,128)(2,1)S(1)}, u32[]{:S(2)}, u32[]{:S(2)}) collective-permute-start(bf16[16,128]{1,0:T(8,128)(2,1)S(1)} %get-tuple-element.43), channel_id=1, source_target_pairs={{0,16},{1,17},{2,66},{3,67},{4,20},{5,21},{6,70},{7,71},{8,24},{9,... | collective-permute-start | bytes 12296 | tf_op jit(solution)/shard_map/ppermute | solution.py:71
  37.5 16.6 %collective-permute-start.13 = (bf16[2304,128]{1,0:T(8,128)(2,1)S(1)}, bf16[2304,128]{1,0:T(8,128)(2,1)S(1)}, u32[]{:S(2)}, u32[]{:S(2)}) collective-permute-start(bf16[2304,128]{1,0:T(8,128)(2,1)S(1)} %get-tuple-element.52), channel_id=1, source_target_pairs={{0,48},{1,49},{2,194},{3,195},{4,52},{5,53},{6,198},{7,199},{8,56}... | collective-permute-start | bytes 1769480 | tf_op jit(solution)/shard_map/ppermute | solution.py:71
  40.1 14.1 %collective-permute-start.14 = (bf16[2304,128]{1,0:T(8,128)(2,1)S(1)}, bf16[2304,128]{1,0:T(8,128)(2,1)S(1)}, u32[]{:S(2)}, u32[]{:S(2)}) collective-permute-start(bf16[2304,128]{1,0:T(8,128)(2,1)S(1)} %get-tuple-element.53), channel_id=1, source_target_pairs={{0,32},{1,33},{2,130},{3,131},{4,36},{5,37},{6,134},{7,135},{8,40}... | collective-permute-start | bytes 1769480 | tf_op jit(solution)/shard_map/ppermute | solution.py:71
  40.6 14.2 %collective-permute-start.15 = (bf16[2304,128]{1,0:T(8,128)(2,1)S(1)}, bf16[2304,128]{1,0:T(8,128)(2,1)S(1)}, u32[]{:S(2)}, u32[]{:S(2)}) collective-permute-start(bf16[2304,128]{1,0:T(8,128)(2,1)S(1)} %get-tuple-element.54), channel_id=1, source_target_pairs={{0,16},{1,17},{2,66},{3,67},{4,20},{5,21},{6,70},{7,71},{8,24},{9,... | collective-permute-start | bytes 1769480 | tf_op jit(solution)/shard_map/ppermute | solution.py:71
  55.5 6.2 %collective-permute-start.16 = (bf16[1152,128]{1,0:T(8,128)(2,1)S(1)}, bf16[1152,128]{1,0:T(8,128)(2,1)S(1)}, u32[]{:S(2)}, u32[]{:S(2)}) collective-permute-start(bf16[1152,128]{1,0:T(8,128)(2,1)S(1)} %get-tuple-element.56), channel_id=1, source_target_pairs={{0,2},{2,0},{1,3},{3,1},{4,6},{6,4},{5,7},{7,5},{8,10},{10,8},{9,1... | collective-permute-start | bytes 884744 | tf_op jit(solution)/shard_map/ppermute | solution.py:75
  74.8 1.6 %collective-permute-start.17 = (bf16[1152,128]{1,0:T(8,128)(2,1)S(1)}, bf16[1152,128]{1,0:T(8,128)(2,1)S(1)}, u32[]{:S(2)}, u32[]{:S(2)}) collective-permute-start(bf16[1152,128]{1,0:T(8,128)(2,1)S(1)} %get-tuple-element.59), channel_id=1, source_target_pairs={{0,2},{2,0},{1,3},{3,1},{4,6},{6,4},{5,7},{7,5},{8,10},{10,8},{9,1... | collective-permute-start | bytes 884744 | tf_op jit(solution)/shard_map/ppermute | solution.py:75
  76.4 16.6 %collective-permute-start.20 = (bf16[2304,128]{1,0:T(8,128)(2,1)S(1)}, bf16[2304,128]{1,0:T(8,128)(2,1)S(1)}, u32[]{:S(2)}, u32[]{:S(2)}) collective-permute-start(bf16[2304,128]{1,0:T(8,128)(2,1)S(1)} %slots.1.refs_0_), channel_id=1, source_target_pairs={{0,48},{1,49},{2,194},{3,195},{4,52},{5,53},{6,198},{7,199},{8,56}... | collective-permute-start | bytes 1769480 | tf_op jit(solution)/shard_map/ppermute | solution.py:71
  78.3 14.7 %collective-permute-start.19 = (bf16[2304,128]{1,0:T(8,128)(2,1)S(1)}, bf16[2304,128]{1,0:T(8,128)(2,1)S(1)}, u32[]{:S(2)}, u32[]{:S(2)}) collective-permute-start(bf16[2304,128]{1,0:T(8,128)(2,1)S(1)} %slots.1.refs_0_), channel_id=1, source_target_pairs={{0,32},{1,33},{2,130},{3,131},{4,36},{5,37},{6,134},{7,135},{8,40}... | collective-permute-start | bytes 1769480 | tf_op jit(solution)/shard_map/ppermute | solution.py:71
  78.9 14.8 %collective-permute-start.18 = (bf16[2304,128]{1,0:T(8,128)(2,1)S(1)}, bf16[2304,128]{1,0:T(8,128)(2,1)S(1)}, u32[]{:S(2)}, u32[]{:S(2)}) collective-permute-start(bf16[2304,128]{1,0:T(8,128)(2,1)S(1)} %slots.1.refs_0_), channel_id=1, source_target_pairs={{0,16},{1,17},{2,66},{3,67},{4,20},{5,21},{6,70},{7,71},{8,24},{9,... | collective-permute-start | bytes 1769480 | tf_op jit(solution)/shard_map/ppermute | solution.py:71
  95.3 13.5 %collective-permute-start.24 = (bf16[1728,128]{1,0:T(8,128)(2,1)S(1)}, bf16[1728,128]{1,0:T(8,128)(2,1)S(1)}, u32[]{:S(2)}, u32[]{:S(2)}) collective-permute-start(bf16[1728,128]{1,0:T(8,128)(2,1)S(1)} %get-tuple-element.65), channel_id=1, source_target_pairs={{0,192},{1,193},{2,50},{3,51},{4,196},{5,197},{6,54},{7,55},{8,200... | collective-permute-start | bytes 1327112 | tf_op jit(solution)/shard_map/ppermute | solution.py:71
  98.0 10.8 %collective-permute-start.25 = (bf16[1728,128]{1,0:T(8,128)(2,1)S(1)}, bf16[1728,128]{1,0:T(8,128)(2,1)S(1)}, u32[]{:S(2)}, u32[]{:S(2)}) collective-permute-start(bf16[1728,128]{1,0:T(8,128)(2,1)S(1)} %get-tuple-element.66), channel_id=1, source_target_pairs={{0,128},{1,129},{2,34},{3,35},{4,132},{5,133},{6,38},{7,39},{8,136... | collective-permute-start | bytes 1327112 | tf_op jit(solution)/shard_map/ppermute | solution.py:71
  98.4 11.1 %collective-permute-start.26 = (bf16[1728,128]{1,0:T(8,128)(2,1)S(1)}, bf16[1728,128]{1,0:T(8,128)(2,1)S(1)}, u32[]{:S(2)}, u32[]{:S(2)}) collective-permute-start(bf16[1728,128]{1,0:T(8,128)(2,1)S(1)} %get-tuple-element.67), channel_id=1, source_target_pairs={{0,64},{1,65},{2,18},{3,19},{4,68},{5,69},{6,22},{7,23},{8,72},{9,... | collective-permute-start | bytes 1327112 | tf_op jit(solution)/shard_map/ppermute | solution.py:71
  98.7 12.5 %collective-permute-start.21 = (bf16[576,128]{1,0:T(8,128)(2,1)S(1)}, bf16[576,128]{1,0:T(8,128)(2,1)S(1)}, u32[]{:S(2)}, u32[]{:S(2)}) collective-permute-start(bf16[576,128]{1,0:T(8,128)(2,1)S(1)} %get-tuple-element.61), channel_id=1, source_target_pairs={{0,192},{1,193},{2,50},{3,51},{4,196},{5,197},{6,54},{7,55},{8,200... | collective-permute-start | bytes 442376 | tf_op jit(solution)/shard_map/ppermute | solution.py:71
  101.3 12.1 %collective-permute-start.22 = (bf16[576,128]{1,0:T(8,128)(2,1)S(1)}, bf16[576,128]{1,0:T(8,128)(2,1)S(1)}, u32[]{:S(2)}, u32[]{:S(2)}) collective-permute-start(bf16[576,128]{1,0:T(8,128)(2,1)S(1)} %get-tuple-element.62), channel_id=1, source_target_pairs={{0,128},{1,129},{2,34},{3,35},{4,132},{5,133},{6,38},{7,39},{8,136... | collective-permute-start | bytes 442376 | tf_op jit(solution)/shard_map/ppermute | solution.py:71
  108.8 4.6 %collective-permute-start.23 = (bf16[576,128]{1,0:T(8,128)(2,1)S(1)}, bf16[576,128]{1,0:T(8,128)(2,1)S(1)}, u32[]{:S(2)}, u32[]{:S(2)}) collective-permute-start(bf16[576,128]{1,0:T(8,128)(2,1)S(1)} %get-tuple-element.63), channel_id=1, source_target_pairs={{0,64},{1,65},{2,18},{3,19},{4,68},{5,69},{6,22},{7,23},{8,72},{9,... | collective-permute-start | bytes 442376 | tf_op jit(solution)/shard_map/ppermute | solution.py:71
  109.7 5.3 %collective-permute-start.27 = (bf16[576,128]{1,0:T(8,128)(2,1)S(1)}, bf16[576,128]{1,0:T(8,128)(2,1)S(1)}, u32[]{:S(2)}, u32[]{:S(2)}) collective-permute-start(bf16[576,128]{1,0:T(8,128)(2,1)S(1)} %get-tuple-element.68), channel_id=1, source_target_pairs={{0,13},{1,12},{2,15},{3,14},{4,8},{5,9},{6,10},{7,11},{8,4},{9,5},... | collective-permute-start | bytes 442376 | tf_op jit(solution)/shard_map/ppermute | solution.py:71
  110.4 9.1 %collective-permute-start.28 = (bf16[576,128]{1,0:T(8,128)(2,1)S(1)}, bf16[576,128]{1,0:T(8,128)(2,1)S(1)}, u32[]{:S(2)}, u32[]{:S(2)}) collective-permute-start(bf16[576,128]{1,0:T(8,128)(2,1)S(1)} %get-tuple-element.69), channel_id=1, source_target_pairs={{0,8},{1,9},{2,10},{3,11},{4,12},{5,13},{6,14},{7,15},{8,0},{9,1},... | collective-permute-start | bytes 442376 | tf_op jit(solution)/shard_map/ppermute | solution.py:71
  111.2 8.3 %collective-permute-start.29 = (bf16[576,128]{1,0:T(8,128)(2,1)S(1)}, bf16[576,128]{1,0:T(8,128)(2,1)S(1)}, u32[]{:S(2)}, u32[]{:S(2)}) collective-permute-start(bf16[576,128]{1,0:T(8,128)(2,1)S(1)} %get-tuple-element.70), channel_id=1, source_target_pairs={{0,4},{1,5},{2,6},{3,7},{4,0},{5,1},{6,2},{7,3},{8,12},{9,13},{10,... | collective-permute-start | bytes 442376 | tf_op jit(solution)/shard_map/ppermute | solution.py:71
  119.6 3.5 %collective-permute-start.30 = (f32[288,128]{1,0:T(8,128)S(1)}, f32[288,128]{1,0:T(8,128)S(1)}, u32[]{:S(2)}, u32[]{:S(2)}) collective-permute-start(f32[288,128]{1,0:T(8,128)S(1)} %get-tuple-element.72), channel_id=1, source_target_pairs={{0,2},{2,0},{1,3},{3,1},{4,6},{6,4},{5,7},{7,5},{8,10},{10,8},{9,1... | collective-permute-start | bytes 442376 | tf_op jit(solution)/shard_map/ppermute | solution.py:75
  123.7 12.0 %collective-permute-start.31 = (bf16[576,128]{1,0:T(8,128)(2,1)S(1)}, bf16[576,128]{1,0:T(8,128)(2,1)S(1)}, u32[]{:S(2)}, u32[]{:S(2)}) collective-permute-start(bf16[576,128]{1,0:T(8,128)(2,1)S(1)} %half_sum.1.mine), channel_id=1, source_target_pairs={{0,1},{1,0},{2,3},{3,2},{4,5},{5,4},{6,7},{7,6},{8,9},{9,8},{10,11... | collective-permute-start | bytes 442376 | tf_op jit(solution)/shard_map/ppermute | solution.py:75

commit v4 on v3

--- a/solution.py
+++ b/solution.py
@@ -135,7 +135,7 @@
 
 def attention_kernel(
     meta, lat, rot, mine, other, q_ref, qr_ref, do_ref,
-    out_ref, dkl_ref, dkr_ref, gm_ref, go_ref,
+    probs_ref, ds_ref, keys_out, gm_ref, go_ref,
     units, keys, keys_r, acc, acc_r,
 ):
     i, t = pl.program_id(0), pl.program_id(1)
@@ -161,14 +161,15 @@
             packed = units[1, s * HALF + 112 : s * HALF + 144, :]
             keys_r[base : base + 32] = packed[:, :64]
             keys_r[base + 32 : base + 64] = packed[:, 64:]
+        keys_out[...] = keys[...]
         acc[...] = jnp.zeros_like(acc)
         acc_r[...] = jnp.zeros_like(acc_r)
 
     nt = (((1,), (1,)), ((), ()))
     limit = jnp.minimum(block + 1, SEL) * BLK
     part = TILE // 4
-    grad = jnp.zeros((SEL * BLK, LAT), f32)
-    grad_r = jnp.zeros((SEL * BLK, ROPE), f32)
+    grad = jnp.zeros(((SEL - 1) * BLK, LAT), f32)
+    grad_r = jnp.zeros(((SEL - 1) * BLK, ROPE), f32)
     raws, dps = [], []
     for j in range(4):
         rows = slice(j * part, (j + 1) * part)
@@ -193,21 +194,18 @@
         probs_low = probs.astype(bf16)
         row_delta = jnp.sum(probs * dprobs, axis=0, keepdims=True)
         dscores = (probs * ((dprobs - row_delta) * softmax_scale)).astype(bf16)
-        out_ref[rows, :] = lax.dot_general(
-            probs_low, keys[...], (((0,), (0,)), ((), ())), preferred_element_type=f32
-        ).astype(bf16)
-        grad = grad + jnp.dot(dscores, q, preferred_element_type=f32) + jnp.dot(probs_low, do, preferred_element_type=f32)
-        grad_r = grad_r + jnp.dot(dscores, qr, preferred_element_type=f32)
+        probs_ref[:, rows] = probs_low
+        ds_ref[:, rows] = dscores[:BLK]
+        grad = grad + jnp.dot(dscores[BLK:], q, preferred_element_type=f32)
+        grad = grad + jnp.dot(probs_low[BLK:], do, preferred_element_type=f32)
+        grad_r = grad_r + jnp.dot(dscores[BLK:], qr, preferred_element_type=f32)
     acc[...] += grad
     acc_r[...] += grad_r
 
     @pl.when(t == pl.num_programs(1) - 1)
     def _():
-        rows = pl.ds(pl.multiple_of(i * BLK, BLK), BLK)
-        dkl_ref[rows, :] = acc[0:BLK]
-        dkr_ref[rows, :] = acc_r[0:BLK]
         for s in range(4):
-            base = (s + 1) * BLK
+            base = s * BLK
             packed = jnp.concatenate(
                 [acc_r[base : base + 32, :], acc_r[base + 32 : base + 64, :]], axis=1
             )
@@ -233,9 +231,9 @@
         attention_kernel,
         grid=(2, tiles),
         out_shape=[
-            jax.ShapeDtypeStruct(q.shape, bf16),
-            jax.ShapeDtypeStruct((128, LAT), f32),
-            jax.ShapeDtypeStruct((128, ROPE), f32),
+            pltpu.HBM((2 * SEL * BLK, BLK * HEADS), bf16),
+            pltpu.HBM((2 * BLK, BLK * HEADS), bf16),
+            jax.ShapeDtypeStruct((2 * SEL * BLK, LAT), bf16),
             jax.ShapeDtypeStruct((8 * HALF, 128), bf16),
             jax.ShapeDtypeStruct((8 * HALF, 128), bf16),
         ],
@@ -250,9 +248,9 @@
             rows(LAT),
         ],
         out_specs=[
-            rows(LAT),
-            whole((128, LAT)),
-            whole((128, ROPE)),
+            pl.BlockSpec((SEL * BLK, TILE), lambda i, t: (i, t)),
+            pl.BlockSpec((BLK, TILE), lambda i, t: (i, t)),
+            pl.BlockSpec((SEL * BLK, LAT), lambda i, t: (i, 0)),
             whole((8 * HALF, 128)),
             whole((8 * HALF, 128)),
         ],
@@ -260,12 +258,58 @@
             pltpu.VMEM((2, 576, 128), bf16),
             pltpu.VMEM((SEL * BLK, LAT), bf16),
             pltpu.VMEM((SEL * BLK, ROPE), bf16),
-            pltpu.VMEM((SEL * BLK, LAT), f32),
-            pltpu.VMEM((SEL * BLK, ROPE), f32),
+            pltpu.VMEM(((SEL - 1) * BLK, LAT), f32),
+            pltpu.VMEM(((SEL - 1) * BLK, ROPE), f32),
         ],
         compiler_params=PARAMS,
         name="attention",
     )(meta, lat, rot, mine, other, q, qr, do)
+
+
+def output_kernel(probs_ref, ds_ref, keys, q_ref, qr_ref, do_ref, out_ref, dkl_ref, dkr_ref):
+    @pl.when(pl.program_id(1) == 0)
+    def _():
+        dkl_ref[...] = jnp.zeros_like(dkl_ref)
+        dkr_ref[...] = jnp.zeros_like(dkr_ref)
+
+    probs = probs_ref[...]
+    out_ref[...] = lax.dot_general(
+        probs, keys[...], (((0,), (0,)), ((), ())), preferred_element_type=f32
+    ).astype(bf16)
+    dscores = ds_ref[...]
+    dkl_ref[...] += jnp.dot(dscores, q_ref[...], preferred_element_type=f32) + jnp.dot(
+        probs[:BLK], do_ref[...], preferred_element_type=f32
+    )
+    dkr_ref[...] += jnp.dot(dscores, qr_ref[...], preferred_element_type=f32)
+
+
+def output(probs, ds, keys, q, qr, do):
+    tiles = BLK * HEADS // TILE
+    rows = lambda width: pl.BlockSpec((TILE, width), lambda i, t: (i * tiles + t, 0))
+    return pl.pallas_call(
+        output_kernel,
+        grid=(2, tiles),
+        out_shape=[
+            jax.ShapeDtypeStruct(q.shape, bf16),
+            jax.ShapeDtypeStruct((2 * BLK, LAT), f32),
+            jax.ShapeDtypeStruct((2 * BLK, ROPE), f32),
+        ],
+        in_specs=[
+            pl.BlockSpec((SEL * BLK, TILE), lambda i, t: (i, t)),
+            pl.BlockSpec((BLK, TILE), lambda i, t: (i, t)),
+            pl.BlockSpec((SEL * BLK, LAT), lambda i, t: (i, 0)),
+            rows(LAT),
+            rows(ROPE),
+            rows(LAT),
+        ],
+        out_specs=[
+            rows(LAT),
+            pl.BlockSpec((BLK, LAT), lambda i, t: (i, 0)),
+            pl.BlockSpec((BLK, ROPE), lambda i, t: (i, 0)),
+        ],
+        compiler_params=PARAMS,
+        name="output",
+    )(probs, ds, keys, q, qr, do)
 
 
 def slots_kernel(mine, recv, g):
@@ -412,9 +456,12 @@
     q = queries.reshape(128 * HEADS, LAT)
     do = grad_out.reshape(128 * HEADS, LAT)
     qr = query_rope.reshape(128 * HEADS, ROPE)
-    out, dkl, dkr, g_mine, g_other = attention(meta, latent, rot, key_mine, key_recv, q, qr, do)
+    probs, ds, keys, g_mine, g_other = attention(meta, latent, rot, key_mine, key_recv, q, qr, do)
 
     (slots,) = call(slots_kernel, (g_mine, swap(g_other, "c")), [((2304, 128), bf16)], name="slots")
+    keys, slots = lax.optimization_barrier((keys, slots))
+    out, dkl, dkr = output(probs, ds, keys, q, qr, do)
+    add_at, dkl, dkr = lax.optimization_barrier((add_at, dkl, dkr))
     sums = call(
         plane_kernel,
         [add_at] + all_of(slots, "w"),

time: 137 us -> 136 us (level)
  waiting for transfers between devices: 65.5 us -> 55.4 us
  Pallas kernels: 18.9 us -> 24.7 us
  local copies, waits for them, and re-layouts: 3.4 us -> 7.16 us
    ppermute x27, waiting for transfers between devices: 55.4 us -> 45.1 us  [exchange(): lax.ppermute(a, MESH, [(number(p), number(partner(p, phase, k))) for p in...]
    pallas_call x1 -> x2, Pallas kernels: 13.1 us -> 18.4 us  [the longest x1 10.7 us: attention(): pl.pallas_call(attention_kernel, grid=(2, tiles), out_shape=[pltpu.HBM((2...]
    unnamed x8 -> x10, local copies, waits for them, and re-layouts: 1.62 us -> 4.4 us
  transfers between devices with their start and end apart: 32 -> 32, of which waited for: 21 -> 20; matrix products, arithmetic and copies ran while one was open for 1% -> 2% of each run, Pallas kernels for 0% -> 6%
where the time goes in v4:
time: 136 us
  waiting for transfers between devices  55.4 us (41%)
  starting transfers between devices  46.7 us (34%)
  Pallas kernels  24.7 us (18%)
  local copies, waits for them, and re-layouts  7.16 us (5%)
    ppermute x27, waiting for transfers between devices, exchange(): lax.ppermute(a, MESH, [(number(p), number(partner(p, phase, k))) for p in...  45.1 us
    ppermute x27, starting transfers between devices, exchange(): lax.ppermute(a, MESH, [(number(p), number(partner(p, phase, k))) for p in...  30.7 us
    ppermute x5, starting transfers between devices, swap(): return lax.ppermute(a, axis, [(0, 1), (1, 0)])  15.9 us
    pallas_call x1, Pallas kernels, attention(): pl.pallas_call(attention_kernel, grid=(2, tiles), out_shape=[pltpu.HBM((2...  10.7 us
    ppermute x5, waiting for transfers between devices, swap(): return lax.ppermute(a, axis, [(0, 1), (1, 0)])  10.3 us
    pallas_call x1, Pallas kernels, output(): pl.pallas_call(output_kernel, grid=(2, tiles), out_shape=[jax.ShapeDtypeS...  7.66 us
    pallas_call x11, Pallas kernels, call(): pl.pallas_call(kernel, out_shape=[jax.ShapeDtypeStruct(s, d) for s, d in...  6.32 us
    unnamed x10, local copies, waits for them, and re-layouts  4.4 us
  transfers between devices with their start and end apart: 32, of which 20 were waited for; matrix products, arithmetic and copies ran while one was open for 2% of the time, Pallas kernels for 6%

profile of v4, /device:TPU:1, one launch (start us, length us, event | category | flops | bytes accessed | tf_op | source)
XLA Modules:
  0.0 135.7 jit_solution(10609921897620562245)
XLA Ops:
  0.7 0.7 convert.3
  1.6 0.1 multiply_sine_fusion
  1.8 0.9 copy-done.1
  2.7 0.7 copy-done.4
  3.4 0.7 prep.1
  4.1 3.3 %collective-permute-start = (bf16[304,128]{1,0:T(8,128)(2,1)S(1)}, bf16[304,128]{1,0:T(8,128)(2,1)S(1)}, u32[]{:S(2)}, u32[]{:S(2)}) collective-permute-start(bf16[304,128]{1,0:T(8,128)(2,1)S(1)} %get-tuple-element.50), channel_id=1, source_target_pairs={{0,2},{2,0},{1,3},{3,1},{4,6},{6,4},{5,7},{7,5},{8,10},{10,8},{9,1... | collective-permute-start | bytes 233480 | tf_op jit(solution)/shard_map/ppermute | solution.py:75
  7.5 0.9 collective-permute-done.recv
  8.4 3.9 %collective-permute-start.9 = (bf16[576,128]{1,0:T(8,128)(2,1)S(1)}, bf16[576,128]{1,0:T(8,128)(2,1)S(1)}, u32[]{:S(2)}, u32[]{:S(2)}) collective-permute-start(bf16[576,128]{1,0:T(8,128)(2,1)S(1)} %get-tuple-element.52.refs_0_), channel_id=1, source_target_pairs={{0,13},{1,12},{2,15},{3,14},{4,8},{5,9},{6,10},{7,11},{8,4},{9,5},... | collective-permute-start | bytes 442376 | tf_op jit(solution)/shard_map/ppermute | solution.py:71
  12.3 1.9 %collective-permute-start.7 = (bf16[576,128]{1,0:T(8,128)(2,1)S(1)}, bf16[576,128]{1,0:T(8,128)(2,1)S(1)}, u32[]{:S(2)}, u32[]{:S(2)}) collective-permute-start(bf16[576,128]{1,0:T(8,128)(2,1)S(1)} %get-tuple-element.52.refs_0_), channel_id=1, source_target_pairs={{0,4},{1,5},{2,6},{3,7},{4,0},{5,1},{6,2},{7,3},{8,12},{9,13},{10,... | collective-permute-start | bytes 442376 | tf_op jit(solution)/shard_map/ppermute | solution.py:71
  14.2 2.7 %collective-permute-start.6 = (bf16[576,128]{1,0:T(8,128)(2,1)S(1)}, bf16[576,128]{1,0:T(8,128)(2,1)S(1)}, u32[]{:S(2)}, u32[]{:S(2)}) collective-permute-start(bf16[576,128]{1,0:T(8,128)(2,1)S(1)} %get-tuple-element.52.refs_0_), channel_id=1, source_target_pairs={{0,192},{1,193},{2,50},{3,51},{4,196},{5,197},{6,54},{7,55},{8,200... | collective-permute-start | bytes 442376 | tf_op jit(solution)/shard_map/ppermute | solution.py:71
  16.9 0.3 collective-permute-start.5
  17.3 0.2 collective-permute-start.4
  17.5 3.9 %collective-permute-done.8.refs_1_ = bf16[576,128]{1,0:T(8,128)(2,1)S(1)} collective-permute-done((bf16[576,128]{1,0:T(8,128)(2,1)S(1)}, bf16[576,128]{1,0:T(8,128)(2,1)S(1)}, u32[]{:S(2)}, u32[]{:S(2)}) %collective-permute-start.8) | collective-permute-done | bytes 147488 | tf_op jit(solution)/shard_map/ppermute | solution.py:71
  21.5 1.0 collective-permute-done.5.refs_2_
  22.5 2.1 %collective-permute-start.12 = (bf16[1728,128]{1,0:T(8,128)(2,1)S(1)}, bf16[1728,128]{1,0:T(8,128)(2,1)S(1)}, u32[]{:S(2)}, u32[]{:S(2)}) collective-permute-start(bf16[1728,128]{1,0:T(8,128)(2,1)S(1)} %line.1.refs_4_), channel_id=1, source_target_pairs={{0,192},{1,193},{2,50},{3,51},{4,196},{5,197},{6,54},{7,55},{8,200... | collective-permute-start | bytes 1327112 | tf_op jit(solution)/shard_map/ppermute | solution.py:71
  24.6 0.3 collective-permute-start.11
  25.0 0.8 collective-permute-start.10
  25.8 2.5 %collective-permute-start.3 = (bf16[16,128]{1,0:T(8,128)(2,1)S(1)}, bf16[16,128]{1,0:T(8,128)(2,1)S(1)}, u32[]{:S(2)}, u32[]{:S(2)}) collective-permute-start(bf16[16,128]{1,0:T(8,128)(2,1)S(1)} %get-tuple-element.51), channel_id=1, source_target_pairs={{0,48},{1,49},{2,194},{3,195},{4,52},{5,53},{6,198},{7,199},{8,56}... | collective-permute-start | bytes 12296 | tf_op jit(solution)/shard_map/ppermute | solution.py:71
  28.3 0.5 collective-permute-start.2
  28.8 1.0 collective-permute-done.3
  30.0 2.6 %collective-permute-done.2 = bf16[16,128]{1,0:T(8,128)(2,1)S(1)} collective-permute-done((bf16[16,128]{1,0:T(8,128)(2,1)S(1)}, bf16[16,128]{1,0:T(8,128)(2,1)S(1)}, u32[]{:S(2)}, u32[]{:S(2)}) %collective-permute-start.2) | collective-permute-done | bytes 4128 | tf_op jit(solution)/shard_map/ppermute | solution.py:71
  32.9 3.2 %collective-permute-done.12.refs_7_ = bf16[1728,128]{1,0:T(8,128)(2,1)S(1)} collective-permute-done((bf16[1728,128]{1,0:T(8,128)(2,1)S(1)}, bf16[1728,128]{1,0:T(8,128)(2,1)S(1)}, u32[]{:S(2)}, u32[]{:S(2)}) %collective-permute-start.12) | collective-permute-done | bytes 442400 | tf_op jit(solution)/shard_map/ppermute | solution.py:71
  36.0 0.6 collective-permute-done.10.refs_5_
  36.6 0.9 pack.1
  37.5 2.6 %collective-permute-start.13 = (bf16[2304,128]{1,0:T(8,128)(2,1)S(1)}, bf16[2304,128]{1,0:T(8,128)(2,1)S(1)}, u32[]{:S(2)}, u32[]{:S(2)}) collective-permute-start(bf16[2304,128]{1,0:T(8,128)(2,1)S(1)} %get-tuple-element.60), channel_id=1, source_target_pairs={{0,48},{1,49},{2,194},{3,195},{4,52},{5,53},{6,198},{7,199},{8,56}... | collective-permute-start | bytes 1769480 | tf_op jit(solution)/shard_map/ppermute | solution.py:71
  40.1 0.5 collective-permute-start.14
  40.6 0.3 collective-permute-start.15
  40.9 13.3 %collective-permute-done.13.refs_1_ = bf16[2304,128]{1,0:T(8,128)(2,1)S(1)} collective-permute-done((bf16[2304,128]{1,0:T(8,128)(2,1)S(1)}, bf16[2304,128]{1,0:T(8,128)(2,1)S(1)}, u32[]{:S(2)}, u32[]{:S(2)}) %collective-permute-start.13) | collective-permute-done | bytes 589856 | tf_op jit(solution)/shard_map/ppermute | solution.py:71
  54.1 0.6 collective-permute-done.15.refs_3_
  54.8 0.7 merge.1
  55.5 5.0 %collective-permute-start.16 = (bf16[1152,128]{1,0:T(8,128)(2,1)S(1)}, bf16[1152,128]{1,0:T(8,128)(2,1)S(1)}, u32[]{:S(2)}, u32[]{:S(2)}) collective-permute-start(bf16[1152,128]{1,0:T(8,128)(2,1)S(1)} %get-tuple-element.64), channel_id=1, source_target_pairs={{0,2},{2,0},{1,3},{3,1},{4,6},{6,4},{5,7},{7,5},{8,10},{10,8},{9,1... | collective-permute-start | bytes 884744 | tf_op jit(solution)/shard_map/ppermute | solution.py:75
  60.5 2.1 %reshape.81.qr_ref = bf16[4096,64]{1,0:T(8,128)(2,1)S(1)} reshape(bf16[128,2048]{1,0:T(8,128)(2,1)} %param.9) | data formatting | bytes 1048576 | tf_op jit(solution)/shard_map/reshape | solution.py:458
  62.5 10.7 %attention.1 = (bf16[640,2048]{1,0:T(8,128)(2,1)}, bf16[128,2048]{1,0:T(8,128)(2,1)}, bf16[640,512]{1,0:T(8,128)(2,1)S(1)}, bf16[1152,128]{1,0:T(8,128)(2,1)S(1)}, bf16[1152,128]{1,0:T(8,128)(2,1)S(1)}) custom-call(s32[2]{0:T(128)S(1)} %pad_add_fusion.meta, bf16[128,512]{1,0:T(8,128)(2,1)S(1)} %copy-done.2, bf16[128,64]{1,0:T(8,128)(2,1)S(1)} %get-tuple-element.48.rot, ...), custom_call_target="tpu_custom_call" | custom-call | tf_op jit(solution)/shard_map/attention/pallas_call | solution.py:230
  73.3 1.6 %collective-permute-done.17.recv = bf16[1152,128]{1,0:T(8,128)(2,1)S(1)} collective-permute-done((bf16[1152,128]{1,0:T(8,128)(2,1)S(1)}, bf16[1152,128]{1,0:T(8,128)(2,1)S(1)}, u32[]{:S(2)}, u32[]{:S(2)}) %collective-permute-start.17) | collective-permute-done | bytes 294944 | tf_op jit(solution)/shard_map/ppermute | solution.py:75
  74.9 2.0 %collective-permute-start.20 = (bf16[2304,128]{1,0:T(8,128)(2,1)S(1)}, bf16[2304,128]{1,0:T(8,128)(2,1)S(1)}, u32[]{:S(2)}, u32[]{:S(2)}) collective-permute-start(bf16[2304,128]{1,0:T(8,128)(2,1)S(1)} %slots.1.refs_0_), channel_id=1, source_target_pairs={{0,48},{1,49},{2,194},{3,195},{4,52},{5,53},{6,198},{7,199},{8,56}... | collective-permute-start | bytes 1769480 | tf_op jit(solution)/shard_map/ppermute | solution.py:71
  76.9 0.5 collective-permute-start.19
  77.4 0.9 collective-permute-start.18
  78.3 1.7 %copy-done = bf16[640,2048]{1,0:T(8,128)(2,1)S(1)} copy-done((bf16[640,2048]{1,0:T(8,128)(2,1)S(1)}, bf16[640,2048]{1,0:T(8,128)(2,1)}, u32[]{:S(2)}) %copy-start) | copy-done | bytes 2621464
  80.1 1.0 copy-done.3
  81.1 7.7 %output.1 = (bf16[4096,512]{1,0:T(8,128)(2,1)}, f32[128,512]{1,0:T(8,128)S(1)}, f32[128,64]{1,0:T(8,128)S(1)}) custom-call(bf16[640,2048]{1,0:T(8,128)(2,1)S(1)} %copy-done, bf16[128,2048]{1,0:T(8,128)(2,1)S(1)} %copy-done.3, bf16[640,512]{1,0:T(8,128)(2,1)S(1)} %get-tuple-element.70.keys, bf16[4096,512]{1,0:T(8,128)(2,1)} %bitcast.13, ...), custom_call_target="tpu_custom_call" | custom-call | tf_op jit(solution)/shard_map/output/pallas_call | solution.py:289
  88.8 2.8 %collective-permute-done.20.refs_3_ = bf16[2304,128]{1,0:T(8,128)(2,1)S(1)} collective-permute-done((bf16[2304,128]{1,0:T(8,128)(2,1)S(1)}, bf16[2304,128]{1,0:T(8,128)(2,1)S(1)}, u32[]{:S(2)}, u32[]{:S(2)}) %collective-permute-start.20) | collective-permute-done | bytes 589856 | tf_op jit(solution)/shard_map/ppermute | solution.py:71
  91.5 0.7 collective-permute-done.18.refs_1_
  92.3 2.2 %plane.1 = (f32[1728,128]{1,0:T(8,128)S(1)}, bf16[1728,128]{1,0:T(8,128)(2,1)S(1)}, bf16[1728,128]{1,0:T(8,128)(2,1)S(1)}, bf16[1728,128]{1,0:T(8,128)(2,1)S(1)}...) custom-call(s32[64]{0:T(128)S(1)} %broadcast_select_fusion.where_, ...), custom_call_target="tpu_custom_call" | custom-call | tf_op jit(solution)/shard_map/plane/pallas_call | solution.py:33
  94.4 2.7 %collective-permute-start.24 = (bf16[1728,128]{1,0:T(8,128)(2,1)S(1)}, bf16[1728,128]{1,0:T(8,128)(2,1)S(1)}, u32[]{:S(2)}, u32[]{:S(2)}) collective-permute-start(bf16[1728,128]{1,0:T(8,128)(2,1)S(1)} %get-tuple-element.81), channel_id=1, source_target_pairs={{0,192},{1,193},{2,50},{3,51},{4,196},{5,197},{6,54},{7,55},{8,200... | collective-permute-start | bytes 1327112 | tf_op jit(solution)/shard_map/ppermute | solution.py:71
  97.2 0.4 collective-permute-start.25
  97.5 0.3 collective-permute-start.26
  97.8 2.6 %collective-permute-start.21 = (bf16[576,128]{1,0:T(8,128)(2,1)S(1)}, bf16[576,128]{1,0:T(8,128)(2,1)S(1)}, u32[]{:S(2)}, u32[]{:S(2)}) collective-permute-start(bf16[576,128]{1,0:T(8,128)(2,1)S(1)} %get-tuple-element.77), channel_id=1, source_target_pairs={{0,192},{1,193},{2,50},{3,51},{4,196},{5,197},{6,54},{7,55},{8,200... | collective-permute-start | bytes 442376 | tf_op jit(solution)/shard_map/ppermute | solution.py:71
  100.4 0.4 collective-permute-start.22
  100.8 7.1 %collective-permute-done.24.refs_1_ = bf16[1728,128]{1,0:T(8,128)(2,1)S(1)} collective-permute-done((bf16[1728,128]{1,0:T(8,128)(2,1)S(1)}, bf16[1728,128]{1,0:T(8,128)(2,1)S(1)}, u32[]{:S(2)}, u32[]{:S(2)}) %collective-permute-start.24) | collective-permute-done | bytes 442400 | tf_op jit(solution)/shard_map/ppermute | solution.py:71
  107.9 0.7 collective-permute-done.26.refs_3_
  108.6 0.2 column.1
  108.8 0.7 collective-permute-start.27
  109.6 0.3 collective-permute-start.28
  109.8 0.5 collective-permute-done.21.refs_1_
  110.3 1.2 collective-permute-start.29
  111.5 1.0 collective-permute-done.22.refs_2_
  112.5 1.6 %collective-permute-done.27.refs_4_ = bf16[576,128]{1,0:T(8,128)(2,1)S(1)} collective-permute-done((bf16[576,128]{1,0:T(8,128)(2,1)S(1)}, bf16[576,128]{1,0:T(8,128)(2,1)S(1)}, u32[]{:S(2)}, u32[]{:S(2)}) %collective-permute-start.27) | collective-permute-done | bytes 147488 | tf_op jit(solution)/shard_map/ppermute | solution.py:71
  114.1 4.6 %collective-permute-done.28.refs_5_ = bf16[576,128]{1,0:T(8,128)(2,1)S(1)} collective-permute-done((bf16[576,128]{1,0:T(8,128)(2,1)S(1)}, bf16[576,128]{1,0:T(8,128)(2,1)S(1)}, u32[]{:S(2)}, u32[]{:S(2)}) %collective-permute-start.28) | collective-permute-done | bytes 147488 | tf_op jit(solution)/shard_map/ppermute | solution.py:71
  118.8 2.4 %collective-permute-start.30 = (f32[288,128]{1,0:T(8,128)S(1)}, f32[288,128]{1,0:T(8,128)S(1)}, u32[]{:S(2)}, u32[]{:S(2)}) collective-permute-start(f32[288,128]{1,0:T(8,128)S(1)} %get-tuple-element.88), channel_id=1, source_target_pairs={{0,2},{2,0},{1,3},{3,1},{4,6},{6,4},{5,7},{7,5},{8,10},{10,8},{9,1... | collective-permute-start | bytes 442376 | tf_op jit(solution)/shard_map/ppermute | solution.py:75
  121.2 1.0 collective-permute-done.30.recv
  122.3 0.6 half_sum.1.mine
  122.9 5.2 %collective-permute-start.31 = (bf16[576,128]{1,0:T(8,128)(2,1)S(1)}, bf16[576,128]{1,0:T(8,128)(2,1)S(1)}, u32[]{:S(2)}, u32[]{:S(2)}) collective-permute-start(bf16[576,128]{1,0:T(8,128)(2,1)S(1)} %half_sum.1.mine), channel_id=1, source_target_pairs={{0,1},{1,0},{2,3},{3,2},{4,5},{5,4},{6,7},{7,6},{8,9},{9,8},{10,11... | collective-permute-start | bytes 442376 | tf_op jit(solution)/shard_map/ppermute | solution.py:75
  128.1 6.9 %collective-permute-done.31.recv = bf16[576,128]{1,0:T(8,128)(2,1)S(1)} collective-permute-done((bf16[576,128]{1,0:T(8,128)(2,1)S(1)}, bf16[576,128]{1,0:T(8,128)(2,1)S(1)}, u32[]{:S(2)}, u32[]{:S(2)}) %collective-permute-start.31) | collective-permute-done | bytes 147488 | tf_op jit(solution)/shard_map/ppermute | solution.py:75
  134.9 0.8 final.1
  (47 shorter events, 1.2 us)
Async XLA Ops:
  1.8 0.9 copy-start.1
  2.7 0.7 copy-start.4
  3.4 59.1 %copy-start.2 = (bf16[128,512]{1,0:T(8,128)(2,1)S(1)}, bf16[128,512]{1,0:T(8,128)(2,1)}, u32[]{:S(2)}) copy-start(bf16[128,512]{1,0:T(8,128)(2,1)} %lat.3) | copy-start | bytes 393220
  4.1 4.2 %collective-permute-start = (bf16[304,128]{1,0:T(8,128)(2,1)S(1)}, bf16[304,128]{1,0:T(8,128)(2,1)S(1)}, u32[]{:S(2)}, u32[]{:S(2)}) collective-permute-start(bf16[304,128]{1,0:T(8,128)(2,1)S(1)} %get-tuple-element.50), channel_id=1, source_target_pairs={{0,2},{2,0},{1,3},{3,1},{4,6},{6,4},{5,7},{7,5},{8,10},{10,8},{9,1... | collective-permute-start | bytes 233480 | tf_op jit(solution)/shard_map/ppermute | solution.py:75
  8.4 8.9 %collective-permute-start.9 = (bf16[576,128]{1,0:T(8,128)(2,1)S(1)}, bf16[576,128]{1,0:T(8,128)(2,1)S(1)}, u32[]{:S(2)}, u32[]{:S(2)}) collective-permute-start(bf16[576,128]{1,0:T(8,128)(2,1)S(1)} %get-tuple-element.52.refs_0_), channel_id=1, source_target_pairs={{0,13},{1,12},{2,15},{3,14},{4,8},{5,9},{6,10},{7,11},{8,4},{9,5},... | collective-permute-start | bytes 442376 | tf_op jit(solution)/shard_map/ppermute | solution.py:71
  12.3 9.1 %collective-permute-start.8 = (bf16[576,128]{1,0:T(8,128)(2,1)S(1)}, bf16[576,128]{1,0:T(8,128)(2,1)S(1)}, u32[]{:S(2)}, u32[]{:S(2)}) collective-permute-start(bf16[576,128]{1,0:T(8,128)(2,1)S(1)} %get-tuple-element.52.refs_0_), channel_id=1, source_target_pairs={{0,8},{1,9},{2,10},{3,11},{4,12},{5,13},{6,14},{7,15},{8,0},{9,1},... | collective-permute-start | bytes 442376 | tf_op jit(solution)/shard_map/ppermute | solution.py:71
  12.3 9.1 %collective-permute-start.7 = (bf16[576,128]{1,0:T(8,128)(2,1)S(1)}, bf16[576,128]{1,0:T(8,128)(2,1)S(1)}, u32[]{:S(2)}, u32[]{:S(2)}) collective-permute-start(bf16[576,128]{1,0:T(8,128)(2,1)S(1)} %get-tuple-element.52.refs_0_), channel_id=1, source_target_pairs={{0,4},{1,5},{2,6},{3,7},{4,0},{5,1},{6,2},{7,3},{8,12},{9,13},{10,... | collective-permute-start | bytes 442376 | tf_op jit(solution)/shard_map/ppermute | solution.py:71
  14.2 7.2 %collective-permute-start.6 = (bf16[576,128]{1,0:T(8,128)(2,1)S(1)}, bf16[576,128]{1,0:T(8,128)(2,1)S(1)}, u32[]{:S(2)}, u32[]{:S(2)}) collective-permute-start(bf16[576,128]{1,0:T(8,128)(2,1)S(1)} %get-tuple-element.52.refs_0_), channel_id=1, source_target_pairs={{0,192},{1,193},{2,50},{3,51},{4,196},{5,197},{6,54},{7,55},{8,200... | collective-permute-start | bytes 442376 | tf_op jit(solution)/shard_map/ppermute | solution.py:71
  16.9 5.5 %collective-permute-start.5 = (bf16[576,128]{1,0:T(8,128)(2,1)S(1)}, bf16[576,128]{1,0:T(8,128)(2,1)S(1)}, u32[]{:S(2)}, u32[]{:S(2)}) collective-permute-start(bf16[576,128]{1,0:T(8,128)(2,1)S(1)} %get-tuple-element.52.refs_0_), channel_id=1, source_target_pairs={{0,128},{1,129},{2,34},{3,35},{4,132},{5,133},{6,38},{7,39},{8,136... | collective-permute-start | bytes 442376 | tf_op jit(solution)/shard_map/ppermute | solution.py:71
  17.3 5.1 %collective-permute-start.4 = (bf16[576,128]{1,0:T(8,128)(2,1)S(1)}, bf16[576,128]{1,0:T(8,128)(2,1)S(1)}, u32[]{:S(2)}, u32[]{:S(2)}) collective-permute-start(bf16[576,128]{1,0:T(8,128)(2,1)S(1)} %get-tuple-element.52.refs_0_), channel_id=1, source_target_pairs={{0,64},{1,65},{2,18},{3,19},{4,68},{5,69},{6,22},{7,23},{8,72},{9,... | collective-permute-start | bytes 442376 | tf_op jit(solution)/shard_map/ppermute | solution.py:71
  22.5 13.5 %collective-permute-start.12 = (bf16[1728,128]{1,0:T(8,128)(2,1)S(1)}, bf16[1728,128]{1,0:T(8,128)(2,1)S(1)}, u32[]{:S(2)}, u32[]{:S(2)}) collective-permute-start(bf16[1728,128]{1,0:T(8,128)(2,1)S(1)} %line.1.refs_4_), channel_id=1, source_target_pairs={{0,192},{1,193},{2,50},{3,51},{4,196},{5,197},{6,54},{7,55},{8,200... | collective-permute-start | bytes 1327112 | tf_op jit(solution)/shard_map/ppermute | solution.py:71
  24.6 11.4 %collective-permute-start.11 = (bf16[1728,128]{1,0:T(8,128)(2,1)S(1)}, bf16[1728,128]{1,0:T(8,128)(2,1)S(1)}, u32[]{:S(2)}, u32[]{:S(2)}) collective-permute-start(bf16[1728,128]{1,0:T(8,128)(2,1)S(1)} %line.1.refs_4_), channel_id=1, source_target_pairs={{0,128},{1,129},{2,34},{3,35},{4,132},{5,133},{6,38},{7,39},{8,136... | collective-permute-start | bytes 1327112 | tf_op jit(solution)/shard_map/ppermute | solution.py:71
  25.0 11.7 %collective-permute-start.10 = (bf16[1728,128]{1,0:T(8,128)(2,1)S(1)}, bf16[1728,128]{1,0:T(8,128)(2,1)S(1)}, u32[]{:S(2)}, u32[]{:S(2)}) collective-permute-start(bf16[1728,128]{1,0:T(8,128)(2,1)S(1)} %line.1.refs_4_), channel_id=1, source_target_pairs={{0,64},{1,65},{2,18},{3,19},{4,68},{5,69},{6,22},{7,23},{8,72},{9,... | collective-permute-start | bytes 1327112 | tf_op jit(solution)/shard_map/ppermute | solution.py:71
  25.8 4.0 %collective-permute-start.3 = (bf16[16,128]{1,0:T(8,128)(2,1)S(1)}, bf16[16,128]{1,0:T(8,128)(2,1)S(1)}, u32[]{:S(2)}, u32[]{:S(2)}) collective-permute-start(bf16[16,128]{1,0:T(8,128)(2,1)S(1)} %get-tuple-element.51), channel_id=1, source_target_pairs={{0,48},{1,49},{2,194},{3,195},{4,52},{5,53},{6,198},{7,199},{8,56}... | collective-permute-start | bytes 12296 | tf_op jit(solution)/shard_map/ppermute | solution.py:71
  28.3 4.3 %collective-permute-start.2 = (bf16[16,128]{1,0:T(8,128)(2,1)S(1)}, bf16[16,128]{1,0:T(8,128)(2,1)S(1)}, u32[]{:S(2)}, u32[]{:S(2)}) collective-permute-start(bf16[16,128]{1,0:T(8,128)(2,1)S(1)} %get-tuple-element.51), channel_id=1, source_target_pairs={{0,32},{1,33},{2,130},{3,131},{4,36},{5,37},{6,134},{7,135},{8,40}... | collective-permute-start | bytes 12296 | tf_op jit(solution)/shard_map/ppermute | solution.py:71
  29.8 2.9 %collective-permute-start.1 = (bf16[16,128]{1,0:T(8,128)(2,1)S(1)}, bf16[16,128]{1,0:T(8,128)(2,1)S(1)}, u32[]{:S(2)}, u32[]{:S(2)}) collective-permute-start(bf16[16,128]{1,0:T(8,128)(2,1)S(1)} %get-tuple-element.51), channel_id=1, source_target_pairs={{0,16},{1,17},{2,66},{3,67},{4,20},{5,21},{6,70},{7,71},{8,24},{9,... | collective-permute-start | bytes 12296 | tf_op jit(solution)/shard_map/ppermute | solution.py:71
  37.5 16.6 %collective-permute-start.13 = (bf16[2304,128]{1,0:T(8,128)(2,1)S(1)}, bf16[2304,128]{1,0:T(8,128)(2,1)S(1)}, u32[]{:S(2)}, u32[]{:S(2)}) collective-permute-start(bf16[2304,128]{1,0:T(8,128)(2,1)S(1)} %get-tuple-element.60), channel_id=1, source_target_pairs={{0,48},{1,49},{2,194},{3,195},{4,52},{5,53},{6,198},{7,199},{8,56}... | collective-permute-start | bytes 1769480 | tf_op jit(solution)/shard_map/ppermute | solution.py:71
  40.1 14.1 %collective-permute-start.14 = (bf16[2304,128]{1,0:T(8,128)(2,1)S(1)}, bf16[2304,128]{1,0:T(8,128)(2,1)S(1)}, u32[]{:S(2)}, u32[]{:S(2)}) collective-permute-start(bf16[2304,128]{1,0:T(8,128)(2,1)S(1)} %get-tuple-element.61), channel_id=1, source_target_pairs={{0,32},{1,33},{2,130},{3,131},{4,36},{5,37},{6,134},{7,135},{8,40}... | collective-permute-start | bytes 1769480 | tf_op jit(solution)/shard_map/ppermute | solution.py:71
  40.6 14.2 %collective-permute-start.15 = (bf16[2304,128]{1,0:T(8,128)(2,1)S(1)}, bf16[2304,128]{1,0:T(8,128)(2,1)S(1)}, u32[]{:S(2)}, u32[]{:S(2)}) collective-permute-start(bf16[2304,128]{1,0:T(8,128)(2,1)S(1)} %get-tuple-element.62), channel_id=1, source_target_pairs={{0,16},{1,17},{2,66},{3,67},{4,20},{5,21},{6,70},{7,71},{8,24},{9,... | collective-permute-start | bytes 1769480 | tf_op jit(solution)/shard_map/ppermute | solution.py:71
  55.5 7.0 %collective-permute-start.16 = (bf16[1152,128]{1,0:T(8,128)(2,1)S(1)}, bf16[1152,128]{1,0:T(8,128)(2,1)S(1)}, u32[]{:S(2)}, u32[]{:S(2)}) collective-permute-start(bf16[1152,128]{1,0:T(8,128)(2,1)S(1)} %get-tuple-element.64), channel_id=1, source_target_pairs={{0,2},{2,0},{1,3},{3,1},{4,6},{6,4},{5,7},{7,5},{8,10},{10,8},{9,1... | collective-permute-start | bytes 884744 | tf_op jit(solution)/shard_map/ppermute | solution.py:75
  73.3 1.6 %collective-permute-start.17 = (bf16[1152,128]{1,0:T(8,128)(2,1)S(1)}, bf16[1152,128]{1,0:T(8,128)(2,1)S(1)}, u32[]{:S(2)}, u32[]{:S(2)}) collective-permute-start(bf16[1152,128]{1,0:T(8,128)(2,1)S(1)} %get-tuple-element.69), channel_id=1, source_target_pairs={{0,2},{2,0},{1,3},{3,1},{4,6},{6,4},{5,7},{7,5},{8,10},{10,8},{9,1... | collective-permute-start | bytes 884744 | tf_op jit(solution)/shard_map/ppermute | solution.py:75
  74.9 16.6 %collective-permute-start.20 = (bf16[2304,128]{1,0:T(8,128)(2,1)S(1)}, bf16[2304,128]{1,0:T(8,128)(2,1)S(1)}, u32[]{:S(2)}, u32[]{:S(2)}) collective-permute-start(bf16[2304,128]{1,0:T(8,128)(2,1)S(1)} %slots.1.refs_0_), channel_id=1, source_target_pairs={{0,48},{1,49},{2,194},{3,195},{4,52},{5,53},{6,198},{7,199},{8,56}... | collective-permute-start | bytes 1769480 | tf_op jit(solution)/shard_map/ppermute | solution.py:71
  76.9 14.7 %collective-permute-start.19 = (bf16[2304,128]{1,0:T(8,128)(2,1)S(1)}, bf16[2304,128]{1,0:T(8,128)(2,1)S(1)}, u32[]{:S(2)}, u32[]{:S(2)}) collective-permute-start(bf16[2304,128]{1,0:T(8,128)(2,1)S(1)} %slots.1.refs_0_), channel_id=1, source_target_pairs={{0,32},{1,33},{2,130},{3,131},{4,36},{5,37},{6,134},{7,135},{8,40}... | collective-permute-start | bytes 1769480 | tf_op jit(solution)/shard_map/ppermute | solution.py:71
  77.4 14.9 %collective-permute-start.18 = (bf16[2304,128]{1,0:T(8,128)(2,1)S(1)}, bf16[2304,128]{1,0:T(8,128)(2,1)}, u32[]{:S(2)}, u32[]{:S(2)}) collective-permute-start(bf16[2304,128]{1,0:T(8,128)(2,1)S(1)} %slots.1.refs_0_), channel_id=1, source_target_pairs={{0,16},{1,17},{2,66},{3,67},{4,20},{5,21},{6,70},{7,71},{8,24},{9,... | collective-permute-start | bytes 1769480 | tf_op jit(solution)/shard_map/ppermute | solution.py:71
  78.3 1.7 %copy-start = (bf16[640,2048]{1,0:T(8,128)(2,1)S(1)}, bf16[640,2048]{1,0:T(8,128)(2,1)}, u32[]{:S(2)}) copy-start(bf16[640,2048]{1,0:T(8,128)(2,1)} %get-tuple-element.65.probs_ref) | copy-start | bytes 7864324
  80.1 1.0 copy-start.3
  94.4 13.5 %collective-permute-start.24 = (bf16[1728,128]{1,0:T(8,128)(2,1)S(1)}, bf16[1728,128]{1,0:T(8,128)(2,1)S(1)}, u32[]{:S(2)}, u32[]{:S(2)}) collective-permute-start(bf16[1728,128]{1,0:T(8,128)(2,1)S(1)} %get-tuple-element.81), channel_id=1, source_target_pairs={{0,192},{1,193},{2,50},{3,51},{4,196},{5,197},{6,54},{7,55},{8,200... | collective-permute-start | bytes 1327112 | tf_op jit(solution)/shard_map/ppermute | solution.py:71
  97.2 10.8 %collective-permute-start.25 = (bf16[1728,128]{1,0:T(8,128)(2,1)S(1)}, bf16[1728,128]{1,0:T(8,128)(2,1)S(1)}, u32[]{:S(2)}, u32[]{:S(2)}) collective-permute-start(bf16[1728,128]{1,0:T(8,128)(2,1)S(1)} %get-tuple-element.82), channel_id=1, source_target_pairs={{0,128},{1,129},{2,34},{3,35},{4,132},{5,133},{6,38},{7,39},{8,136... | collective-permute-start | bytes 1327112 | tf_op jit(solution)/shard_map/ppermute | solution.py:71
  97.5 11.1 %collective-permute-start.26 = (bf16[1728,128]{1,0:T(8,128)(2,1)S(1)}, bf16[1728,128]{1,0:T(8,128)(2,1)S(1)}, u32[]{:S(2)}, u32[]{:S(2)}) collective-permute-start(bf16[1728,128]{1,0:T(8,128)(2,1)S(1)} %get-tuple-element.83), channel_id=1, source_target_pairs={{0,64},{1,65},{2,18},{3,19},{4,68},{5,69},{6,22},{7,23},{8,72},{9,... | collective-permute-start | bytes 1327112 | tf_op jit(solution)/shard_map/ppermute | solution.py:71
  97.8 12.5 %collective-permute-start.21 = (bf16[576,128]{1,0:T(8,128)(2,1)S(1)}, bf16[576,128]{1,0:T(8,128)(2,1)S(1)}, u32[]{:S(2)}, u32[]{:S(2)}) collective-permute-start(bf16[576,128]{1,0:T(8,128)(2,1)S(1)} %get-tuple-element.77), channel_id=1, source_target_pairs={{0,192},{1,193},{2,50},{3,51},{4,196},{5,197},{6,54},{7,55},{8,200... | collective-permute-start | bytes 442376 | tf_op jit(solution)/shard_map/ppermute | solution.py:71
  100.4 12.1 %collective-permute-start.22 = (bf16[576,128]{1,0:T(8,128)(2,1)S(1)}, bf16[576,128]{1,0:T(8,128)(2,1)S(1)}, u32[]{:S(2)}, u32[]{:S(2)}) collective-permute-start(bf16[576,128]{1,0:T(8,128)(2,1)S(1)} %get-tuple-element.78), channel_id=1, source_target_pairs={{0,128},{1,129},{2,34},{3,35},{4,132},{5,133},{6,38},{7,39},{8,136... | collective-permute-start | bytes 442376 | tf_op jit(solution)/shard_map/ppermute | solution.py:71
  107.9 4.6 %collective-permute-start.23 = (bf16[576,128]{1,0:T(8,128)(2,1)S(1)}, bf16[576,128]{1,0:T(8,128)(2,1)S(1)}, u32[]{:S(2)}, u32[]{:S(2)}) collective-permute-start(bf16[576,128]{1,0:T(8,128)(2,1)S(1)} %get-tuple-element.79), channel_id=1, source_target_pairs={{0,64},{1,65},{2,18},{3,19},{4,68},{5,69},{6,22},{7,23},{8,72},{9,... | collective-permute-start | bytes 442376 | tf_op jit(solution)/shard_map/ppermute | solution.py:71
  108.8 5.3 %collective-permute-start.27 = (bf16[576,128]{1,0:T(8,128)(2,1)S(1)}, bf16[576,128]{1,0:T(8,128)(2,1)S(1)}, u32[]{:S(2)}, u32[]{:S(2)}) collective-permute-start(bf16[576,128]{1,0:T(8,128)(2,1)S(1)} %get-tuple-element.84), channel_id=1, source_target_pairs={{0,13},{1,12},{2,15},{3,14},{4,8},{5,9},{6,10},{7,11},{8,4},{9,5},... | collective-permute-start | bytes 442376 | tf_op jit(solution)/shard_map/ppermute | solution.py:71
  109.6 9.1 %collective-permute-start.28 = (bf16[576,128]{1,0:T(8,128)(2,1)S(1)}, bf16[576,128]{1,0:T(8,128)(2,1)S(1)}, u32[]{:S(2)}, u32[]{:S(2)}) collective-permute-start(bf16[576,128]{1,0:T(8,128)(2,1)S(1)} %get-tuple-element.85), channel_id=1, source_target_pairs={{0,8},{1,9},{2,10},{3,11},{4,12},{5,13},{6,14},{7,15},{8,0},{9,1},... | collective-permute-start | bytes 442376 | tf_op jit(solution)/shard_map/ppermute | solution.py:71
  110.3 8.4 %collective-permute-start.29 = (bf16[576,128]{1,0:T(8,128)(2,1)S(1)}, bf16[576,128]{1,0:T(8,128)(2,1)S(1)}, u32[]{:S(2)}, u32[]{:S(2)}) collective-permute-start(bf16[576,128]{1,0:T(8,128)(2,1)S(1)} %get-tuple-element.86), channel_id=1, source_target_pairs={{0,4},{1,5},{2,6},{3,7},{4,0},{5,1},{6,2},{7,3},{8,12},{9,13},{10,... | collective-permute-start | bytes 442376 | tf_op jit(solution)/shard_map/ppermute | solution.py:71
  118.8 3.4 %collective-permute-start.30 = (f32[288,128]{1,0:T(8,128)S(1)}, f32[288,128]{1,0:T(8,128)S(1)}, u32[]{:S(2)}, u32[]{:S(2)}) collective-permute-start(f32[288,128]{1,0:T(8,128)S(1)} %get-tuple-element.88), channel_id=1, source_target_pairs={{0,2},{2,0},{1,3},{3,1},{4,6},{6,4},{5,7},{7,5},{8,10},{10,8},{9,1... | collective-permute-start | bytes 442376 | tf_op jit(solution)/shard_map/ppermute | solution.py:75
  122.9 12.1 %collective-permute-start.31 = (bf16[576,128]{1,0:T(8,128)(2,1)S(1)}, bf16[576,128]{1,0:T(8,128)(2,1)S(1)}, u32[]{:S(2)}, u32[]{:S(2)}) collective-permute-start(bf16[576,128]{1,0:T(8,128)(2,1)S(1)} %half_sum.1.mine), channel_id=1, source_target_pairs={{0,1},{1,0},{2,3},{3,2},{4,5},{5,4},{6,7},{7,6},{8,9},{9,8},{10,11... | collective-permute-start | bytes 442376 | tf_op jit(solution)/shard_map/ppermute | solution.py:75

commit v5 on v4

--- a/solution.py
+++ b/solution.py
@@ -443,6 +443,7 @@
         name="pack",
     )
     got = [packed[0]] + each_of(packed[1:], "w")
+    merge_at, qr = lax.optimization_barrier((merge_at, query_rope.reshape(128 * HEADS, ROPE)))
     key_mine, key_other = call(
         merge_kernel,
         [merge_at] + got,
@@ -455,7 +456,6 @@
 
     q = queries.reshape(128 * HEADS, LAT)
     do = grad_out.reshape(128 * HEADS, LAT)
-    qr = query_rope.reshape(128 * HEADS, ROPE)
     probs, ds, keys, g_mine, g_other = attention(meta, latent, rot, key_mine, key_recv, q, qr, do)
 
     (slots,) = call(slots_kernel, (g_mine, swap(g_other, "c")), [((2304, 128), bf16)], name="slots")

time: 136 us -> 138 us (1.015)
  waiting for transfers between devices: 55.4 us -> 51.8 us
  local copies, waits for them, and re-layouts: 7.16 us -> 9.23 us
  other arithmetic: 0.96 us -> 2.81 us
    ppermute x27, waiting for transfers between devices: 45.1 us -> 40.6 us  [exchange(): lax.ppermute(a, MESH, [(number(p), number(partner(p, phase, k))) for p in...]
    unnamed x10 -> x34, local copies, waits for them, and re-layouts: 4.4 us -> 5.81 us
  transfers between devices with their start and end apart: 32 -> 32, of which waited for: 20 -> 21; matrix products, arithmetic and copies ran while one was open for 2% -> 4% of each run, Pallas kernels for 6% -> 6%
where the time goes in v5:
time: 138 us; the launch traced here: 137 us
  waiting for transfers between devices  51.8 us (38%)
  starting transfers between devices  47 us (34%)
  Pallas kernels  25.8 us (19%)
  local copies, waits for them, and re-layouts  9.23 us (7%)
  other arithmetic  2.81 us (2%)
    ppermute x27, waiting for transfers between devices, exchange(): lax.ppermute(a, MESH, [(number(p), number(partner(p, phase, k))) for p in...  40.6 us
    ppermute x27, starting transfers between devices, exchange(): lax.ppermute(a, MESH, [(number(p), number(partner(p, phase, k))) for p in...  30.7 us
    ppermute x5, starting transfers between devices, swap(): return lax.ppermute(a, axis, [(0, 1), (1, 0)])  16.3 us
    ppermute x5, waiting for transfers between devices, swap(): return lax.ppermute(a, axis, [(0, 1), (1, 0)])  11.2 us
    pallas_call x1, Pallas kernels, attention(): pl.pallas_call(attention_kernel, grid=(2, tiles), out_shape=[pltpu.HBM((2...  10.7 us
    pallas_call x1, Pallas kernels, output(): pl.pallas_call(output_kernel, grid=(2, tiles), out_shape=[jax.ShapeDtypeS...  7.66 us
    pallas_call x11, Pallas kernels, call(): pl.pallas_call(kernel, out_shape=[jax.ShapeDtypeStruct(s, d) for s, d in...  7.4 us
    unnamed x34, local copies, waits for them, and re-layouts  5.81 us
  transfers between devices with their start and end apart: 32, of which 21 were waited for; matrix products, arithmetic and copies ran while one was open for 4% of the time, Pallas kernels for 6%

profile of v5, /device:TPU:1, one launch (start us, length us, event | category | flops | bytes accessed | tf_op | source)
XLA Modules:
  0.0 137.4 jit_solution(8036746970862954972)
XLA Ops:
  0.7 0.7 convert.3
  1.8 0.9 copy-done.1
  2.7 0.7 copy-done.8
  3.4 0.7 prep.1
  4.2 3.3 %collective-permute-start = (bf16[304,128]{1,0:T(8,128)(2,1)S(1)}, bf16[304,128]{1,0:T(8,128)(2,1)S(1)}, u32[]{:S(2)}, u32[]{:S(2)}) collective-permute-start(bf16[304,128]{1,0:T(8,128)(2,1)S(1)} %get-tuple-element.52), channel_id=1, source_target_pairs={{0,2},{2,0},{1,3},{3,1},{4,6},{6,4},{5,7},{7,5},{8,10},{10,8},{9,1... | collective-permute-start | bytes 233480 | tf_op jit(solution)/shard_map/ppermute | solution.py:75
  7.5 0.9 collective-permute-done.recv
  8.4 3.9 %collective-permute-start.9 = (bf16[576,128]{1,0:T(8,128)(2,1)S(1)}, bf16[576,128]{1,0:T(8,128)(2,1)S(1)}, u32[]{:S(2)}, u32[]{:S(2)}) collective-permute-start(bf16[576,128]{1,0:T(8,128)(2,1)S(1)} %get-tuple-element.55.refs_0_), channel_id=1, source_target_pairs={{0,13},{1,12},{2,15},{3,14},{4,8},{5,9},{6,10},{7,11},{8,4},{9,5},... | collective-permute-start | bytes 442376 | tf_op jit(solution)/shard_map/ppermute | solution.py:71
  12.4 1.9 %collective-permute-start.7 = (bf16[576,128]{1,0:T(8,128)(2,1)S(1)}, bf16[576,128]{1,0:T(8,128)(2,1)S(1)}, u32[]{:S(2)}, u32[]{:S(2)}) collective-permute-start(bf16[576,128]{1,0:T(8,128)(2,1)S(1)} %get-tuple-element.55.refs_0_), channel_id=1, source_target_pairs={{0,4},{1,5},{2,6},{3,7},{4,0},{5,1},{6,2},{7,3},{8,12},{9,13},{10,... | collective-permute-start | bytes 442376 | tf_op jit(solution)/shard_map/ppermute | solution.py:71
  14.3 2.7 %collective-permute-start.6 = (bf16[576,128]{1,0:T(8,128)(2,1)S(1)}, bf16[576,128]{1,0:T(8,128)(2,1)S(1)}, u32[]{:S(2)}, u32[]{:S(2)}) collective-permute-start(bf16[576,128]{1,0:T(8,128)(2,1)S(1)} %get-tuple-element.55.refs_0_), channel_id=1, source_target_pairs={{0,192},{1,193},{2,50},{3,51},{4,196},{5,197},{6,54},{7,55},{8,200... | collective-permute-start | bytes 442376 | tf_op jit(solution)/shard_map/ppermute | solution.py:71
  17.0 0.3 collective-permute-start.5
  17.6 3.9 %collective-permute-done.8.refs_1_ = bf16[576,128]{1,0:T(8,128)(2,1)S(1)} collective-permute-done((bf16[576,128]{1,0:T(8,128)(2,1)S(1)}, bf16[576,128]{1,0:T(8,128)(2,1)S(1)}, u32[]{:S(2)}, u32[]{:S(2)}) %collective-permute-start.8) | collective-permute-done | bytes 147488 | tf_op jit(solution)/shard_map/ppermute | solution.py:71
  21.5 1.0 collective-permute-done.5.refs_2_
  22.5 2.1 %collective-permute-start.12 = (bf16[1728,128]{1,0:T(8,128)(2,1)S(1)}, bf16[1728,128]{1,0:T(8,128)(2,1)S(1)}, u32[]{:S(2)}, u32[]{:S(2)}) collective-permute-start(bf16[1728,128]{1,0:T(8,128)(2,1)S(1)} %line.1.refs_4_), channel_id=1, source_target_pairs={{0,192},{1,193},{2,50},{3,51},{4,196},{5,197},{6,54},{7,55},{8,200... | collective-permute-start | bytes 1327112 | tf_op jit(solution)/shard_map/ppermute | solution.py:71
  24.7 0.3 collective-permute-start.11
  25.0 0.8 collective-permute-start.10
  25.9 2.5 %collective-permute-start.3 = (bf16[16,128]{1,0:T(8,128)(2,1)S(1)}, bf16[16,128]{1,0:T(8,128)(2,1)S(1)}, u32[]{:S(2)}, u32[]{:S(2)}) collective-permute-start(bf16[16,128]{1,0:T(8,128)(2,1)S(1)} %get-tuple-element.53), channel_id=1, source_target_pairs={{0,48},{1,49},{2,194},{3,195},{4,52},{5,53},{6,198},{7,199},{8,56}... | collective-permute-start | bytes 12296 | tf_op jit(solution)/shard_map/ppermute | solution.py:71
  28.3 0.5 collective-permute-start.2
  28.9 1.0 collective-permute-done.3
  30.1 2.5 %collective-permute-done.2 = bf16[16,128]{1,0:T(8,128)(2,1)S(1)} collective-permute-done((bf16[16,128]{1,0:T(8,128)(2,1)S(1)}, bf16[16,128]{1,0:T(8,128)(2,1)S(1)}, u32[]{:S(2)}, u32[]{:S(2)}) %collective-permute-start.2) | collective-permute-done | bytes 4128 | tf_op jit(solution)/shard_map/ppermute | solution.py:71
  32.9 3.1 %collective-permute-done.12.refs_7_ = bf16[1728,128]{1,0:T(8,128)(2,1)S(1)} collective-permute-done((bf16[1728,128]{1,0:T(8,128)(2,1)S(1)}, bf16[1728,128]{1,0:T(8,128)(2,1)S(1)}, u32[]{:S(2)}, u32[]{:S(2)}) %collective-permute-start.12) | collective-permute-done | bytes 442400 | tf_op jit(solution)/shard_map/ppermute | solution.py:71
  36.1 0.6 collective-permute-done.10.refs_5_
  36.7 1.9 %pack.1 = (bf16[2304,128]{1,0:T(8,128)(2,1)S(1)}, bf16[2304,128]{1,0:T(8,128)(2,1)}, bf16[2304,128]{1,0:T(8,128)(2,1)}, bf16[2304,128]{1,0:T(8,128)(2,1)}) custom-call(s32[64]{0:T(128)S(1)} %reshape.99.where_, bf16[576,128]{1,0:T(8,128)(2,1)S(1)} %get-tuple-element.55.refs_0_, bf16[576,128]{1,0:T(8,128)(2,1)S(1)} %collective-permute-done.4.refs_1_, ...), custom_call_target="tpu_custom_call" | custom-call | tf_op jit(solution)/shard_map/pack/pallas_call | solution.py:33
  38.6 2.5 %collective-permute-start.13 = (bf16[2304,128]{1,0:T(8,128)(2,1)}, bf16[2304,128]{1,0:T(8,128)(2,1)S(1)}, u32[]{:S(2)}, u32[]{:S(2)}) collective-permute-start(bf16[2304,128]{1,0:T(8,128)(2,1)} %get-tuple-element.63), channel_id=1, source_target_pairs={{0,48},{1,49},{2,194},{3,195},{4,52},{5,53},{6,198},{7,199},{8,56}... | collective-permute-start | bytes 1769480 | tf_op jit(solution)/shard_map/ppermute | solution.py:71
  41.1 0.5 collective-permute-start.14
  41.6 0.3 collective-permute-start.15
  42.0 2.1 %reshape.80.qr_ref = bf16[4096,64]{1,0:T(8,128)(2,1)S(1)} reshape(bf16[128,2048]{1,0:T(8,128)(2,1)} %param.9) | data formatting | bytes 1048576 | tf_op jit(solution)/shard_map/reshape | solution.py:446
  44.0 1.3 broadcast_compare_fusion
  45.3 10.1 %collective-permute-done.13.refs_1_ = bf16[2304,128]{1,0:T(8,128)(2,1)S(1)} collective-permute-done((bf16[2304,128]{1,0:T(8,128)(2,1)}, bf16[2304,128]{1,0:T(8,128)(2,1)S(1)}, u32[]{:S(2)}, u32[]{:S(2)}) %collective-permute-start.13) | collective-permute-done | bytes 589856 | tf_op jit(solution)/shard_map/ppermute | solution.py:71
  55.4 0.6 collective-permute-done.15.refs_3_
  56.0 0.7 merge.1
  56.7 5.0 %collective-permute-start.16 = (bf16[1152,128]{1,0:T(8,128)(2,1)S(1)}, bf16[1152,128]{1,0:T(8,128)(2,1)S(1)}, u32[]{:S(2)}, u32[]{:S(2)}) collective-permute-start(bf16[1152,128]{1,0:T(8,128)(2,1)S(1)} %get-tuple-element.67), channel_id=1, source_target_pairs={{0,2},{2,0},{1,3},{3,1},{4,6},{6,4},{5,7},{7,5},{8,10},{10,8},{9,1... | collective-permute-start | bytes 884744 | tf_op jit(solution)/shard_map/ppermute | solution.py:75
  61.7 1.2 collective-permute-done.16.other
  62.9 0.8 copy-done.7
  63.7 0.6 copy-done.10
  64.3 10.7 %attention.1 = (bf16[640,2048]{1,0:T(8,128)(2,1)}, bf16[128,2048]{1,0:T(8,128)(2,1)}, bf16[640,512]{1,0:T(8,128)(2,1)S(1)}, bf16[1152,128]{1,0:T(8,128)(2,1)S(1)}, bf16[1152,128]{1,0:T(8,128)(2,1)S(1)}) custom-call(s32[2]{0:T(128)S(1)} %copy-done.10, bf16[128,512]{1,0:T(8,128)(2,1)S(1)} %copy-done.2, bf16[128,64]{1,0:T(8,128)(2,1)S(1)} %copy-done.7, ...), custom_call_target="tpu_custom_call" | custom-call | tf_op jit(solution)/shard_map/attention/pallas_call | solution.py:230
  75.0 0.4 collective-permute-start.17
  75.3 1.2 collective-permute-done.17.recv
  76.6 1.9 %collective-permute-start.20 = (bf16[2304,128]{1,0:T(8,128)(2,1)S(1)}, bf16[2304,128]{1,0:T(8,128)(2,1)S(1)}, u32[]{:S(2)}, u32[]{:S(2)}) collective-permute-start(bf16[2304,128]{1,0:T(8,128)(2,1)S(1)} %slots.1.refs_0_), channel_id=1, source_target_pairs={{0,48},{1,49},{2,194},{3,195},{4,52},{5,53},{6,198},{7,199},{8,56}... | collective-permute-start | bytes 1769480 | tf_op jit(solution)/shard_map/ppermute | solution.py:71
  78.5 0.5 collective-permute-start.19
  79.1 0.9 collective-permute-start.18
  79.9 0.7 reshape.97
  80.7 0.6 broadcast_select_fusion.where_
  81.3 1.7 %copy-done = bf16[640,2048]{1,0:T(8,128)(2,1)S(1)} copy-done((bf16[640,2048]{1,0:T(8,128)(2,1)S(1)}, bf16[640,2048]{1,0:T(8,128)(2,1)}, u32[]{:S(2)}) %copy-start) | copy-done | bytes 2621464
  83.0 1.0 copy-done.3
  84.1 7.7 %output.1 = (bf16[4096,512]{1,0:T(8,128)(2,1)}, f32[128,512]{1,0:T(8,128)S(1)}, f32[128,64]{1,0:T(8,128)S(1)}) custom-call(bf16[640,2048]{1,0:T(8,128)(2,1)S(1)} %copy-done, bf16[128,2048]{1,0:T(8,128)(2,1)S(1)} %copy-done.3, bf16[640,512]{1,0:T(8,128)(2,1)S(1)} %get-tuple-element.74.keys, bf16[4096,512]{1,0:T(8,128)(2,1)} %bitcast.13, ...), custom_call_target="tpu_custom_call" | custom-call | tf_op jit(solution)/shard_map/output/pallas_call | solution.py:289
  91.7 1.5 %collective-permute-done.20.refs_3_ = bf16[2304,128]{1,0:T(8,128)(2,1)S(1)} collective-permute-done((bf16[2304,128]{1,0:T(8,128)(2,1)S(1)}, bf16[2304,128]{1,0:T(8,128)(2,1)S(1)}, u32[]{:S(2)}, u32[]{:S(2)}) %collective-permute-start.20) | collective-permute-done | bytes 589856 | tf_op jit(solution)/shard_map/ppermute | solution.py:71
  93.3 0.7 collective-permute-done.18.refs_1_
  94.0 2.2 %plane.1 = (f32[1728,128]{1,0:T(8,128)S(1)}, bf16[1728,128]{1,0:T(8,128)(2,1)S(1)}, bf16[1728,128]{1,0:T(8,128)(2,1)S(1)}, bf16[1728,128]{1,0:T(8,128)(2,1)S(1)}...) custom-call(s32[64]{0:T(128)S(1)} %broadcast_select_fusion.where_, ...), custom_call_target="tpu_custom_call" | custom-call | tf_op jit(solution)/shard_map/plane/pallas_call | solution.py:33
  96.1 2.7 %collective-permute-start.24 = (bf16[1728,128]{1,0:T(8,128)(2,1)S(1)}, bf16[1728,128]{1,0:T(8,128)(2,1)S(1)}, u32[]{:S(2)}, u32[]{:S(2)}) collective-permute-start(bf16[1728,128]{1,0:T(8,128)(2,1)S(1)} %get-tuple-element.85), channel_id=1, source_target_pairs={{0,192},{1,193},{2,50},{3,51},{4,196},{5,197},{6,54},{7,55},{8,200... | collective-permute-start | bytes 1327112 | tf_op jit(solution)/shard_map/ppermute | solution.py:71
  99.6 2.6 %collective-permute-start.21 = (bf16[576,128]{1,0:T(8,128)(2,1)S(1)}, bf16[576,128]{1,0:T(8,128)(2,1)S(1)}, u32[]{:S(2)}, u32[]{:S(2)}) collective-permute-start(bf16[576,128]{1,0:T(8,128)(2,1)S(1)} %get-tuple-element.81), channel_id=1, source_target_pairs={{0,192},{1,193},{2,50},{3,51},{4,196},{5,197},{6,54},{7,55},{8,200... | collective-permute-start | bytes 442376 | tf_op jit(solution)/shard_map/ppermute | solution.py:71
  102.5 7.2 %collective-permute-done.24.refs_1_ = bf16[1728,128]{1,0:T(8,128)(2,1)S(1)} collective-permute-done((bf16[1728,128]{1,0:T(8,128)(2,1)S(1)}, bf16[1728,128]{1,0:T(8,128)(2,1)S(1)}, u32[]{:S(2)}, u32[]{:S(2)}) %collective-permute-start.24) | collective-permute-done | bytes 442400 | tf_op jit(solution)/shard_map/ppermute | solution.py:71
  109.6 0.7 collective-permute-done.26.refs_3_
  110.6 0.7 collective-permute-start.27
  111.5 0.5 collective-permute-done.21.refs_1_
  112.0 1.2 collective-permute-start.29
  113.2 1.0 collective-permute-done.22.refs_2_
  114.2 1.6 %collective-permute-done.27.refs_4_ = bf16[576,128]{1,0:T(8,128)(2,1)S(1)} collective-permute-done((bf16[576,128]{1,0:T(8,128)(2,1)S(1)}, bf16[576,128]{1,0:T(8,128)(2,1)S(1)}, u32[]{:S(2)}, u32[]{:S(2)}) %collective-permute-start.27) | collective-permute-done | bytes 147488 | tf_op jit(solution)/shard_map/ppermute | solution.py:71
  115.8 4.5 %collective-permute-done.28.refs_5_ = bf16[576,128]{1,0:T(8,128)(2,1)S(1)} collective-permute-done((bf16[576,128]{1,0:T(8,128)(2,1)S(1)}, bf16[576,128]{1,0:T(8,128)(2,1)S(1)}, u32[]{:S(2)}, u32[]{:S(2)}) %collective-permute-start.28) | collective-permute-done | bytes 147488 | tf_op jit(solution)/shard_map/ppermute | solution.py:71
  120.5 2.4 %collective-permute-start.30 = (f32[288,128]{1,0:T(8,128)S(1)}, f32[288,128]{1,0:T(8,128)S(1)}, u32[]{:S(2)}, u32[]{:S(2)}) collective-permute-start(f32[288,128]{1,0:T(8,128)S(1)} %get-tuple-element.92), channel_id=1, source_target_pairs={{0,2},{2,0},{1,3},{3,1},{4,6},{6,4},{5,7},{7,5},{8,10},{10,8},{9,1... | collective-permute-start | bytes 442376 | tf_op jit(solution)/shard_map/ppermute | solution.py:75
  122.9 1.0 collective-permute-done.30.recv
  124.0 0.6 half_sum.1.mine
  124.6 5.2 %collective-permute-start.31 = (bf16[576,128]{1,0:T(8,128)(2,1)S(1)}, bf16[576,128]{1,0:T(8,128)(2,1)S(1)}, u32[]{:S(2)}, u32[]{:S(2)}) collective-permute-start(bf16[576,128]{1,0:T(8,128)(2,1)S(1)} %half_sum.1.mine), channel_id=1, source_target_pairs={{0,1},{1,0},{2,3},{3,2},{4,5},{5,4},{6,7},{7,6},{8,9},{9,8},{10,11... | collective-permute-start | bytes 442376 | tf_op jit(solution)/shard_map/ppermute | solution.py:75
  129.8 6.8 %collective-permute-done.31.recv = bf16[576,128]{1,0:T(8,128)(2,1)S(1)} collective-permute-done((bf16[576,128]{1,0:T(8,128)(2,1)S(1)}, bf16[576,128]{1,0:T(8,128)(2,1)S(1)}, u32[]{:S(2)}, u32[]{:S(2)}) %collective-permute-start.31) | collective-permute-done | bytes 147488 | tf_op jit(solution)/shard_map/ppermute | solution.py:75
  136.6 0.8 final.1
  (71 shorter events, 3.0 us)
Async XLA Ops:
  1.6 2.5 %copy-start.9 = (s32[2]{0:T(128)}, s32[2]{0:T(128)S(1)}, u32[]{:S(2)}) copy-start(s32[2]{0:T(128)S(1)} %pad_add_fusion.meta) | copy-start | bytes 28
  1.8 6.6 %copy-start.4 = (f32[32,128]{1,0:T(8,128)}, f32[32,128]{1,0:T(8,128)S(1)}, u32[]{:S(2)}) copy-start(f32[32,128]{1,0:T(8,128)S(1)} %get-tuple-element.100.cosine) | copy-start | bytes 49156
  1.8 0.9 copy-start.1
  2.7 0.7 copy-start.8
  3.4 59.5 %copy-start.2 = (bf16[128,512]{1,0:T(8,128)(2,1)S(1)}, bf16[128,512]{1,0:T(8,128)(2,1)}, u32[]{:S(2)}) copy-start(bf16[128,512]{1,0:T(8,128)(2,1)} %lat.3) | copy-start | bytes 393220
  4.1 20.5 %copy-start.6 = (bf16[128,64]{1,0:T(8,128)(2,1)}, bf16[128,64]{1,0:T(8,128)(2,1)S(1)}, u32[]{:S(2)}) copy-start(bf16[128,64]{1,0:T(8,128)(2,1)S(1)} %get-tuple-element.50.rot) | copy-start | bytes 49156
  4.2 4.2 %collective-permute-start = (bf16[304,128]{1,0:T(8,128)(2,1)S(1)}, bf16[304,128]{1,0:T(8,128)(2,1)S(1)}, u32[]{:S(2)}, u32[]{:S(2)}) collective-permute-start(bf16[304,128]{1,0:T(8,128)(2,1)S(1)} %get-tuple-element.52), channel_id=1, source_target_pairs={{0,2},{2,0},{1,3},{3,1},{4,6},{6,4},{5,7},{7,5},{8,10},{10,8},{9,1... | collective-permute-start | bytes 233480 | tf_op jit(solution)/shard_map/ppermute | solution.py:75
  8.4 8.9 %collective-permute-start.9 = (bf16[576,128]{1,0:T(8,128)(2,1)S(1)}, bf16[576,128]{1,0:T(8,128)(2,1)S(1)}, u32[]{:S(2)}, u32[]{:S(2)}) collective-permute-start(bf16[576,128]{1,0:T(8,128)(2,1)S(1)} %get-tuple-element.55.refs_0_), channel_id=1, source_target_pairs={{0,13},{1,12},{2,15},{3,14},{4,8},{5,9},{6,10},{7,11},{8,4},{9,5},... | collective-permute-start | bytes 442376 | tf_op jit(solution)/shard_map/ppermute | solution.py:71
  12.3 9.1 %collective-permute-start.8 = (bf16[576,128]{1,0:T(8,128)(2,1)S(1)}, bf16[576,128]{1,0:T(8,128)(2,1)S(1)}, u32[]{:S(2)}, u32[]{:S(2)}) collective-permute-start(bf16[576,128]{1,0:T(8,128)(2,1)S(1)} %get-tuple-element.55.refs_0_), channel_id=1, source_target_pairs={{0,8},{1,9},{2,10},{3,11},{4,12},{5,13},{6,14},{7,15},{8,0},{9,1},... | collective-permute-start | bytes 442376 | tf_op jit(solution)/shard_map/ppermute | solution.py:71
  12.4 9.1 %collective-permute-start.7 = (bf16[576,128]{1,0:T(8,128)(2,1)S(1)}, bf16[576,128]{1,0:T(8,128)(2,1)S(1)}, u32[]{:S(2)}, u32[]{:S(2)}) collective-permute-start(bf16[576,128]{1,0:T(8,128)(2,1)S(1)} %get-tuple-element.55.refs_0_), channel_id=1, source_target_pairs={{0,4},{1,5},{2,6},{3,7},{4,0},{5,1},{6,2},{7,3},{8,12},{9,13},{10,... | collective-permute-start | bytes 442376 | tf_op jit(solution)/shard_map/ppermute | solution.py:71
  14.3 7.2 %collective-permute-start.6 = (bf16[576,128]{1,0:T(8,128)(2,1)S(1)}, bf16[576,128]{1,0:T(8,128)(2,1)S(1)}, u32[]{:S(2)}, u32[]{:S(2)}) collective-permute-start(bf16[576,128]{1,0:T(8,128)(2,1)S(1)} %get-tuple-element.55.refs_0_), channel_id=1, source_target_pairs={{0,192},{1,193},{2,50},{3,51},{4,196},{5,197},{6,54},{7,55},{8,200... | collective-permute-start | bytes 442376 | tf_op jit(solution)/shard_map/ppermute | solution.py:71
  17.0 5.5 %collective-permute-start.5 = (bf16[576,128]{1,0:T(8,128)(2,1)S(1)}, bf16[576,128]{1,0:T(8,128)(2,1)S(1)}, u32[]{:S(2)}, u32[]{:S(2)}) collective-permute-start(bf16[576,128]{1,0:T(8,128)(2,1)S(1)} %get-tuple-element.55.refs_0_), channel_id=1, source_target_pairs={{0,128},{1,129},{2,34},{3,35},{4,132},{5,133},{6,38},{7,39},{8,136... | collective-permute-start | bytes 442376 | tf_op jit(solution)/shard_map/ppermute | solution.py:71
  17.3 5.1 %collective-permute-start.4 = (bf16[576,128]{1,0:T(8,128)(2,1)S(1)}, bf16[576,128]{1,0:T(8,128)(2,1)S(1)}, u32[]{:S(2)}, u32[]{:S(2)}) collective-permute-start(bf16[576,128]{1,0:T(8,128)(2,1)S(1)} %get-tuple-element.55.refs_0_), channel_id=1, source_target_pairs={{0,64},{1,65},{2,18},{3,19},{4,68},{5,69},{6,22},{7,23},{8,72},{9,... | collective-permute-start | bytes 442376 | tf_op jit(solution)/shard_map/ppermute | solution.py:71
  22.5 13.5 %collective-permute-start.12 = (bf16[1728,128]{1,0:T(8,128)(2,1)S(1)}, bf16[1728,128]{1,0:T(8,128)(2,1)S(1)}, u32[]{:S(2)}, u32[]{:S(2)}) collective-permute-start(bf16[1728,128]{1,0:T(8,128)(2,1)S(1)} %line.1.refs_4_), channel_id=1, source_target_pairs={{0,192},{1,193},{2,50},{3,51},{4,196},{5,197},{6,54},{7,55},{8,200... | collective-permute-start | bytes 1327112 | tf_op jit(solution)/shard_map/ppermute | solution.py:71
  24.7 11.4 %collective-permute-start.11 = (bf16[1728,128]{1,0:T(8,128)(2,1)S(1)}, bf16[1728,128]{1,0:T(8,128)(2,1)S(1)}, u32[]{:S(2)}, u32[]{:S(2)}) collective-permute-start(bf16[1728,128]{1,0:T(8,128)(2,1)S(1)} %line.1.refs_4_), channel_id=1, source_target_pairs={{0,128},{1,129},{2,34},{3,35},{4,132},{5,133},{6,38},{7,39},{8,136... | collective-permute-start | bytes 1327112 | tf_op jit(solution)/shard_map/ppermute | solution.py:71
  25.0 11.7 %collective-permute-start.10 = (bf16[1728,128]{1,0:T(8,128)(2,1)S(1)}, bf16[1728,128]{1,0:T(8,128)(2,1)S(1)}, u32[]{:S(2)}, u32[]{:S(2)}) collective-permute-start(bf16[1728,128]{1,0:T(8,128)(2,1)S(1)} %line.1.refs_4_), channel_id=1, source_target_pairs={{0,64},{1,65},{2,18},{3,19},{4,68},{5,69},{6,22},{7,23},{8,72},{9,... | collective-permute-start | bytes 1327112 | tf_op jit(solution)/shard_map/ppermute | solution.py:71
  25.9 4.0 %collective-permute-start.3 = (bf16[16,128]{1,0:T(8,128)(2,1)S(1)}, bf16[16,128]{1,0:T(8,128)(2,1)S(1)}, u32[]{:S(2)}, u32[]{:S(2)}) collective-permute-start(bf16[16,128]{1,0:T(8,128)(2,1)S(1)} %get-tuple-element.53), channel_id=1, source_target_pairs={{0,48},{1,49},{2,194},{3,195},{4,52},{5,53},{6,198},{7,199},{8,56}... | collective-permute-start | bytes 12296 | tf_op jit(solution)/shard_map/ppermute | solution.py:71
  28.3 4.3 %collective-permute-start.2 = (bf16[16,128]{1,0:T(8,128)(2,1)S(1)}, bf16[16,128]{1,0:T(8,128)(2,1)S(1)}, u32[]{:S(2)}, u32[]{:S(2)}) collective-permute-start(bf16[16,128]{1,0:T(8,128)(2,1)S(1)} %get-tuple-element.53), channel_id=1, source_target_pairs={{0,32},{1,33},{2,130},{3,131},{4,36},{5,37},{6,134},{7,135},{8,40}... | collective-permute-start | bytes 12296 | tf_op jit(solution)/shard_map/ppermute | solution.py:71
  29.8 2.9 %collective-permute-start.1 = (bf16[16,128]{1,0:T(8,128)(2,1)S(1)}, bf16[16,128]{1,0:T(8,128)(2,1)S(1)}, u32[]{:S(2)}, u32[]{:S(2)}) collective-permute-start(bf16[16,128]{1,0:T(8,128)(2,1)S(1)} %get-tuple-element.53), channel_id=1, source_target_pairs={{0,16},{1,17},{2,66},{3,67},{4,20},{5,21},{6,70},{7,71},{8,24},{9,... | collective-permute-start | bytes 12296 | tf_op jit(solution)/shard_map/ppermute | solution.py:71
  30.0 11.6 %copy-start.13 = (bf16[1,16]{1,0:T(2,128)(2,1)}, bf16[1,16]{1,0:T(2,128)(2,1)S(1)}, u32[]{:S(2)}) copy-start(bf16[1,16]{1,0:T(2,128)(2,1)S(1)} %stack.27) | copy-start | bytes 100
  30.1 11.6 %copy-start.14 = (bf16[1,16]{1,0:T(2,128)(2,1)}, bf16[1,16]{1,0:T(2,128)(2,1)S(1)}, u32[]{:S(2)}) copy-start(bf16[1,16]{1,0:T(2,128)(2,1)S(1)} %stack.30) | copy-start | bytes 100
  32.7 8.9 %copy-start.15 = (bf16[1,16]{1,0:T(2,128)(2,1)}, bf16[1,16]{1,0:T(2,128)(2,1)S(1)}, u32[]{:S(2)}) copy-start(bf16[1,16]{1,0:T(2,128)(2,1)S(1)} %stack.29) | copy-start | bytes 100
  32.8 8.8 %copy-start.16 = (bf16[1,16]{1,0:T(2,128)(2,1)}, bf16[1,16]{1,0:T(2,128)(2,1)S(1)}, u32[]{:S(2)}) copy-start(bf16[1,16]{1,0:T(2,128)(2,1)S(1)} %stack.28) | copy-start | bytes 100
  32.9 8.7 %copy-start.12 = (s32[64]{0:T(128)}, s32[64]{0:T(128)S(1)}, u32[]{:S(2)}) copy-start(s32[64]{0:T(128)S(1)} %reshape.99.where_) | copy-start | bytes 772
  38.6 16.8 %collective-permute-start.13 = (bf16[2304,128]{1,0:T(8,128)(2,1)}, bf16[2304,128]{1,0:T(8,128)(2,1)S(1)}, u32[]{:S(2)}, u32[]{:S(2)}) collective-permute-start(bf16[2304,128]{1,0:T(8,128)(2,1)} %get-tuple-element.63), channel_id=1, source_target_pairs={{0,48},{1,49},{2,194},{3,195},{4,52},{5,53},{6,198},{7,199},{8,56}... | collective-permute-start | bytes 1769480 | tf_op jit(solution)/shard_map/ppermute | solution.py:71
  41.1 14.3 %collective-permute-start.14 = (bf16[2304,128]{1,0:T(8,128)(2,1)}, bf16[2304,128]{1,0:T(8,128)(2,1)S(1)}, u32[]{:S(2)}, u32[]{:S(2)}) collective-permute-start(bf16[2304,128]{1,0:T(8,128)(2,1)} %get-tuple-element.64), channel_id=1, source_target_pairs={{0,32},{1,33},{2,130},{3,131},{4,36},{5,37},{6,134},{7,135},{8,40}... | collective-permute-start | bytes 1769480 | tf_op jit(solution)/shard_map/ppermute | solution.py:71
  41.6 14.4 %collective-permute-start.15 = (bf16[2304,128]{1,0:T(8,128)(2,1)}, bf16[2304,128]{1,0:T(8,128)(2,1)S(1)}, u32[]{:S(2)}, u32[]{:S(2)}) collective-permute-start(bf16[2304,128]{1,0:T(8,128)(2,1)} %get-tuple-element.65), channel_id=1, source_target_pairs={{0,16},{1,17},{2,66},{3,67},{4,20},{5,21},{6,70},{7,71},{8,24},{9,... | collective-permute-start | bytes 1769480 | tf_op jit(solution)/shard_map/ppermute | solution.py:71
  56.7 6.2 %collective-permute-start.16 = (bf16[1152,128]{1,0:T(8,128)(2,1)S(1)}, bf16[1152,128]{1,0:T(8,128)(2,1)S(1)}, u32[]{:S(2)}, u32[]{:S(2)}) collective-permute-start(bf16[1152,128]{1,0:T(8,128)(2,1)S(1)} %get-tuple-element.67), channel_id=1, source_target_pairs={{0,2},{2,0},{1,3},{3,1},{4,6},{6,4},{5,7},{7,5},{8,10},{10,8},{9,1... | collective-permute-start | bytes 884744 | tf_op jit(solution)/shard_map/ppermute | solution.py:75
  62.9 0.8 copy-start.7
  63.7 0.6 copy-start.10
  75.0 1.6 %collective-permute-start.17 = (bf16[1152,128]{1,0:T(8,128)(2,1)S(1)}, bf16[1152,128]{1,0:T(8,128)(2,1)S(1)}, u32[]{:S(2)}, u32[]{:S(2)}) collective-permute-start(bf16[1152,128]{1,0:T(8,128)(2,1)S(1)} %get-tuple-element.73), channel_id=1, source_target_pairs={{0,2},{2,0},{1,3},{3,1},{4,6},{6,4},{5,7},{7,5},{8,10},{10,8},{9,1... | collective-permute-start | bytes 884744 | tf_op jit(solution)/shard_map/ppermute | solution.py:75
  76.6 16.6 %collective-permute-start.20 = (bf16[2304,128]{1,0:T(8,128)(2,1)S(1)}, bf16[2304,128]{1,0:T(8,128)(2,1)S(1)}, u32[]{:S(2)}, u32[]{:S(2)}) collective-permute-start(bf16[2304,128]{1,0:T(8,128)(2,1)S(1)} %slots.1.refs_0_), channel_id=1, source_target_pairs={{0,48},{1,49},{2,194},{3,195},{4,52},{5,53},{6,198},{7,199},{8,56}... | collective-permute-start | bytes 1769480 | tf_op jit(solution)/shard_map/ppermute | solution.py:71
  78.5 14.7 %collective-permute-start.19 = (bf16[2304,128]{1,0:T(8,128)(2,1)S(1)}, bf16[2304,128]{1,0:T(8,128)(2,1)S(1)}, u32[]{:S(2)}, u32[]{:S(2)}) collective-permute-start(bf16[2304,128]{1,0:T(8,128)(2,1)S(1)} %slots.1.refs_0_), channel_id=1, source_target_pairs={{0,32},{1,33},{2,130},{3,131},{4,36},{5,37},{6,134},{7,135},{8,40}... | collective-permute-start | bytes 1769480 | tf_op jit(solution)/shard_map/ppermute | solution.py:71
  79.1 14.9 %collective-permute-start.18 = (bf16[2304,128]{1,0:T(8,128)(2,1)S(1)}, bf16[2304,128]{1,0:T(8,128)(2,1)}, u32[]{:S(2)}, u32[]{:S(2)}) collective-permute-start(bf16[2304,128]{1,0:T(8,128)(2,1)S(1)} %slots.1.refs_0_), channel_id=1, source_target_pairs={{0,16},{1,17},{2,66},{3,67},{4,20},{5,21},{6,70},{7,71},{8,24},{9,... | collective-permute-start | bytes 1769480 | tf_op jit(solution)/shard_map/ppermute | solution.py:71
  81.3 1.7 %copy-start = (bf16[640,2048]{1,0:T(8,128)(2,1)S(1)}, bf16[640,2048]{1,0:T(8,128)(2,1)}, u32[]{:S(2)}) copy-start(bf16[640,2048]{1,0:T(8,128)(2,1)} %get-tuple-element.69.probs_ref) | copy-start | bytes 7864324
  83.0 1.0 copy-start.3
  91.7 32.2 %copy-start.11 = (s32[2]{0:T(128)S(1)}, s32[2]{0:T(128)}, u32[]{:S(2)}) copy-start(s32[2]{0:T(128)} %copy-done.9) | copy-start | bytes 28
  91.7 44.9 %copy-start.5 = (f32[32,128]{1,0:T(8,128)S(1)}, f32[32,128]{1,0:T(8,128)}, u32[]{:S(2)}) copy-start(f32[32,128]{1,0:T(8,128)} %copy-done.4) | copy-start | bytes 49156
  96.1 13.5 %collective-permute-start.24 = (bf16[1728,128]{1,0:T(8,128)(2,1)S(1)}, bf16[1728,128]{1,0:T(8,128)(2,1)S(1)}, u32[]{:S(2)}, u32[]{:S(2)}) collective-permute-start(bf16[1728,128]{1,0:T(8,128)(2,1)S(1)} %get-tuple-element.85), channel_id=1, source_target_pairs={{0,192},{1,193},{2,50},{3,51},{4,196},{5,197},{6,54},{7,55},{8,200... | collective-permute-start | bytes 1327112 | tf_op jit(solution)/shard_map/ppermute | solution.py:71
  98.9 10.8 %collective-permute-start.25 = (bf16[1728,128]{1,0:T(8,128)(2,1)S(1)}, bf16[1728,128]{1,0:T(8,128)(2,1)S(1)}, u32[]{:S(2)}, u32[]{:S(2)}) collective-permute-start(bf16[1728,128]{1,0:T(8,128)(2,1)S(1)} %get-tuple-element.86), channel_id=1, source_target_pairs={{0,128},{1,129},{2,34},{3,35},{4,132},{5,133},{6,38},{7,39},{8,136... | collective-permute-start | bytes 1327112 | tf_op jit(solution)/shard_map/ppermute | solution.py:71
  99.2 11.1 %collective-permute-start.26 = (bf16[1728,128]{1,0:T(8,128)(2,1)S(1)}, bf16[1728,128]{1,0:T(8,128)(2,1)S(1)}, u32[]{:S(2)}, u32[]{:S(2)}) collective-permute-start(bf16[1728,128]{1,0:T(8,128)(2,1)S(1)} %get-tuple-element.87), channel_id=1, source_target_pairs={{0,64},{1,65},{2,18},{3,19},{4,68},{5,69},{6,22},{7,23},{8,72},{9,... | collective-permute-start | bytes 1327112 | tf_op jit(solution)/shard_map/ppermute | solution.py:71
  99.6 12.5 %collective-permute-start.21 = (bf16[576,128]{1,0:T(8,128)(2,1)S(1)}, bf16[576,128]{1,0:T(8,128)(2,1)S(1)}, u32[]{:S(2)}, u32[]{:S(2)}) collective-permute-start(bf16[576,128]{1,0:T(8,128)(2,1)S(1)} %get-tuple-element.81), channel_id=1, source_target_pairs={{0,192},{1,193},{2,50},{3,51},{4,196},{5,197},{6,54},{7,55},{8,200... | collective-permute-start | bytes 442376 | tf_op jit(solution)/shard_map/ppermute | solution.py:71
  102.1 12.1 %collective-permute-start.22 = (bf16[576,128]{1,0:T(8,128)(2,1)S(1)}, bf16[576,128]{1,0:T(8,128)(2,1)S(1)}, u32[]{:S(2)}, u32[]{:S(2)}) collective-permute-start(bf16[576,128]{1,0:T(8,128)(2,1)S(1)} %get-tuple-element.82), channel_id=1, source_target_pairs={{0,128},{1,129},{2,34},{3,35},{4,132},{5,133},{6,38},{7,39},{8,136... | collective-permute-start | bytes 442376 | tf_op jit(solution)/shard_map/ppermute | solution.py:71
  109.6 4.6 %collective-permute-start.23 = (bf16[576,128]{1,0:T(8,128)(2,1)S(1)}, bf16[576,128]{1,0:T(8,128)(2,1)S(1)}, u32[]{:S(2)}, u32[]{:S(2)}) collective-permute-start(bf16[576,128]{1,0:T(8,128)(2,1)S(1)} %get-tuple-element.83), channel_id=1, source_target_pairs={{0,64},{1,65},{2,18},{3,19},{4,68},{5,69},{6,22},{7,23},{8,72},{9,... | collective-permute-start | bytes 442376 | tf_op jit(solution)/shard_map/ppermute | solution.py:71
  110.6 5.3 %collective-permute-start.27 = (bf16[576,128]{1,0:T(8,128)(2,1)S(1)}, bf16[576,128]{1,0:T(8,128)(2,1)S(1)}, u32[]{:S(2)}, u32[]{:S(2)}) collective-permute-start(bf16[576,128]{1,0:T(8,128)(2,1)S(1)} %get-tuple-element.88), channel_id=1, source_target_pairs={{0,13},{1,12},{2,15},{3,14},{4,8},{5,9},{6,10},{7,11},{8,4},{9,5},... | collective-permute-start | bytes 442376 | tf_op jit(solution)/shard_map/ppermute | solution.py:71
  111.3 9.1 %collective-permute-start.28 = (bf16[576,128]{1,0:T(8,128)(2,1)S(1)}, bf16[576,128]{1,0:T(8,128)(2,1)S(1)}, u32[]{:S(2)}, u32[]{:S(2)}) collective-permute-start(bf16[576,128]{1,0:T(8,128)(2,1)S(1)} %get-tuple-element.89), channel_id=1, source_target_pairs={{0,8},{1,9},{2,10},{3,11},{4,12},{5,13},{6,14},{7,15},{8,0},{9,1},... | collective-permute-start | bytes 442376 | tf_op jit(solution)/shard_map/ppermute | solution.py:71
  112.0 8.3 %collective-permute-start.29 = (bf16[576,128]{1,0:T(8,128)(2,1)S(1)}, bf16[576,128]{1,0:T(8,128)(2,1)S(1)}, u32[]{:S(2)}, u32[]{:S(2)}) collective-permute-start(bf16[576,128]{1,0:T(8,128)(2,1)S(1)} %get-tuple-element.90), channel_id=1, source_target_pairs={{0,4},{1,5},{2,6},{3,7},{4,0},{5,1},{6,2},{7,3},{8,12},{9,13},{10,... | collective-permute-start | bytes 442376 | tf_op jit(solution)/shard_map/ppermute | solution.py:71
  120.5 3.5 %collective-permute-start.30 = (f32[288,128]{1,0:T(8,128)S(1)}, f32[288,128]{1,0:T(8,128)S(1)}, u32[]{:S(2)}, u32[]{:S(2)}) collective-permute-start(f32[288,128]{1,0:T(8,128)S(1)} %get-tuple-element.92), channel_id=1, source_target_pairs={{0,2},{2,0},{1,3},{3,1},{4,6},{6,4},{5,7},{7,5},{8,10},{10,8},{9,1... | collective-permute-start | bytes 442376 | tf_op jit(solution)/shard_map/ppermute | solution.py:75
  124.6 12.0 %collective-permute-start.31 = (bf16[576,128]{1,0:T(8,128)(2,1)S(1)}, bf16[576,128]{1,0:T(8,128)(2,1)S(1)}, u32[]{:S(2)}, u32[]{:S(2)}) collective-permute-start(bf16[576,128]{1,0:T(8,128)(2,1)S(1)} %half_sum.1.mine), channel_id=1, source_target_pairs={{0,1},{1,0},{2,3},{3,2},{4,5},{5,4},{6,7},{7,6},{8,9},{9,8},{10,11... | collective-permute-start | bytes 442376 | tf_op jit(solution)/shard_map/ppermute | solution.py:75

commit v6 on v4

--- a/solution.py
+++ b/solution.py
@@ -25,7 +25,7 @@
 f32 = jnp.float32
 VMEM = pl.BlockSpec(memory_space=pltpu.VMEM)
 SMEM = pl.BlockSpec(memory_space=pltpu.SMEM)
-PARAMS = pltpu.CompilerParams(vmem_limit_bytes=48 * 1024 * 1024)
+PARAMS = pltpu.CompilerParams(vmem_limit_bytes=44 * 1024 * 1024)
 
 
 def call(kernel, ins, outs, scratch=(), scalars=0, name=None):

time: 136 us -> 138 us (1.015)
  local copies, waits for them, and re-layouts: 7.16 us -> 11.5 us
    unnamed x10 -> x14, local copies, waits for them, and re-layouts: 4.4 us -> 8.77 us
  transfers between devices with their start and end apart: 32 -> 32, of which waited for: 20 -> 20; matrix products, arithmetic and copies ran while one was open for 2% -> 2% of each run, Pallas kernels for 6% -> 5%
where the time goes in v6:
time: 138 us
  waiting for transfers between devices  54.3 us (39%)
  starting transfers between devices  46.6 us (34%)
  Pallas kernels  23.7 us (17%)
  local copies, waits for them, and re-layouts  11.5 us (8%)
    ppermute x27, waiting for transfers between devices, exchange(): lax.ppermute(a, MESH, [(number(p), number(partner(p, phase, k))) for p in...  43.9 us
    ppermute x27, starting transfers between devices, exchange(): lax.ppermute(a, MESH, [(number(p), number(partner(p, phase, k))) for p in...  30.7 us
    ppermute x5, starting transfers between devices, swap(): return lax.ppermute(a, axis, [(0, 1), (1, 0)])  15.9 us
    pallas_call x1, Pallas kernels, attention(): pl.pallas_call(attention_kernel, grid=(2, tiles), out_shape=[pltpu.HBM((2...  10.7 us
    ppermute x5, waiting for transfers between devices, swap(): return lax.ppermute(a, axis, [(0, 1), (1, 0)])  10.3 us
    unnamed x14, local copies, waits for them, and re-layouts  8.77 us
    pallas_call x1, Pallas kernels, output(): pl.pallas_call(output_kernel, grid=(2, tiles), out_shape=[jax.ShapeDtypeS...  6.67 us
    pallas_call x11, Pallas kernels, call(): pl.pallas_call(kernel, out_shape=[jax.ShapeDtypeStruct(s, d) for s, d in...  6.32 us
  transfers between devices with their start and end apart: 32, of which 20 were waited for; matrix products, arithmetic and copies ran while one was open for 2% of the time, Pallas kernels for 5%

profile of v6, /device:TPU:1, one launch (start us, length us, event | category | flops | bytes accessed | tf_op | source)
XLA Modules:
  0.0 137.9 jit_solution(10166388742216862472)
XLA Ops:
  0.7 0.7 convert.3
  1.8 0.9 copy-done.3
  2.7 0.7 copy-done.6
  3.4 0.7 prep.1
  4.1 3.3 %collective-permute-start = (bf16[304,128]{1,0:T(8,128)(2,1)S(1)}, bf16[304,128]{1,0:T(8,128)(2,1)S(1)}, u32[]{:S(2)}, u32[]{:S(2)}) collective-permute-start(bf16[304,128]{1,0:T(8,128)(2,1)S(1)} %get-tuple-element.50), channel_id=1, source_target_pairs={{0,2},{2,0},{1,3},{3,1},{4,6},{6,4},{5,7},{7,5},{8,10},{10,8},{9,1... | collective-permute-start | bytes 233480 | tf_op jit(solution)/shard_map/ppermute | solution.py:75
  7.5 0.9 collective-permute-done.recv
  8.4 3.9 %collective-permute-start.9 = (bf16[576,128]{1,0:T(8,128)(2,1)S(1)}, bf16[576,128]{1,0:T(8,128)(2,1)S(1)}, u32[]{:S(2)}, u32[]{:S(2)}) collective-permute-start(bf16[576,128]{1,0:T(8,128)(2,1)S(1)} %get-tuple-element.52.refs_0_), channel_id=1, source_target_pairs={{0,13},{1,12},{2,15},{3,14},{4,8},{5,9},{6,10},{7,11},{8,4},{9,5},... | collective-permute-start | bytes 442376 | tf_op jit(solution)/shard_map/ppermute | solution.py:71
  12.3 1.9 %collective-permute-start.7 = (bf16[576,128]{1,0:T(8,128)(2,1)S(1)}, bf16[576,128]{1,0:T(8,128)(2,1)S(1)}, u32[]{:S(2)}, u32[]{:S(2)}) collective-permute-start(bf16[576,128]{1,0:T(8,128)(2,1)S(1)} %get-tuple-element.52.refs_0_), channel_id=1, source_target_pairs={{0,4},{1,5},{2,6},{3,7},{4,0},{5,1},{6,2},{7,3},{8,12},{9,13},{10,... | collective-permute-start | bytes 442376 | tf_op jit(solution)/shard_map/ppermute | solution.py:71
  14.2 2.7 %collective-permute-start.6 = (bf16[576,128]{1,0:T(8,128)(2,1)S(1)}, bf16[576,128]{1,0:T(8,128)(2,1)S(1)}, u32[]{:S(2)}, u32[]{:S(2)}) collective-permute-start(bf16[576,128]{1,0:T(8,128)(2,1)S(1)} %get-tuple-element.52.refs_0_), channel_id=1, source_target_pairs={{0,192},{1,193},{2,50},{3,51},{4,196},{5,197},{6,54},{7,55},{8,200... | collective-permute-start | bytes 442376 | tf_op jit(solution)/shard_map/ppermute | solution.py:71
  16.9 0.3 collective-permute-start.5
  17.3 0.2 collective-permute-start.4
  17.5 3.9 %collective-permute-done.8.refs_1_ = bf16[576,128]{1,0:T(8,128)(2,1)S(1)} collective-permute-done((bf16[576,128]{1,0:T(8,128)(2,1)S(1)}, bf16[576,128]{1,0:T(8,128)(2,1)S(1)}, u32[]{:S(2)}, u32[]{:S(2)}) %collective-permute-start.8) | collective-permute-done | bytes 147488 | tf_op jit(solution)/shard_map/ppermute | solution.py:71
  21.5 1.0 collective-permute-done.5.refs_2_
  22.5 2.1 %collective-permute-start.12 = (bf16[1728,128]{1,0:T(8,128)(2,1)S(1)}, bf16[1728,128]{1,0:T(8,128)(2,1)S(1)}, u32[]{:S(2)}, u32[]{:S(2)}) collective-permute-start(bf16[1728,128]{1,0:T(8,128)(2,1)S(1)} %line.1.refs_4_), channel_id=1, source_target_pairs={{0,192},{1,193},{2,50},{3,51},{4,196},{5,197},{6,54},{7,55},{8,200... | collective-permute-start | bytes 1327112 | tf_op jit(solution)/shard_map/ppermute | solution.py:71
  24.6 0.3 collective-permute-start.11
  25.0 0.8 collective-permute-start.10
  25.8 2.5 %collective-permute-start.3 = (bf16[16,128]{1,0:T(8,128)(2,1)S(1)}, bf16[16,128]{1,0:T(8,128)(2,1)S(1)}, u32[]{:S(2)}, u32[]{:S(2)}) collective-permute-start(bf16[16,128]{1,0:T(8,128)(2,1)S(1)} %get-tuple-element.51), channel_id=1, source_target_pairs={{0,48},{1,49},{2,194},{3,195},{4,52},{5,53},{6,198},{7,199},{8,56}... | collective-permute-start | bytes 12296 | tf_op jit(solution)/shard_map/ppermute | solution.py:71
  28.3 0.5 collective-permute-start.2
  28.8 1.0 collective-permute-done.3
  30.0 2.6 %collective-permute-done.2 = bf16[16,128]{1,0:T(8,128)(2,1)S(1)} collective-permute-done((bf16[16,128]{1,0:T(8,128)(2,1)S(1)}, bf16[16,128]{1,0:T(8,128)(2,1)S(1)}, u32[]{:S(2)}, u32[]{:S(2)}) %collective-permute-start.2) | collective-permute-done | bytes 4128 | tf_op jit(solution)/shard_map/ppermute | solution.py:71
  32.9 3.2 %collective-permute-done.12.refs_7_ = bf16[1728,128]{1,0:T(8,128)(2,1)S(1)} collective-permute-done((bf16[1728,128]{1,0:T(8,128)(2,1)S(1)}, bf16[1728,128]{1,0:T(8,128)(2,1)S(1)}, u32[]{:S(2)}, u32[]{:S(2)}) %collective-permute-start.12) | collective-permute-done | bytes 442400 | tf_op jit(solution)/shard_map/ppermute | solution.py:71
  36.0 0.6 collective-permute-done.10.refs_5_
  36.6 0.9 pack.1
  37.5 2.6 %collective-permute-start.13 = (bf16[2304,128]{1,0:T(8,128)(2,1)S(1)}, bf16[2304,128]{1,0:T(8,128)(2,1)S(1)}, u32[]{:S(2)}, u32[]{:S(2)}) collective-permute-start(bf16[2304,128]{1,0:T(8,128)(2,1)S(1)} %get-tuple-element.60), channel_id=1, source_target_pairs={{0,48},{1,49},{2,194},{3,195},{4,52},{5,53},{6,198},{7,199},{8,56}... | collective-permute-start | bytes 1769480 | tf_op jit(solution)/shard_map/ppermute | solution.py:71
  40.1 0.5 collective-permute-start.14
  40.6 0.3 collective-permute-start.15
  40.9 13.3 %collective-permute-done.13.refs_1_ = bf16[2304,128]{1,0:T(8,128)(2,1)S(1)} collective-permute-done((bf16[2304,128]{1,0:T(8,128)(2,1)S(1)}, bf16[2304,128]{1,0:T(8,128)(2,1)S(1)}, u32[]{:S(2)}, u32[]{:S(2)}) %collective-permute-start.13) | collective-permute-done | bytes 589856 | tf_op jit(solution)/shard_map/ppermute | solution.py:71
  54.1 0.6 collective-permute-done.15.refs_3_
  54.8 0.7 merge.1
  55.5 5.0 %collective-permute-start.16 = (bf16[1152,128]{1,0:T(8,128)(2,1)S(1)}, bf16[1152,128]{1,0:T(8,128)(2,1)S(1)}, u32[]{:S(2)}, u32[]{:S(2)}) collective-permute-start(bf16[1152,128]{1,0:T(8,128)(2,1)S(1)} %get-tuple-element.64), channel_id=1, source_target_pairs={{0,2},{2,0},{1,3},{3,1},{4,6},{6,4},{5,7},{7,5},{8,10},{10,8},{9,1... | collective-permute-start | bytes 884744 | tf_op jit(solution)/shard_map/ppermute | solution.py:75
  60.5 2.1 %reshape.81.qr_ref = bf16[4096,64]{1,0:T(8,128)(2,1)S(1)} reshape(bf16[128,2048]{1,0:T(8,128)(2,1)} %param.9) | data formatting | bytes 1048576 | tf_op jit(solution)/shard_map/reshape | solution.py:458
  62.6 2.2 %copy-done = bf16[128,32,512]{2,1,0:T(8,128)(2,1)S(1)} copy-done((bf16[128,32,512]{2,1,0:T(8,128)(2,1)S(1)}, bf16[128,32,512]{2,1,0:T(8,128)(2,1)}, u32[]{:S(2)}) %copy-start) | copy-done | bytes 4194328
  64.7 10.7 %attention.1 = (bf16[640,2048]{1,0:T(8,128)(2,1)}, bf16[128,2048]{1,0:T(8,128)(2,1)}, bf16[640,512]{1,0:T(8,128)(2,1)S(1)}, bf16[1152,128]{1,0:T(8,128)(2,1)S(1)}, bf16[1152,128]{1,0:T(8,128)(2,1)S(1)}) custom-call(s32[2]{0:T(128)S(1)} %pad_add_fusion.meta, bf16[128,512]{1,0:T(8,128)(2,1)S(1)} %copy-done.4, bf16[128,64]{1,0:T(8,128)(2,1)S(1)} %get-tuple-element.48.rot, ...), custom_call_target="tpu_custom_call" | custom-call | tf_op jit(solution)/shard_map/attention/pallas_call | solution.py:230
  75.5 1.6 %collective-permute-done.17.recv = bf16[1152,128]{1,0:T(8,128)(2,1)S(1)} collective-permute-done((bf16[1152,128]{1,0:T(8,128)(2,1)S(1)}, bf16[1152,128]{1,0:T(8,128)(2,1)S(1)}, u32[]{:S(2)}, u32[]{:S(2)}) %collective-permute-start.17) | collective-permute-done | bytes 294944 | tf_op jit(solution)/shard_map/ppermute | solution.py:75
  77.1 1.9 %collective-permute-start.20 = (bf16[2304,128]{1,0:T(8,128)(2,1)S(1)}, bf16[2304,128]{1,0:T(8,128)(2,1)S(1)}, u32[]{:S(2)}, u32[]{:S(2)}) collective-permute-start(bf16[2304,128]{1,0:T(8,128)(2,1)S(1)} %slots.1.refs_0_), channel_id=1, source_target_pairs={{0,48},{1,49},{2,194},{3,195},{4,52},{5,53},{6,198},{7,199},{8,56}... | collective-permute-start | bytes 1769480 | tf_op jit(solution)/shard_map/ppermute | solution.py:71
  79.0 0.5 collective-permute-start.19
  79.5 0.9 collective-permute-start.18
  80.5 2.2 %copy-done.1 = bf16[128,32,512]{2,1,0:T(8,128)(2,1)S(1)} copy-done((bf16[128,32,512]{2,1,0:T(8,128)(2,1)S(1)}, bf16[128,32,512]{2,1,0:T(8,128)(2,1)}, u32[]{:S(2)}) %copy-start.1) | copy-done | bytes 4194328
  82.7 1.7 %copy-done.2 = bf16[640,2048]{1,0:T(8,128)(2,1)S(1)} copy-done((bf16[640,2048]{1,0:T(8,128)(2,1)S(1)}, bf16[640,2048]{1,0:T(8,128)(2,1)}, u32[]{:S(2)}) %copy-start.2) | copy-done | bytes 2621464
  84.4 1.0 copy-done.5
  85.5 6.7 %output.1 = (bf16[4096,512]{1,0:T(8,128)(2,1)}, f32[128,512]{1,0:T(8,128)S(1)}, f32[128,64]{1,0:T(8,128)S(1)}) custom-call(bf16[640,2048]{1,0:T(8,128)(2,1)S(1)} %copy-done.2, bf16[128,2048]{1,0:T(8,128)(2,1)S(1)} %copy-done.5, bf16[640,512]{1,0:T(8,128)(2,1)S(1)} %get-tuple-element.70.keys, bf16[4096,512]{1,0:T(8,128)(2,1)S(1)} %bitcast.12, ...), custom_call_target="tpu_custom_call" | custom-call | tf_op jit(solution)/shard_map/output/pallas_call | solution.py:289
  92.2 1.6 %collective-permute-done.20.refs_3_ = bf16[2304,128]{1,0:T(8,128)(2,1)S(1)} collective-permute-done((bf16[2304,128]{1,0:T(8,128)(2,1)S(1)}, bf16[2304,128]{1,0:T(8,128)(2,1)S(1)}, u32[]{:S(2)}, u32[]{:S(2)}) %collective-permute-start.20) | collective-permute-done | bytes 589856 | tf_op jit(solution)/shard_map/ppermute | solution.py:71
  93.7 0.7 collective-permute-done.18.refs_1_
  94.4 2.2 %plane.1 = (f32[1728,128]{1,0:T(8,128)S(1)}, bf16[1728,128]{1,0:T(8,128)(2,1)S(1)}, bf16[1728,128]{1,0:T(8,128)(2,1)S(1)}, bf16[1728,128]{1,0:T(8,128)(2,1)S(1)}...) custom-call(s32[64]{0:T(128)S(1)} %broadcast_select_fusion.where_, ...), custom_call_target="tpu_custom_call" | custom-call | tf_op jit(solution)/shard_map/plane/pallas_call | solution.py:33
  96.6 2.7 %collective-permute-start.24 = (bf16[1728,128]{1,0:T(8,128)(2,1)S(1)}, bf16[1728,128]{1,0:T(8,128)(2,1)S(1)}, u32[]{:S(2)}, u32[]{:S(2)}) collective-permute-start(bf16[1728,128]{1,0:T(8,128)(2,1)S(1)} %get-tuple-element.81), channel_id=1, source_target_pairs={{0,192},{1,193},{2,50},{3,51},{4,196},{5,197},{6,54},{7,55},{8,200... | collective-permute-start | bytes 1327112 | tf_op jit(solution)/shard_map/ppermute | solution.py:71
  99.3 0.3 collective-permute-start.25
  99.7 0.3 collective-permute-start.26
  100.0 2.6 %collective-permute-start.21 = (bf16[576,128]{1,0:T(8,128)(2,1)S(1)}, bf16[576,128]{1,0:T(8,128)(2,1)S(1)}, u32[]{:S(2)}, u32[]{:S(2)}) collective-permute-start(bf16[576,128]{1,0:T(8,128)(2,1)S(1)} %get-tuple-element.77), channel_id=1, source_target_pairs={{0,192},{1,193},{2,50},{3,51},{4,196},{5,197},{6,54},{7,55},{8,200... | collective-permute-start | bytes 442376 | tf_op jit(solution)/shard_map/ppermute | solution.py:71
  102.6 0.3 collective-permute-start.22
  102.9 7.2 %collective-permute-done.24.refs_1_ = bf16[1728,128]{1,0:T(8,128)(2,1)S(1)} collective-permute-done((bf16[1728,128]{1,0:T(8,128)(2,1)S(1)}, bf16[1728,128]{1,0:T(8,128)(2,1)S(1)}, u32[]{:S(2)}, u32[]{:S(2)}) %collective-permute-start.24) | collective-permute-done | bytes 442400 | tf_op jit(solution)/shard_map/ppermute | solution.py:71
  110.1 0.7 collective-permute-done.26.refs_3_
  111.0 0.7 collective-permute-start.27
  111.8 0.3 collective-permute-start.28
  112.0 0.5 collective-permute-done.21.refs_1_
  112.5 1.2 collective-permute-start.29
  113.7 1.0 collective-permute-done.22.refs_2_
  114.7 1.6 %collective-permute-done.27.refs_4_ = bf16[576,128]{1,0:T(8,128)(2,1)S(1)} collective-permute-done((bf16[576,128]{1,0:T(8,128)(2,1)S(1)}, bf16[576,128]{1,0:T(8,128)(2,1)S(1)}, u32[]{:S(2)}, u32[]{:S(2)}) %collective-permute-start.27) | collective-permute-done | bytes 147488 | tf_op jit(solution)/shard_map/ppermute | solution.py:71
  116.3 4.5 %collective-permute-done.28.refs_5_ = bf16[576,128]{1,0:T(8,128)(2,1)S(1)} collective-permute-done((bf16[576,128]{1,0:T(8,128)(2,1)S(1)}, bf16[576,128]{1,0:T(8,128)(2,1)S(1)}, u32[]{:S(2)}, u32[]{:S(2)}) %collective-permute-start.28) | collective-permute-done | bytes 147488 | tf_op jit(solution)/shard_map/ppermute | solution.py:71
  121.0 2.4 %collective-permute-start.30 = (f32[288,128]{1,0:T(8,128)S(1)}, f32[288,128]{1,0:T(8,128)S(1)}, u32[]{:S(2)}, u32[]{:S(2)}) collective-permute-start(f32[288,128]{1,0:T(8,128)S(1)} %get-tuple-element.88), channel_id=1, source_target_pairs={{0,2},{2,0},{1,3},{3,1},{4,6},{6,4},{5,7},{7,5},{8,10},{10,8},{9,1... | collective-permute-start | bytes 442376 | tf_op jit(solution)/shard_map/ppermute | solution.py:75
  123.4 1.0 collective-permute-done.30.recv
  124.4 0.6 half_sum.1.mine
  125.0 5.2 %collective-permute-start.31 = (bf16[576,128]{1,0:T(8,128)(2,1)S(1)}, bf16[576,128]{1,0:T(8,128)(2,1)S(1)}, u32[]{:S(2)}, u32[]{:S(2)}) collective-permute-start(bf16[576,128]{1,0:T(8,128)(2,1)S(1)} %half_sum.1.mine), channel_id=1, source_target_pairs={{0,1},{1,0},{2,3},{3,2},{4,5},{5,4},{6,7},{7,6},{8,9},{9,8},{10,11... | collective-permute-start | bytes 442376 | tf_op jit(solution)/shard_map/ppermute | solution.py:75
  130.2 6.9 %collective-permute-done.31.recv = bf16[576,128]{1,0:T(8,128)(2,1)S(1)} collective-permute-done((bf16[576,128]{1,0:T(8,128)(2,1)S(1)}, bf16[576,128]{1,0:T(8,128)(2,1)S(1)}, u32[]{:S(2)}, u32[]{:S(2)}) %collective-permute-start.31) | collective-permute-done | bytes 147488 | tf_op jit(solution)/shard_map/ppermute | solution.py:75
  137.1 0.8 final.1
  (51 shorter events, 1.5 us)
Async XLA Ops:
  1.8 0.9 copy-start.3
  2.7 0.7 copy-start.6
  3.4 59.1 %copy-start.4 = (bf16[128,512]{1,0:T(8,128)(2,1)S(1)}, bf16[128,512]{1,0:T(8,128)(2,1)}, u32[]{:S(2)}) copy-start(bf16[128,512]{1,0:T(8,128)(2,1)} %lat.3) | copy-start | bytes 393220
  4.1 4.2 %collective-permute-start = (bf16[304,128]{1,0:T(8,128)(2,1)S(1)}, bf16[304,128]{1,0:T(8,128)(2,1)S(1)}, u32[]{:S(2)}, u32[]{:S(2)}) collective-permute-start(bf16[304,128]{1,0:T(8,128)(2,1)S(1)} %get-tuple-element.50), channel_id=1, source_target_pairs={{0,2},{2,0},{1,3},{3,1},{4,6},{6,4},{5,7},{7,5},{8,10},{10,8},{9,1... | collective-permute-start | bytes 233480 | tf_op jit(solution)/shard_map/ppermute | solution.py:75
  8.4 8.9 %collective-permute-start.9 = (bf16[576,128]{1,0:T(8,128)(2,1)S(1)}, bf16[576,128]{1,0:T(8,128)(2,1)S(1)}, u32[]{:S(2)}, u32[]{:S(2)}) collective-permute-start(bf16[576,128]{1,0:T(8,128)(2,1)S(1)} %get-tuple-element.52.refs_0_), channel_id=1, source_target_pairs={{0,13},{1,12},{2,15},{3,14},{4,8},{5,9},{6,10},{7,11},{8,4},{9,5},... | collective-permute-start | bytes 442376 | tf_op jit(solution)/shard_map/ppermute | solution.py:71
  12.3 9.1 %collective-permute-start.8 = (bf16[576,128]{1,0:T(8,128)(2,1)S(1)}, bf16[576,128]{1,0:T(8,128)(2,1)S(1)}, u32[]{:S(2)}, u32[]{:S(2)}) collective-permute-start(bf16[576,128]{1,0:T(8,128)(2,1)S(1)} %get-tuple-element.52.refs_0_), channel_id=1, source_target_pairs={{0,8},{1,9},{2,10},{3,11},{4,12},{5,13},{6,14},{7,15},{8,0},{9,1},... | collective-permute-start | bytes 442376 | tf_op jit(solution)/shard_map/ppermute | solution.py:71
  12.3 9.1 %collective-permute-start.7 = (bf16[576,128]{1,0:T(8,128)(2,1)S(1)}, bf16[576,128]{1,0:T(8,128)(2,1)S(1)}, u32[]{:S(2)}, u32[]{:S(2)}) collective-permute-start(bf16[576,128]{1,0:T(8,128)(2,1)S(1)} %get-tuple-element.52.refs_0_), channel_id=1, source_target_pairs={{0,4},{1,5},{2,6},{3,7},{4,0},{5,1},{6,2},{7,3},{8,12},{9,13},{10,... | collective-permute-start | bytes 442376 | tf_op jit(solution)/shard_map/ppermute | solution.py:71
  14.2 7.2 %collective-permute-start.6 = (bf16[576,128]{1,0:T(8,128)(2,1)S(1)}, bf16[576,128]{1,0:T(8,128)(2,1)S(1)}, u32[]{:S(2)}, u32[]{:S(2)}) collective-permute-start(bf16[576,128]{1,0:T(8,128)(2,1)S(1)} %get-tuple-element.52.refs_0_), channel_id=1, source_target_pairs={{0,192},{1,193},{2,50},{3,51},{4,196},{5,197},{6,54},{7,55},{8,200... | collective-permute-start | bytes 442376 | tf_op jit(solution)/shard_map/ppermute | solution.py:71
  16.9 5.5 %collective-permute-start.5 = (bf16[576,128]{1,0:T(8,128)(2,1)S(1)}, bf16[576,128]{1,0:T(8,128)(2,1)S(1)}, u32[]{:S(2)}, u32[]{:S(2)}) collective-permute-start(bf16[576,128]{1,0:T(8,128)(2,1)S(1)} %get-tuple-element.52.refs_0_), channel_id=1, source_target_pairs={{0,128},{1,129},{2,34},{3,35},{4,132},{5,133},{6,38},{7,39},{8,136... | collective-permute-start | bytes 442376 | tf_op jit(solution)/shard_map/ppermute | solution.py:71
  17.3 5.1 %collective-permute-start.4 = (bf16[576,128]{1,0:T(8,128)(2,1)S(1)}, bf16[576,128]{1,0:T(8,128)(2,1)S(1)}, u32[]{:S(2)}, u32[]{:S(2)}) collective-permute-start(bf16[576,128]{1,0:T(8,128)(2,1)S(1)} %get-tuple-element.52.refs_0_), channel_id=1, source_target_pairs={{0,64},{1,65},{2,18},{3,19},{4,68},{5,69},{6,22},{7,23},{8,72},{9,... | collective-permute-start | bytes 442376 | tf_op jit(solution)/shard_map/ppermute | solution.py:71
  22.5 13.5 %collective-permute-start.12 = (bf16[1728,128]{1,0:T(8,128)(2,1)S(1)}, bf16[1728,128]{1,0:T(8,128)(2,1)S(1)}, u32[]{:S(2)}, u32[]{:S(2)}) collective-permute-start(bf16[1728,128]{1,0:T(8,128)(2,1)S(1)} %line.1.refs_4_), channel_id=1, source_target_pairs={{0,192},{1,193},{2,50},{3,51},{4,196},{5,197},{6,54},{7,55},{8,200... | collective-permute-start | bytes 1327112 | tf_op jit(solution)/shard_map/ppermute | solution.py:71
  24.6 11.4 %collective-permute-start.11 = (bf16[1728,128]{1,0:T(8,128)(2,1)S(1)}, bf16[1728,128]{1,0:T(8,128)(2,1)S(1)}, u32[]{:S(2)}, u32[]{:S(2)}) collective-permute-start(bf16[1728,128]{1,0:T(8,128)(2,1)S(1)} %line.1.refs_4_), channel_id=1, source_target_pairs={{0,128},{1,129},{2,34},{3,35},{4,132},{5,133},{6,38},{7,39},{8,136... | collective-permute-start | bytes 1327112 | tf_op jit(solution)/shard_map/ppermute | solution.py:71
  25.0 11.7 %collective-permute-start.10 = (bf16[1728,128]{1,0:T(8,128)(2,1)S(1)}, bf16[1728,128]{1,0:T(8,128)(2,1)S(1)}, u32[]{:S(2)}, u32[]{:S(2)}) collective-permute-start(bf16[1728,128]{1,0:T(8,128)(2,1)S(1)} %line.1.refs_4_), channel_id=1, source_target_pairs={{0,64},{1,65},{2,18},{3,19},{4,68},{5,69},{6,22},{7,23},{8,72},{9,... | collective-permute-start | bytes 1327112 | tf_op jit(solution)/shard_map/ppermute | solution.py:71
  25.8 4.0 %collective-permute-start.3 = (bf16[16,128]{1,0:T(8,128)(2,1)S(1)}, bf16[16,128]{1,0:T(8,128)(2,1)S(1)}, u32[]{:S(2)}, u32[]{:S(2)}) collective-permute-start(bf16[16,128]{1,0:T(8,128)(2,1)S(1)} %get-tuple-element.51), channel_id=1, source_target_pairs={{0,48},{1,49},{2,194},{3,195},{4,52},{5,53},{6,198},{7,199},{8,56}... | collective-permute-start | bytes 12296 | tf_op jit(solution)/shard_map/ppermute | solution.py:71
  28.3 4.3 %collective-permute-start.2 = (bf16[16,128]{1,0:T(8,128)(2,1)S(1)}, bf16[16,128]{1,0:T(8,128)(2,1)S(1)}, u32[]{:S(2)}, u32[]{:S(2)}) collective-permute-start(bf16[16,128]{1,0:T(8,128)(2,1)S(1)} %get-tuple-element.51), channel_id=1, source_target_pairs={{0,32},{1,33},{2,130},{3,131},{4,36},{5,37},{6,134},{7,135},{8,40}... | collective-permute-start | bytes 12296 | tf_op jit(solution)/shard_map/ppermute | solution.py:71
  29.8 2.9 %collective-permute-start.1 = (bf16[16,128]{1,0:T(8,128)(2,1)S(1)}, bf16[16,128]{1,0:T(8,128)(2,1)S(1)}, u32[]{:S(2)}, u32[]{:S(2)}) collective-permute-start(bf16[16,128]{1,0:T(8,128)(2,1)S(1)} %get-tuple-element.51), channel_id=1, source_target_pairs={{0,16},{1,17},{2,66},{3,67},{4,20},{5,21},{6,70},{7,71},{8,24},{9,... | collective-permute-start | bytes 12296 | tf_op jit(solution)/shard_map/ppermute | solution.py:71
  37.5 16.6 %collective-permute-start.13 = (bf16[2304,128]{1,0:T(8,128)(2,1)S(1)}, bf16[2304,128]{1,0:T(8,128)(2,1)S(1)}, u32[]{:S(2)}, u32[]{:S(2)}) collective-permute-start(bf16[2304,128]{1,0:T(8,128)(2,1)S(1)} %get-tuple-element.60), channel_id=1, source_target_pairs={{0,48},{1,49},{2,194},{3,195},{4,52},{5,53},{6,198},{7,199},{8,56}... | collective-permute-start | bytes 1769480 | tf_op jit(solution)/shard_map/ppermute | solution.py:71
  40.1 14.1 %collective-permute-start.14 = (bf16[2304,128]{1,0:T(8,128)(2,1)S(1)}, bf16[2304,128]{1,0:T(8,128)(2,1)S(1)}, u32[]{:S(2)}, u32[]{:S(2)}) collective-permute-start(bf16[2304,128]{1,0:T(8,128)(2,1)S(1)} %get-tuple-element.61), channel_id=1, source_target_pairs={{0,32},{1,33},{2,130},{3,131},{4,36},{5,37},{6,134},{7,135},{8,40}... | collective-permute-start | bytes 1769480 | tf_op jit(solution)/shard_map/ppermute | solution.py:71
  40.6 14.2 %collective-permute-start.15 = (bf16[2304,128]{1,0:T(8,128)(2,1)S(1)}, bf16[2304,128]{1,0:T(8,128)(2,1)S(1)}, u32[]{:S(2)}, u32[]{:S(2)}) collective-permute-start(bf16[2304,128]{1,0:T(8,128)(2,1)S(1)} %get-tuple-element.62), channel_id=1, source_target_pairs={{0,16},{1,17},{2,66},{3,67},{4,20},{5,21},{6,70},{7,71},{8,24},{9,... | collective-permute-start | bytes 1769480 | tf_op jit(solution)/shard_map/ppermute | solution.py:71
  55.5 7.0 %collective-permute-start.16 = (bf16[1152,128]{1,0:T(8,128)(2,1)S(1)}, bf16[1152,128]{1,0:T(8,128)(2,1)S(1)}, u32[]{:S(2)}, u32[]{:S(2)}) collective-permute-start(bf16[1152,128]{1,0:T(8,128)(2,1)S(1)} %get-tuple-element.64), channel_id=1, source_target_pairs={{0,2},{2,0},{1,3},{3,1},{4,6},{6,4},{5,7},{7,5},{8,10},{10,8},{9,1... | collective-permute-start | bytes 884744 | tf_op jit(solution)/shard_map/ppermute | solution.py:75
  62.5 2.2 %copy-start = (bf16[128,32,512]{2,1,0:T(8,128)(2,1)S(1)}, bf16[128,32,512]{2,1,0:T(8,128)(2,1)}, u32[]{:S(2)}) copy-start(bf16[128,32,512]{2,1,0:T(8,128)(2,1)} %param.8) | copy-start | bytes 12582916
  75.4 1.6 %collective-permute-start.17 = (bf16[1152,128]{1,0:T(8,128)(2,1)S(1)}, bf16[1152,128]{1,0:T(8,128)(2,1)S(1)}, u32[]{:S(2)}, u32[]{:S(2)}) collective-permute-start(bf16[1152,128]{1,0:T(8,128)(2,1)S(1)} %get-tuple-element.69), channel_id=1, source_target_pairs={{0,2},{2,0},{1,3},{3,1},{4,6},{6,4},{5,7},{7,5},{8,10},{10,8},{9,1... | collective-permute-start | bytes 884744 | tf_op jit(solution)/shard_map/ppermute | solution.py:75
  77.1 16.6 %collective-permute-start.20 = (bf16[2304,128]{1,0:T(8,128)(2,1)S(1)}, bf16[2304,128]{1,0:T(8,128)(2,1)S(1)}, u32[]{:S(2)}, u32[]{:S(2)}) collective-permute-start(bf16[2304,128]{1,0:T(8,128)(2,1)S(1)} %slots.1.refs_0_), channel_id=1, source_target_pairs={{0,48},{1,49},{2,194},{3,195},{4,52},{5,53},{6,198},{7,199},{8,56}... | collective-permute-start | bytes 1769480 | tf_op jit(solution)/shard_map/ppermute | solution.py:71
  79.0 14.7 %collective-permute-start.19 = (bf16[2304,128]{1,0:T(8,128)(2,1)S(1)}, bf16[2304,128]{1,0:T(8,128)(2,1)S(1)}, u32[]{:S(2)}, u32[]{:S(2)}) collective-permute-start(bf16[2304,128]{1,0:T(8,128)(2,1)S(1)} %slots.1.refs_0_), channel_id=1, source_target_pairs={{0,32},{1,33},{2,130},{3,131},{4,36},{5,37},{6,134},{7,135},{8,40}... | collective-permute-start | bytes 1769480 | tf_op jit(solution)/shard_map/ppermute | solution.py:71
  79.5 14.9 %collective-permute-start.18 = (bf16[2304,128]{1,0:T(8,128)(2,1)S(1)}, bf16[2304,128]{1,0:T(8,128)(2,1)}, u32[]{:S(2)}, u32[]{:S(2)}) collective-permute-start(bf16[2304,128]{1,0:T(8,128)(2,1)S(1)} %slots.1.refs_0_), channel_id=1, source_target_pairs={{0,16},{1,17},{2,66},{3,67},{4,20},{5,21},{6,70},{7,71},{8,24},{9,... | collective-permute-start | bytes 1769480 | tf_op jit(solution)/shard_map/ppermute | solution.py:71
  80.5 2.2 %copy-start.1 = (bf16[128,32,512]{2,1,0:T(8,128)(2,1)S(1)}, bf16[128,32,512]{2,1,0:T(8,128)(2,1)}, u32[]{:S(2)}) copy-start(bf16[128,32,512]{2,1,0:T(8,128)(2,1)} %param.8) | copy-start | bytes 12582916
  82.7 1.7 %copy-start.2 = (bf16[640,2048]{1,0:T(8,128)(2,1)S(1)}, bf16[640,2048]{1,0:T(8,128)(2,1)}, u32[]{:S(2)}) copy-start(bf16[640,2048]{1,0:T(8,128)(2,1)} %get-tuple-element.65.probs_ref) | copy-start | bytes 7864324
  84.4 1.0 copy-start.5
  96.6 13.5 %collective-permute-start.24 = (bf16[1728,128]{1,0:T(8,128)(2,1)S(1)}, bf16[1728,128]{1,0:T(8,128)(2,1)S(1)}, u32[]{:S(2)}, u32[]{:S(2)}) collective-permute-start(bf16[1728,128]{1,0:T(8,128)(2,1)S(1)} %get-tuple-element.81), channel_id=1, source_target_pairs={{0,192},{1,193},{2,50},{3,51},{4,196},{5,197},{6,54},{7,55},{8,200... | collective-permute-start | bytes 1327112 | tf_op jit(solution)/shard_map/ppermute | solution.py:71
  99.3 10.8 %collective-permute-start.25 = (bf16[1728,128]{1,0:T(8,128)(2,1)S(1)}, bf16[1728,128]{1,0:T(8,128)(2,1)S(1)}, u32[]{:S(2)}, u32[]{:S(2)}) collective-permute-start(bf16[1728,128]{1,0:T(8,128)(2,1)S(1)} %get-tuple-element.82), channel_id=1, source_target_pairs={{0,128},{1,129},{2,34},{3,35},{4,132},{5,133},{6,38},{7,39},{8,136... | collective-permute-start | bytes 1327112 | tf_op jit(solution)/shard_map/ppermute | solution.py:71
  99.7 11.1 %collective-permute-start.26 = (bf16[1728,128]{1,0:T(8,128)(2,1)S(1)}, bf16[1728,128]{1,0:T(8,128)(2,1)S(1)}, u32[]{:S(2)}, u32[]{:S(2)}) collective-permute-start(bf16[1728,128]{1,0:T(8,128)(2,1)S(1)} %get-tuple-element.83), channel_id=1, source_target_pairs={{0,64},{1,65},{2,18},{3,19},{4,68},{5,69},{6,22},{7,23},{8,72},{9,... | collective-permute-start | bytes 1327112 | tf_op jit(solution)/shard_map/ppermute | solution.py:71
  100.0 12.5 %collective-permute-start.21 = (bf16[576,128]{1,0:T(8,128)(2,1)S(1)}, bf16[576,128]{1,0:T(8,128)(2,1)S(1)}, u32[]{:S(2)}, u32[]{:S(2)}) collective-permute-start(bf16[576,128]{1,0:T(8,128)(2,1)S(1)} %get-tuple-element.77), channel_id=1, source_target_pairs={{0,192},{1,193},{2,50},{3,51},{4,196},{5,197},{6,54},{7,55},{8,200... | collective-permute-start | bytes 442376 | tf_op jit(solution)/shard_map/ppermute | solution.py:71
  102.6 12.1 %collective-permute-start.22 = (bf16[576,128]{1,0:T(8,128)(2,1)S(1)}, bf16[576,128]{1,0:T(8,128)(2,1)S(1)}, u32[]{:S(2)}, u32[]{:S(2)}) collective-permute-start(bf16[576,128]{1,0:T(8,128)(2,1)S(1)} %get-tuple-element.78), channel_id=1, source_target_pairs={{0,128},{1,129},{2,34},{3,35},{4,132},{5,133},{6,38},{7,39},{8,136... | collective-permute-start | bytes 442376 | tf_op jit(solution)/shard_map/ppermute | solution.py:71
  110.1 4.6 %collective-permute-start.23 = (bf16[576,128]{1,0:T(8,128)(2,1)S(1)}, bf16[576,128]{1,0:T(8,128)(2,1)S(1)}, u32[]{:S(2)}, u32[]{:S(2)}) collective-permute-start(bf16[576,128]{1,0:T(8,128)(2,1)S(1)} %get-tuple-element.79), channel_id=1, source_target_pairs={{0,64},{1,65},{2,18},{3,19},{4,68},{5,69},{6,22},{7,23},{8,72},{9,... | collective-permute-start | bytes 442376 | tf_op jit(solution)/shard_map/ppermute | solution.py:71
  111.0 5.3 %collective-permute-start.27 = (bf16[576,128]{1,0:T(8,128)(2,1)S(1)}, bf16[576,128]{1,0:T(8,128)(2,1)S(1)}, u32[]{:S(2)}, u32[]{:S(2)}) collective-permute-start(bf16[576,128]{1,0:T(8,128)(2,1)S(1)} %get-tuple-element.84), channel_id=1, source_target_pairs={{0,13},{1,12},{2,15},{3,14},{4,8},{5,9},{6,10},{7,11},{8,4},{9,5},... | collective-permute-start | bytes 442376 | tf_op jit(solution)/shard_map/ppermute | solution.py:71
  111.8 9.1 %collective-permute-start.28 = (bf16[576,128]{1,0:T(8,128)(2,1)S(1)}, bf16[576,128]{1,0:T(8,128)(2,1)S(1)}, u32[]{:S(2)}, u32[]{:S(2)}) collective-permute-start(bf16[576,128]{1,0:T(8,128)(2,1)S(1)} %get-tuple-element.85), channel_id=1, source_target_pairs={{0,8},{1,9},{2,10},{3,11},{4,12},{5,13},{6,14},{7,15},{8,0},{9,1},... | collective-permute-start | bytes 442376 | tf_op jit(solution)/shard_map/ppermute | solution.py:71
  112.5 8.4 %collective-permute-start.29 = (bf16[576,128]{1,0:T(8,128)(2,1)S(1)}, bf16[576,128]{1,0:T(8,128)(2,1)S(1)}, u32[]{:S(2)}, u32[]{:S(2)}) collective-permute-start(bf16[576,128]{1,0:T(8,128)(2,1)S(1)} %get-tuple-element.86), channel_id=1, source_target_pairs={{0,4},{1,5},{2,6},{3,7},{4,0},{5,1},{6,2},{7,3},{8,12},{9,13},{10,... | collective-permute-start | bytes 442376 | tf_op jit(solution)/shard_map/ppermute | solution.py:71
  121.0 3.4 %collective-permute-start.30 = (f32[288,128]{1,0:T(8,128)S(1)}, f32[288,128]{1,0:T(8,128)S(1)}, u32[]{:S(2)}, u32[]{:S(2)}) collective-permute-start(f32[288,128]{1,0:T(8,128)S(1)} %get-tuple-element.88), channel_id=1, source_target_pairs={{0,2},{2,0},{1,3},{3,1},{4,6},{6,4},{5,7},{7,5},{8,10},{10,8},{9,1... | collective-permute-start | bytes 442376 | tf_op jit(solution)/shard_map/ppermute | solution.py:75
  125.0 12.1 %collective-permute-start.31 = (bf16[576,128]{1,0:T(8,128)(2,1)S(1)}, bf16[576,128]{1,0:T(8,128)(2,1)S(1)}, u32[]{:S(2)}, u32[]{:S(2)}) collective-permute-start(bf16[576,128]{1,0:T(8,128)(2,1)S(1)} %half_sum.1.mine), channel_id=1, source_target_pairs={{0,1},{1,0},{2,3},{3,2},{4,5},{5,4},{6,7},{7,6},{8,9},{9,8},{10,11... | collective-permute-start | bytes 442376 | tf_op jit(solution)/shard_map/ppermute | solution.py:75
